TPU v7x, 512 devices: a whole 4x4x16 slice. The times are simulated.
512 devices in a mesh: probe: 32 (over z, core), seq: 16 (over x, y).
Axes of the slice: x: 4, y: 4, z: 16, core: 2. Of those that a mesh axis runs over, the one named last changes fastest.
Arguments:
- noisy: bfloat16 [512, 1152], P('seq'), may hold values from -6 to 6
- probes: bfloat16 [32, 512, 1152], P('probe', 'seq'), may hold values from -40 to 40
- w_qkv: bfloat16 [1152, 3456], P(None, 'seq'), may hold values from -0.1875 to 0.1875
- w_out: bfloat16 [1152, 1152], P('seq'), may hold values from -0.1875 to 0.1875
- w_mod: bfloat16 [256, 3456], replicated, may hold values from -0.375 to 0.375
- timestep: int32 [1], replicated, may hold values from 0 to 999
Outputs:
- basis: float32 [32, 512, 1152], P('probe', 'seq')
- factor: float32 [32, 32], replicated
All inputs are finite; a program needn't handle non-finite values.
Results may differ from a plain program's by a relative error of at most 0.02.
Values may be sent and summed in bfloat16 or wider, within the bound.
No kernel may reach another device: no remote copies, remote signals or barrier semaphores. Data moves between devices by JAX's collectives and lax.ppermute only.
A program may use at most 64 MiB of HBM per device.

v0:
```python
import math

import jax
import jax.numpy as jnp
from jax import lax
from jax.sharding import PartitionSpec as P

HEAD_DIM = 72
FRAMES = 2


def modulation(timestep, w_mod, feat_width):
    half_dim = w_mod.shape[0] // 2
    freq_index = jnp.arange(half_dim, dtype=jnp.float32)
    frequency = jnp.exp(-math.log(10000.0) * freq_index / half_dim)
    angles = timestep[0].astype(jnp.float32) * frequency
    embedding = jnp.concatenate([jnp.cos(angles), jnp.sin(angles)])
    modulated = jnp.dot(
        jax.nn.silu(embedding)[None, :], w_mod.astype(jnp.float32), precision=lax.Precision.HIGHEST
    )[0]
    return (
        modulated[:feat_width],
        modulated[feat_width : 2 * feat_width],
        modulated[2 * feat_width :],
    )


def normalize(noisy):
    values_f = noisy.astype(jnp.float32)
    centered = values_f - jnp.mean(values_f, axis=-1, keepdims=True)
    deviation = jnp.sqrt(jnp.mean(centered * centered, axis=-1, keepdims=True) + 1e-06)
    return (centered / deviation, deviation)


def norm_tangent(field, normed, deviation):
    mean_part = jnp.mean(field, axis=-1, keepdims=True)
    along = jnp.mean(field * normed, axis=-1, keepdims=True)
    return (field - mean_part - normed * along) / deviation


def frame_probs(queries, key_rows):
    score_scale = queries.shape[-1] ** (-0.5)
    scores = (
        jnp.einsum("qhd,khd->hqk", queries, key_rows, preferred_element_type=jnp.float32)
        * score_scale
    )
    expon = jnp.exp(scores - jnp.max(scores, axis=-1, keepdims=True))
    return (expon / jnp.sum(expon, axis=-1, keepdims=True)).astype(jnp.bfloat16)


def frame_tangent(primal_frame, tangent_frame, attn_probs):
    queries = primal_frame[:, :, 0]
    key_rows = primal_frame[:, :, 1]
    values = primal_frame[:, :, 2]
    score_scale = queries.shape[-1] ** (-0.5)
    p_float = attn_probs.astype(jnp.float32)
    base_out = jnp.einsum("hqk,khd->qhd", attn_probs, values, preferred_element_type=jnp.float32)
    d_scores = jnp.einsum(
        "qhd,khd->hqk", tangent_frame[:, :, 0], key_rows, preferred_element_type=jnp.float32
    )
    d_scores = (
        d_scores
        + jnp.einsum(
            "qhd,khd->hqk", queries, tangent_frame[:, :, 1], preferred_element_type=jnp.float32
        )
    ) * score_scale
    row_sum = jnp.sum(p_float * d_scores, axis=-1)
    mixed_p = (p_float * d_scores).astype(jnp.bfloat16)
    out_tan = jnp.einsum("hqk,khd->qhd", mixed_p, values, preferred_element_type=jnp.float32)
    out_tan = out_tan + jnp.einsum(
        "hqk,khd->qhd", attn_probs, tangent_frame[:, :, 2], preferred_element_type=jnp.float32
    )
    out_tan = out_tan - jnp.transpose(row_sum)[:, :, None] * base_out
    return out_tan.astype(jnp.bfloat16)


def frame_adjoint(primal_frame, cot_frame, attn_probs):
    queries = primal_frame[:, :, 0]
    key_rows = primal_frame[:, :, 1]
    values = primal_frame[:, :, 2]
    score_scale = queries.shape[-1] ** (-0.5)
    p_float = attn_probs.astype(jnp.float32)
    d_value = jnp.einsum(
        "hqk,qhd->khd", attn_probs, cot_frame, preferred_element_type=jnp.float32
    ).astype(jnp.bfloat16)
    d_probs = jnp.einsum("qhd,khd->hqk", cot_frame, values, preferred_element_type=jnp.float32)
    row_dot = jnp.sum(p_float * d_probs, axis=-1, keepdims=True)
    scaled_grad = (p_float * (d_probs - row_dot) * score_scale).astype(jnp.bfloat16)
    d_query = jnp.einsum(
        "hqk,khd->qhd", scaled_grad, key_rows, preferred_element_type=jnp.float32
    ).astype(jnp.bfloat16)
    d_key = jnp.einsum(
        "hqk,qhd->khd", scaled_grad, queries, preferred_element_type=jnp.float32
    ).astype(jnp.bfloat16)
    return jnp.stack([d_query, d_key, d_value], axis=2)


def shards(noisy, probes, w_qkv, w_out, w_mod, timestep):
    tok_rows = noisy.shape[0]
    feat_width = noisy.shape[1]
    seq_count = lax.axis_size("seq")
    probe_count = lax.axis_size("probe")
    shift_mod, scale_mod, gate_mod = modulation(timestep, w_mod, feat_width)
    normed, deviation = normalize(noisy)
    hidden = (normed * (1.0 + scale_mod) + shift_mod).astype(jnp.bfloat16)
    vector = probes[0].astype(jnp.float32)
    d_hidden = (norm_tangent(vector, normed, deviation) * (1.0 + scale_mod)).astype(jnp.bfloat16)
    qkv_full, out_full = (
        lax.all_gather(w_qkv, "seq", axis=1, tiled=True),
        lax.all_gather(w_out, "seq", axis=0, tiled=True),
    )
    tangent_tok = jnp.dot(d_hidden, qkv_full, preferred_element_type=jnp.float32).astype(
        jnp.bfloat16
    )
    primal_tok = jnp.dot(hidden, qkv_full, preferred_element_type=jnp.float32).astype(jnp.bfloat16)
    primal_heads, tangent_heads = (
        lax.all_to_all(primal_tok, "seq", split_axis=1, concat_axis=0, tiled=True),
        lax.all_to_all(tangent_tok, "seq", split_axis=1, concat_axis=0, tiled=True),
    )
    local_heads = w_out.shape[0] // HEAD_DIM
    frame_rows = seq_count * tok_rows // FRAMES
    shape_five = (FRAMES, frame_rows, local_heads, 3, HEAD_DIM)
    primal_five = primal_heads.reshape(shape_five)
    tangent_five = tangent_heads.reshape(shape_five)

    def forward_stored(frame_pair):
        attn_probs = frame_probs(frame_pair[0][:, :, 0], frame_pair[0][:, :, 1])
        return (frame_tangent(frame_pair[0], frame_pair[1], attn_probs), attn_probs)

    d_attn, kept_probs = lax.map(forward_stored, (primal_five, tangent_five))
    d_attn_heads = d_attn.reshape(seq_count * tok_rows, local_heads * HEAD_DIM)
    d_attn_tok = lax.all_to_all(d_attn_heads, "seq", split_axis=0, concat_axis=1, tiled=True)
    update = vector + gate_mod * jnp.dot(d_attn_tok, out_full, preferred_element_type=jnp.float32)
    gated = (gate_mod * update).astype(jnp.bfloat16)
    cot_tok = lax.dot_general(
        gated, out_full, (((1,), (1,)), ((), ())), preferred_element_type=jnp.float32
    ).astype(jnp.bfloat16)
    cot_heads = lax.all_to_all(cot_tok, "seq", split_axis=1, concat_axis=0, tiled=True)
    cot_four = cot_heads.reshape(FRAMES, frame_rows, local_heads, HEAD_DIM)
    grads = lax.map(
        lambda frame_set: frame_adjoint(frame_set[0], frame_set[1], frame_set[2]),
        (primal_five, cot_four, kept_probs),
    )
    grads_heads = grads.reshape(seq_count * tok_rows, local_heads * 3 * HEAD_DIM)
    grads_tok = lax.all_to_all(grads_heads, "seq", split_axis=0, concat_axis=1, tiled=True)
    d_bar = lax.dot_general(
        grads_tok, qkv_full, (((1,), (1,)), ((), ())), preferred_element_type=jnp.float32
    )
    pulled = update + norm_tangent((1.0 + scale_mod) * d_bar, normed, deviation)
    sub_count = tok_rows // probe_count
    by_probe = lax.all_to_all(
        pulled.reshape(1, tok_rows, feat_width), "probe", split_axis=1, concat_axis=0, tiled=True
    )
    flat_rows = by_probe.reshape(probe_count, sub_count * feat_width)
    gram_local = jnp.dot(
        flat_rows, flat_rows.T, precision=lax.Precision.HIGHEST, preferred_element_type=jnp.float32
    ) / float(seq_count * tok_rows * feat_width)
    gram_total = lax.psum(gram_local, ("probe", "seq"))
    lower_tri = jnp.linalg.cholesky(gram_total)
    solved = lax.linalg.triangular_solve(lower_tri, flat_rows, left_side=True, lower=True)
    basis = lax.all_to_all(
        solved.reshape(probe_count, sub_count, feat_width),
        "probe",
        split_axis=0,
        concat_axis=1,
        tiled=True,
    )
    return (basis, jnp.transpose(lower_tri))


def solution(mesh):
    placed = (P("seq", None), P("probe", "seq", None), P(None, "seq"), P("seq", None), P(), P())
    return jax.shard_map(
        shards,
        mesh=mesh,
        in_specs=placed,
        out_specs=(P("probe", "seq", None), P()),
        check_vma=False,
    )
```

profile of v0, /device:TPU:1, one launch (start us, length us, event | category | flops | bytes accessed | tf_op | source)
XLA Modules:
  0.0 370.4 jit_solution(6744596010146254661)
XLA Ops:
  8.7 1.0 convert_reduce_fusion
  9.7 1.1 fusion.33
  10.8 1.0 convert_reduce_fusion.1
  11.8 1.1 fusion.37
  13.7 0.8 convolution_reduce_fusion
  14.5 86.2 %all-gather.3.cloned.1.call-done = bf16[1152,3456]{0,1:T(8,128)(2,1)} async-done(((bf16[1152,216]{0,1:T(8,128)(2,1)}), bf16[1152,3456]{0,1:T(8,128)(2,1)}) %all-gather.3.cloned.1.call-update) | async-done | bytes 7962640 | tf_op jit(solution)/shard_map/all_gather | solution.py:109
  100.7 5.5 %convolution_convert_fusion.3 = bf16[32,3456]{1,0:T(8,128)(2,1)S(1)} fusion(bf16[1152,3456]{0,1:T(8,128)(2,1)} %all-gather.3.cloned.1.call-done, bf16[1,32,1152]{2,1,0:T(8,128)(2,1)S(1)} %copy-done.3, f32[32]{0:T(128)S(1)} %broadcast_multiply_fusion.2, f32[32]{0:T(128)S(1)} %broadcast_multiply_fusion.3, f32[1152]{0:T(1024)S(1)} %get-tuple-element.122, ...), kind=kOutput, calls=%fused_computation.53 | convolution fusion | flops 255283200 | bytes 8336384 | tf_op jit(solution)/shard_map/dot_general | solution.py:112
  106.2 0.8 all_to_all.83
  107.8 5.0 %all-to-all-start.1 = ((bf16[32,16,216]{2,0,1:T(8,128)(2,1)}), bf16[32,16,216]{2,0,1:T(8,128)(2,1)S(1)}, u32[]{:S(2)}, u32[]{:S(2)}) async-start(bf16[32,16,216]{2,0,1:T(8,128)(2,1)} %copy.29), calls=%async_computation.1 | async-start | bytes 524288 | tf_op jit(solution)/shard_map/all_to_all | solution.py:118
  112.8 5.6 %convolution_convert_fusion.4 = bf16[32,3456]{1,0:T(8,128)(2,1)S(1)} fusion(bf16[1152,3456]{0,1:T(8,128)(2,1)} %all-gather.3.cloned.1.call-done, f32[1152]{0:T(1024)S(1)} %get-tuple-element.121, f32[1152]{0:T(1024)S(1)} %get-tuple-element.122, bf16[32,1152]{1,0:T(8,128)(2,1)S(1)} %copy-done.2, f32[32]{0:T(128)S(1)} %add_sqrt_fusion, ...), kind=kOutput, calls=%fused_computation.54 | convolution fusion | flops 255135744 | bytes 8267008 | tf_op jit(solution)/shard_map/dot_general | solution.py:115
  118.4 0.8 all_to_all.80
  119.2 0.8 copy.28
  120.2 6.5 %all-to-all-start = ((bf16[32,16,216]{2,0,1:T(8,128)(2,1)}), bf16[32,16,216]{2,0,1:T(8,128)(2,1)}, u32[]{:S(2)}, u32[]{:S(2)}) async-start(bf16[32,16,216]{2,0,1:T(8,128)(2,1)} %copy.28), calls=%async_computation | async-start | bytes 524288 | tf_op jit(solution)/shard_map/all_to_all | solution.py:117
  127.3 7.6 %all-to-all-done = bf16[32,16,216]{2,0,1:T(8,128)(2,1)} async-done(((bf16[32,16,216]{2,0,1:T(8,128)(2,1)}), bf16[32,16,216]{2,0,1:T(8,128)(2,1)}, u32[]{:S(2)}, u32[]{:S(2)}) %all-to-all-start) | async-done | bytes 221216 | tf_op jit(solution)/shard_map/all_to_all | solution.py:117
  134.8 1.5 reshape.213
  136.6 2.9 while.22
  139.6 9.8 %all_to_all.107 = bf16[16,32,72]{2,1,0:T(8,128)(2,1)S(1)} all-to-all(bf16[16,32,72]{2,1,0:T(8,128)(2,1)S(1)} %bitcast.236), channel_id=1, replica_groups=mesh['probe'=32,'seq'=16] {'seq'}, dimensions={0} | all-to-all | bytes 147456 | tf_op jit(solution)/shard_map/all_to_all | solution.py:132
  149.6 16.3 %all-gather.5.cloned.1.call-done = bf16[1152,1152]{1,0:T(8,128)(2,1)} async-done(((bf16[72,1152]{1,0:T(8,128)(2,1)}), bf16[1152,1152]{1,0:T(8,128)(2,1)}) %all-gather.5.cloned.1.call-update) | async-done | bytes 2654224 | tf_op jit(solution)/shard_map/all_gather | solution.py:110
  165.9 2.5 fusion.28
  168.5 0.9 convolution_convert_fusion.5
  170.3 4.1 %all-to-all-start.3 = ((bf16[32,16,72]{2,0,1:T(8,128)(2,1)}), bf16[32,16,72]{2,0,1:T(8,128)(2,1)S(1)}, u32[]{:S(2)}, u32[]{:S(2)}) async-start(bf16[32,16,72]{2,0,1:T(8,128)(2,1)} %copy.34), calls=%async_computation.3 | async-start | bytes 262144 | tf_op jit(solution)/shard_map/all_to_all | solution.py:138
  174.4 6.8 %all-to-all-done.3 = bf16[32,16,72]{2,0,1:T(8,128)(2,1)S(1)} async-done(((bf16[32,16,72]{2,0,1:T(8,128)(2,1)}), bf16[32,16,72]{2,0,1:T(8,128)(2,1)S(1)}, u32[]{:S(2)}, u32[]{:S(2)}) %all-to-all-start.3) | async-done | bytes 73760 | tf_op jit(solution)/shard_map/all_to_all | solution.py:138
  181.2 1.9 while.23
  183.6 10.7 %all_to_all.108 = bf16[16,32,216]{2,1,0:T(8,128)(2,1)S(1)} all-to-all(bf16[16,32,216]{2,1,0:T(8,128)(2,1)S(1)} %all_to_all.93), channel_id=1, replica_groups=mesh['probe'=32,'seq'=16] {'seq'}, dimensions={0} | all-to-all | bytes 442368 | tf_op jit(solution)/shard_map/all_to_all | solution.py:145
  194.8 4.8 %fusion.58 = (f32[32]{0:T(128)S(1)}, f32[32]{0:T(128)S(1)}, f32[32,1152]{1,0:T(8,128)S(1)}) fusion(f32[32]{0:T(128)S(1)} %add_sqrt_fusion, f32[32]{0:T(128)S(1)} %broadcast_multiply_fusion.4, bf16[32,1152]{1,0:T(8,128)(2,1)S(1)} %copy-done.2, bf16[32,3456]{1,0:T(8,128)(2,1)S(1)} %all_to_all.96, bf16[1152,3456]{0,1:T(8,128)(2,1)} %all-gather.3.cloned.1.call-done, ...), kind=kOutput, calls=%fused_computation.113 | convolution fusion | flops 255061952 | bytes 8410112 | tf_op jit(solution)/shard_map/dot_general | solution.py:146
  199.9 32.7 %all_to_all.109 = f32[1,32,1152]{2,0,1:T(1,128)S(1)} all-to-all(f32[1,32,1152]{2,0,1:T(1,128)S(1)} %copy.39), channel_id=1, replica_groups=mesh['probe'=32,'seq'=16] {'probe'}, dimensions={1} | all-to-all | bytes 294912 | tf_op jit(solution)/shard_map/all_to_all | solution.py:151
  232.9 98.9 %psum.7 = f32[32,32]{0,1:T(8,128)S(1)} all-reduce(f32[32,32]{0,1:T(8,128)S(1)} %convolution_multiply_fusion.3), channel_id=1, replica_groups=mesh['probe'=32,'seq'=16] {'probe','seq'}, use_global_device_ids=true, to_apply=%region_14.15 | all-reduce | flops 1024 | bytes 8192 | tf_op jit(solution)/shard_map/psum | solution.py:158
  331.9 2.9 cholesky.16
  336.2 2.4 custom-call.6
  339.0 0.8 copy.42
  339.8 6.6 %all-to-all-start.6 = ((f32[32,1,1152]{2,1,0:T(1,128)}), f32[32,1,1152]{2,1,0:T(1,128)S(1)}, u32[]{:S(2)}, u32[]{:S(2)}) async-start(f32[32,1,1152]{2,1,0:T(1,128)} %copy.42), calls=%async_computation.6 | async-start | bytes 294912 | tf_op jit(solution)/shard_map/all_to_all | solution.py:161
  347.1 15.8 %all-to-all-done.6 = f32[32,1,1152]{2,1,0:T(1,128)S(1)} async-done(((f32[32,1,1152]{2,1,0:T(1,128)}), f32[32,1,1152]{2,1,0:T(1,128)S(1)}, u32[]{:S(2)}, u32[]{:S(2)}) %all-to-all-start.6) | async-done | bytes 147488 | tf_op jit(solution)/shard_map/all_to_all | solution.py:161
  (82 shorter events, 13.8 us)
Async XLA Ops:
  7.2 6.5 %copy-start = (bf16[256,3456]{1,0:T(8,128)(2,1)S(1)}, bf16[256,3456]{1,0:T(8,128)(2,1)}, u32[]{:S(2)}) copy-start(bf16[256,3456]{1,0:T(8,128)(2,1)} %param.14) | copy-start | bytes 5308420
  7.2 93.6 %copy-start.2 = (bf16[32,1152]{1,0:T(8,128)(2,1)S(1)}, bf16[32,1152]{1,0:T(8,128)(2,1)}, u32[]{:S(2)}) copy-start(bf16[32,1152]{1,0:T(8,128)(2,1)} %param.10) | copy-start | bytes 221188
  7.2 93.5 %copy-start.3 = (bf16[1,32,1152]{2,1,0:T(8,128)(2,1)S(1)}, bf16[1,32,1152]{2,1,0:T(8,128)(2,1)}, u32[]{:S(2)}) copy-start(bf16[1,32,1152]{2,1,0:T(8,128)(2,1)} %param.11) | copy-start | bytes 221188
  7.2 93.5 %all-gather.3.cloned.1.call-start = ((), (), s32[]{:S(2)}) async-start(), calls=%async_computation.7 | async-start | bytes 8460288 | tf_op jit(solution)/shard_map/all_gather | solution.py:109
  7.9 158.0 %all-gather.5.cloned.1.call-start = ((), (), s32[]{:S(2)}) async-start(), calls=%async_computation.8 | async-start | bytes 2820096 | tf_op jit(solution)/shard_map/all_gather | solution.py:110
  107.8 12.4 %all-to-all-start.1 = ((bf16[32,16,216]{2,0,1:T(8,128)(2,1)}), bf16[32,16,216]{2,0,1:T(8,128)(2,1)S(1)}, u32[]{:S(2)}, u32[]{:S(2)}) async-start(bf16[32,16,216]{2,0,1:T(8,128)(2,1)} %copy.29), calls=%async_computation.1 | async-start | bytes 524288 | tf_op jit(solution)/shard_map/all_to_all | solution.py:118
  120.2 14.6 %all-to-all-start = ((bf16[32,16,216]{2,0,1:T(8,128)(2,1)}), bf16[32,16,216]{2,0,1:T(8,128)(2,1)}, u32[]{:S(2)}, u32[]{:S(2)}) async-start(bf16[32,16,216]{2,0,1:T(8,128)(2,1)} %copy.28), calls=%async_computation | async-start | bytes 524288 | tf_op jit(solution)/shard_map/all_to_all | solution.py:117
  165.9 2.5 copy-start.1
  170.3 10.8 %all-to-all-start.3 = ((bf16[32,16,72]{2,0,1:T(8,128)(2,1)}), bf16[32,16,72]{2,0,1:T(8,128)(2,1)S(1)}, u32[]{:S(2)}, u32[]{:S(2)}) async-start(bf16[32,16,72]{2,0,1:T(8,128)(2,1)} %copy.34), calls=%async_computation.3 | async-start | bytes 262144 | tf_op jit(solution)/shard_map/all_to_all | solution.py:138
  339.8 23.1 %all-to-all-start.6 = ((f32[32,1,1152]{2,1,0:T(1,128)}), f32[32,1,1152]{2,1,0:T(1,128)S(1)}, u32[]{:S(2)}, u32[]{:S(2)}) async-start(f32[32,1,1152]{2,1,0:T(1,128)} %copy.42), calls=%async_computation.6 | async-start | bytes 294912 | tf_op jit(solution)/shard_map/all_to_all | solution.py:161
Sparse Core Ops, SparseCore 0:
  11.1 89.5 all-gather.2
  103.8 62.0 all-gather.4
where the time goes:
time: 371 us; the launch traced here: 370 us
  blocking collectives  152 us (41%)
  waiting for transfers between devices  134 us (36%)
  matrix products  24.6 us (7%)
  starting transfers between devices  22.2 us (6%)
  between operations  15 us (4%)
  other arithmetic  11.5 us (3%)
  local copies, waits for them, and re-layouts  10.4 us (3%)
    psum x1, blocking collectives, shards(): gram_total = lax.psum(gram_local, ('probe', 'seq'))  98.9 us
    all_gather x1, waiting for transfers between devices, shards(): lax.all_gather(w_qkv, 'seq', axis=1, tiled=True)  86.2 us
    all_to_all x1, blocking collectives, shards(): lax.all_to_all(pulled.reshape(1, tok_rows, feat_width), 'probe', split_ax...  32.7 us
    all_gather x1, waiting for transfers between devices, shards(): lax.all_gather(w_out, 'seq', axis=0, tiled=True)  16.3 us
    all_to_all x1, waiting for transfers between devices, shards(): lax.all_to_all(solved.reshape(probe_count, sub_count, feat_width), 'probe...  15.8 us
    all_to_all x1, blocking collectives, shards(): lax.all_to_all(grads_heads, 'seq', split_axis=0, concat_axis=1, tiled=True)  10.7 us
    all_to_all x1, blocking collectives, shards(): lax.all_to_all(d_attn_heads, 'seq', split_axis=0, concat_axis=1, tiled=True)  9.75 us
    all_to_all x1, waiting for transfers between devices, shards(): lax.all_to_all(primal_tok, 'seq', split_axis=1, concat_axis=0, tiled=True)  7.58 us
  transfers between devices with their start and end apart: 6, of which 6 were waited for; matrix products, arithmetic and copies ran while one was open for 6% of the time, Pallas kernels for 0%

commit v1 on v0

v1 whole, which is shorter than its diff:
```python
import functools
import math

import jax
import jax.numpy as jnp
from jax import lax
from jax.experimental import pallas as pl
from jax.experimental.pallas import tpu as pltpu
from jax.sharding import Mesh
from jax.sharding import PartitionSpec as P

HEAD_DIM = 72
LANES = 128
FRAMES = 2
SEQ = ("frame", "part")
PROBE = ("z", "core")
MIB = 1024 * 1024
STEP = 4
NT = (((1,), (1,)), ((), ()))
NN = (((1,), (0,)), ((), ()))
BF = jnp.bfloat16
F32 = jnp.float32


def mm(a, b, dims=NN):
    return lax.dot_general(a, b, dims, preferred_element_type=F32)


def exact(a, b, dims=NN):
    return lax.dot_general(
        a, b, dims, precision=lax.Precision.HIGHEST, preferred_element_type=F32
    )


def eye(n):
    row = lax.broadcasted_iota(jnp.int32, (n, n), 0)
    col = lax.broadcasted_iota(jnp.int32, (n, n), 1)
    return jnp.where(row == col, 1.0, 0.0)


def flip(a):
    return mm(eye(a.shape[1]).astype(BF), a, NT).astype(BF)


def modulation(timestep, w_mod, feat_width):
    half_dim = w_mod.shape[0] // 2
    freq_index = jnp.arange(half_dim, dtype=jnp.float32)
    frequency = jnp.exp(-math.log(10000.0) * freq_index / half_dim)
    angles = timestep[0].astype(jnp.float32) * frequency
    embedding = jnp.concatenate([jnp.cos(angles), jnp.sin(angles)])
    modulated = jnp.dot(
        jax.nn.silu(embedding)[None, :], w_mod.astype(jnp.float32), precision=lax.Precision.HIGHEST
    )
    return modulated.reshape(3, feat_width)


def normalize(values_f):
    centered = values_f - jnp.mean(values_f, axis=-1, keepdims=True)
    inverse = 1.0 / jnp.sqrt(jnp.mean(centered * centered, axis=-1, keepdims=True) + 1e-06)
    return centered * inverse, inverse


def norm_tangent(field, normed, inverse):
    mean_part = jnp.mean(field, axis=-1, keepdims=True)
    along = jnp.mean(field * normed, axis=-1, keepdims=True)
    return (field - mean_part - normed * along) * inverse


def fetch(pairs, sems):
    copies = [pltpu.make_async_copy(a, b, sems.at[i]) for i, (a, b) in enumerate(pairs)]
    for copy in copies:
        copy.start()
    return copies


def copies_kernel(noisy, probe, out, sems):
    count = out.shape[0]
    pairs = [(noisy, out.at[j, 0]) for j in range(count)]
    pairs += [(probe.at[0], out.at[j, 1]) for j in range(count)]
    for copy in fetch(pairs, sems):
        copy.wait()


def head_forward(hidden, d_hidden, weights, primal, probs):
    c = HEAD_DIM ** (-0.5)
    q, k, v = [mm(hidden, weights[i], NT).astype(BF) for i in range(3)]
    dq, dk, dv = [mm(d_hidden, weights[i], NT).astype(BF) for i in range(3)]
    scores = mm(q, k, NT) * c
    expon = jnp.exp(scores - jnp.max(scores, axis=-1, keepdims=True))
    p = (expon / jnp.sum(expon, axis=-1, keepdims=True)).astype(BF)
    d_scores = (mm(dq, k, NT) + mm(q, dk, NT)) * c
    mixed = p.astype(F32) * d_scores
    row_sum = jnp.sum(mixed, axis=-1, keepdims=True)
    out = mm(mixed.astype(BF), v) + mm(p, dv) - row_sum * mm(p, v)
    probs[...] = p
    for i, value in enumerate((q, k, v)):
        primal[i] = value
    return mm(out.astype(BF), weights[3])


def near_kernel(gath, weights, mods, hidden, d_hidden, term, primal, probs):
    blocks, _, rows, _ = gath.shape
    scale = 1.0 + mods[1:2, :]
    shift = mods[0:1, :]

    def block(i, carry):
        normed, inverse = normalize(gath[i, 0].astype(F32))
        at = pl.ds(pl.multiple_of(i * rows, rows), rows)
        hidden[at, :] = (normed * scale + shift).astype(BF)
        field = norm_tangent(gath[i, 1].astype(F32), normed, inverse)
        d_hidden[at, :] = (field * scale).astype(BF)
        return carry

    lax.fori_loop(0, blocks, block, 0, unroll=2)
    term[...] = head_forward(hidden[...], d_hidden[...], weights, primal, probs)


def far_kernel(hidden, d_hidden, weights, term, parts, primal, probs):
    total = term[...] + head_forward(hidden[...], d_hidden[...], weights, primal, probs)
    parts[...] = total.astype(BF).reshape(parts.shape)


def update_kernel(parts, probe, mods, gated, update):
    total = parts[0].astype(F32)
    for j in range(1, parts.shape[0]):
        total = total + parts[j].astype(F32)
    gate = mods[2:3, :]
    fresh = probe[0].astype(F32) + gate * total
    update[...] = fresh
    value = (gate * fresh).astype(BF)
    for j in range(gated.shape[0]):
        gated[j] = value


def adjoint_kernel(gated, near, near_primal, near_probs, far, far_primal, far_probs, parts):
    c = HEAD_DIM ** (-0.5)
    blocks, rows, width = gated.shape
    whole = gated[...].reshape(blocks * rows, width)
    total = None
    for weights, primal, probs in (
        (near, near_primal, near_probs),
        (far, far_primal, far_probs),
    ):
        co = mm(whole, weights[3], NT).astype(BF)
        q, k, v = primal[0], primal[1], primal[2]
        p = probs[...]
        p_float = p.astype(F32)
        d_probs = mm(co, v, NT)
        row_dot = jnp.sum(p_float * d_probs, axis=-1, keepdims=True)
        scaled = (p_float * (d_probs - row_dot) * c).astype(BF)
        grads = (mm(scaled, k), mm(flip(scaled), q), mm(flip(p), co))
        for i, grad in enumerate(grads):
            term = mm(grad.astype(BF), weights[i])
            total = term if total is None else total + term
    parts[...] = total.astype(BF).reshape(parts.shape)


def pulled_kernel(parts, update, noisy, mods, pulled):
    total = parts[0].astype(F32)
    for j in range(1, parts.shape[0]):
        total = total + parts[j].astype(F32)
    normed, inverse = normalize(noisy[...].astype(F32))
    value = update[...] + norm_tangent((1.0 + mods[1:2, :]) * total, normed, inverse)
    pulled[:, 0, :] = value


def gram_kernel(scale, by_probe, copies, flat):
    rows = by_probe[:, 0, :]
    flat[...] = rows
    gram = exact(rows, rows, NT) * scale
    n = gram.shape[0]
    width = LANES // n
    high = n // width
    packed = jnp.concatenate([gram[i * high : (i + 1) * high] for i in range(width)], axis=1)
    for j in range(copies.shape[0]):
        copies[j] = packed


def tree_sum(terms):
    while len(terms) > 1:
        terms = [terms[i] + terms[i + 1] for i in range(0, len(terms), 2)]
    return terms[0]


def total_kernel(arrived, copies):
    total = tree_sum([arrived[j] for j in range(arrived.shape[0])])
    for j in range(copies.shape[0]):
        copies[j] = total


def solve_kernel(arrived, flat, factor, solved):
    packed = tree_sum([arrived[j] for j in range(arrived.shape[0])])
    n = flat.shape[0]
    width = LANES // n
    a = jnp.concatenate([packed[:, i * n : (i + 1) * n] for i in range(width)], axis=0)
    both = jnp.concatenate([a, eye(n)], axis=1)
    row = lax.broadcasted_iota(jnp.int32, both.shape, 0)
    col = lax.broadcasted_iota(jnp.int32, both.shape, 1)
    wide = (1, both.shape[1])
    for j in range(0, n, STEP):
        span = range(STEP)
        tops = [both[j + i : j + i + 1, :] for i in span]
        sides = [jnp.broadcast_to(both[:, j + i : j + i + 1], both.shape) for i in span]
        corner = [
            [jnp.broadcast_to(tops[i][:, j + k : j + k + 1], wide) for k in span] for i in span
        ]
        change = jnp.zeros_like(both)
        for i in span:
            inverse = 1.0 / corner[i][i]
            for k in range(i + 1, STEP):
                ratio = corner[i][k] * inverse
                tops[k] = tops[k] - ratio * tops[i]
                sides[k] = sides[k] - ratio * sides[i]
                for m in range(k, STEP):
                    corner[k][m] = corner[k][m] - ratio * corner[i][m]
            change = change + sides[i] * (tops[i] * inverse)
        below = both - jnp.where(row >= j + STEP, change, 0.0)
        for i in span:
            below = jnp.where(row == j + i, tops[i], below)
        both = below
    pivots = jnp.sum(jnp.where(row == col, both, 0.0), axis=1, keepdims=True)
    both = both / jnp.sqrt(pivots)
    factor[...] = jnp.where(col >= row, both, 0.0)[:, :n]
    rows = exact(both[:, n:], flat[...])
    half = solved.shape[2]
    for i in range(2):
        solved[:, i, :] = rows[:, i * half : (i + 1) * half].astype(BF)


def basis_kernel(halves, basis):
    half = halves.shape[2]
    for i in range(2):
        basis[0, :, i * half : (i + 1) * half] = halves[:, i, :].astype(F32)


HBM = pl.BlockSpec(memory_space=pl.ANY)
LOCAL = pl.BlockSpec(memory_space=pltpu.VMEM)


def call(
    kernel, out_shape, *args, where=None, out_specs=None, scratch=(), flops=0, moved=0, limit=8
):
    return pl.pallas_call(
        kernel,
        out_shape=out_shape,
        in_specs=where or [LOCAL] * len(args),
        out_specs=out_specs or jax.tree.map(lambda _: LOCAL, out_shape),
        scratch_shapes=list(scratch),
        compiler_params=pltpu.CompilerParams(vmem_limit_bytes=limit * MIB),
        cost_estimate=pl.CostEstimate(flops=flops, bytes_accessed=moved, transcendentals=0),
    )(*args)


def exchange(blocks, axis):
    return lax.all_to_all(blocks, axis, split_axis=0, concat_axis=0, tiled=True)


def shards(noisy, probes, w_qkv, w_out, w_mod, timestep):
    rows, width = noisy.shape
    parts, frames, cores, chips = [lax.axis_size(n) for n in ("part", "frame", "core", "z")]
    seq_count = parts * frames
    probe_count = cores * chips
    frame_rows = parts * rows

    outgoing = call(
        copies_kernel,
        jax.ShapeDtypeStruct((parts, 2, rows, width), BF),
        noisy,
        probes,
        out_specs=HBM,
        scratch=(pltpu.SemaphoreType.DMA((2 * parts,)),),
        moved=2 * 10**6,
        limit=60,
    )
    gath = exchange(outgoing, "part")
    near = jnp.concatenate([w_qkv.T, w_out], axis=0).reshape(4, HEAD_DIM, width)
    half = seq_count - seq_count // 4
    far = lax.ppermute(near, SEQ, [(i, i ^ half) for i in range(seq_count)])
    mods = modulation(timestep, w_mod, width)

    part_sums = jax.ShapeDtypeStruct((parts, rows, width), BF)
    tokens = jax.ShapeDtypeStruct((frame_rows, width), BF)
    kept = (
        jax.ShapeDtypeStruct((3, frame_rows, HEAD_DIM), BF),
        jax.ShapeDtypeStruct((frame_rows, frame_rows), BF),
    )
    hidden, d_hidden, term, near_primal, near_probs = call(
        near_kernel,
        (tokens, tokens, jax.ShapeDtypeStruct((frame_rows, width), F32)) + kept,
        gath,
        near,
        mods,
        flops=10**9,
        moved=6 * 10**6,
        limit=24,
    )
    sums, far_primal, far_probs = call(
        far_kernel,
        (part_sums,) + kept,
        hidden,
        d_hidden,
        far,
        term,
        flops=10**9,
        moved=4 * 10**6,
        limit=24,
    )
    sums = exchange(sums, "part")
    gated, update = call(
        update_kernel,
        (part_sums, jax.ShapeDtypeStruct((rows, width), F32)),
        sums,
        probes,
        mods,
        moved=10**6,
    )
    gated = exchange(gated, "part")
    sums = call(
        adjoint_kernel,
        part_sums,
        gated,
        near,
        near_primal,
        near_probs,
        far,
        far_primal,
        far_probs,
        flops=2 * 10**9,
        moved=5 * 10**6,
        limit=24,
    )
    sums = exchange(sums, "part")
    by_row = jax.ShapeDtypeStruct((rows, 1, width), F32)
    pulled = call(pulled_kernel, by_row, sums, update, noisy, mods, moved=10**6)
    sub_count = rows // probe_count
    by_probe = exchange(pulled, PROBE).reshape(probe_count, 1, sub_count * width)
    high = probe_count * probe_count // LANES

    def blocks_of(count):
        return jax.ShapeDtypeStruct((count, high, LANES), F32)

    grams, flat = call(
        functools.partial(gram_kernel, 1.0 / float(seq_count * rows * width)),
        (blocks_of(cores * seq_count), jax.ShapeDtypeStruct((probe_count, sub_count * width), F32)),
        by_probe,
        moved=10**5,
    )
    grams = exchange(grams, ("core",) + SEQ)
    grams = call(total_kernel, blocks_of(chips), grams, moved=10**5)
    factor, solved = call(
        solve_kernel,
        (
            jax.ShapeDtypeStruct((probe_count, probe_count), F32),
            jax.ShapeDtypeStruct((rows, 2, width // 2), BF),
        ),
        exchange(grams, "z"),
        flat,
        moved=3 * 10**5,
    )
    halves = exchange(solved, PROBE)
    basis = call(
        basis_kernel, jax.ShapeDtypeStruct((1, rows, width), F32), halves, moved=3 * 10**5
    )
    return basis, factor


def solution(mesh):
    split = Mesh(
        mesh.devices.reshape(
            mesh.shape["probe"] // 2, 2, FRAMES, mesh.shape["seq"] // FRAMES
        ),
        PROBE + SEQ,
    )
    placed = (P(SEQ, None), P(PROBE, SEQ, None), P(None, SEQ), P(SEQ, None), P(), P())
    return jax.shard_map(
        shards,
        mesh=split,
        in_specs=placed,
        out_specs=(P(PROBE, SEQ, None), P()),
        check_vma=False,
    )
```

time: 371 us -> 154 us (0.42)
  waiting for transfers between devices: 134 us -> 1.95 us
  blocking collectives: 152 us -> 119 us
  matrix products: 24.6 us -> 2.95 us
  between operations: 15 us -> 1.39 us
  Pallas kernels: 0 us -> 13 us
  starting transfers between devices: 22.2 us -> 10.7 us
  other arithmetic: 11.5 us -> 0.12 us
  local copies, waits for them, and re-layouts: 10.4 us -> 3.89 us
    all_gather x2 -> x0, waiting for transfers between devices: 103 us -> none  [the longest x1 86.2 us: shards(): lax.all_gather(w_qkv, 'seq', axis=1, tiled=True)]
    psum x1 -> x0, blocking collectives: 98.9 us -> none  [shards(): gram_total = lax.psum(gram_local, ('probe', 'seq'))]
    all_to_all x3 -> x7, blocking collectives: 53.1 us -> 119 us  [exchange(): return lax.all_to_all(blocks, axis, split_axis=0, concat_axis=0, tiled=True)]
    all_to_all x4 -> x1, waiting for transfers between devices: 30.4 us -> 0.03 us  [exchange(): return lax.all_to_all(blocks, axis, split_axis=0, concat_axis=0, tiled=True)]
    dot_general x26 -> x0, matrix products: 23.4 us -> none  [the longest x1 5.59 us: shards(): jnp.dot(hidden, qkv_full, preferred_element_type=jnp.float32)]
    all_to_all x4 -> x1, starting transfers between devices: 22.2 us -> 6.09 us  [exchange(): return lax.all_to_all(blocks, axis, split_axis=0, concat_axis=0, tiled=True)]
    pallas_call x0 -> x10, Pallas kernels: none -> 13 us  [call(): pl.pallas_call(kernel, out_shape=out_shape, in_specs=where or [LOCAL] * l...]
    another operation x4 -> x0, other arithmetic: 6.03 us -> none  [the longest x3 3.59 us: shards(): lower_tri = jnp.linalg.cholesky(gram_total)]
  transfers between devices with their start and end apart: 6 -> 2, of which waited for: 6 -> 1; matrix products, arithmetic and copies ran while one was open for 6% -> 5% of each run, Pallas kernels for 0% -> 2%
where the time goes in v1:
time: 154 us; the launch traced here: 153 us
  blocking collectives  119 us (77%)
  Pallas kernels  13 us (8%)
  starting transfers between devices  10.7 us (7%)
  local copies, waits for them, and re-layouts  3.89 us (3%)
  matrix products  2.95 us (2%)
  waiting for transfers between devices  1.95 us (1%)
    all_to_all x7, blocking collectives, exchange(): return lax.all_to_all(blocks, axis, split_axis=0, concat_axis=0, tiled=True)  119 us
    pallas_call x10, Pallas kernels, call(): pl.pallas_call(kernel, out_shape=out_shape, in_specs=where or [LOCAL] * l...  13 us
    all_to_all x1, starting transfers between devices, exchange(): return lax.all_to_all(blocks, axis, split_axis=0, concat_axis=0, tiled=True)  6.09 us
    ppermute x1, starting transfers between devices, shards(): far = lax.ppermute(near, SEQ, [(i, i ^ half) for i in range(seq_count)])  4.63 us
    unnamed x9, local copies, waits for them, and re-layouts  3.88 us
  transfers between devices with their start and end apart: 2, of which 1 were waited for; matrix products, arithmetic and copies ran while one was open for 5% of the time, Pallas kernels for 2%

profile of v1, /device:TPU:1, one launch (start us, length us, event | category | flops | bytes accessed | tf_op | source)
XLA Modules:
  0.0 153.0 jit_solution(10871588035359004209)
XLA Ops:
  0.6 2.1 %shard_map.77 = bf16[8,2,32,1152]{3,2,1,0:T(8,128)(2,1)} custom-call(bf16[32,1152]{1,0:T(8,128)(2,1)} %noisy.3, bf16[1,32,1152]{2,1,0:T(8,128)(2,1)} %probe.3), custom_call_target="tpu_custom_call" | custom-call | bytes 2000000 | tf_op jit(solution)/shard_map/pallas_call | solution.py:243
  2.7 0.0 copy-start.2
  2.7 0.0 copy-start.3
  2.8 6.1 %all-to-all-start = ((bf16[8,2,32,1152]{3,2,1,0:T(8,128)(2,1)}), bf16[8,2,32,1152]{3,2,1,0:T(8,128)(2,1)S(1)}, u32[]{:S(2)}, u32[]{:S(2)}) async-start(bf16[8,2,32,1152]{3,2,1,0:T(8,128)(2,1)} %shard_map.77), calls=%async_computation | async-start | bytes 2359296 | tf_op jit(solution)/shard_map/all_to_all | solution.py:255
  8.9 0.0 copy-done.2
  8.9 0.0 copy-done.3
  8.9 0.1 pad_maximum_fusion
  8.9 4.6 %collective-permute-start = (bf16[4,72,1152]{2,1,0:T(8,128)(2,1)S(1)}, bf16[4,72,1152]{2,1,0:T(8,128)(2,1)S(1)}, u32[]{:S(2)}, u32[]{:S(2)}) collective-permute-start(bf16[4,72,1152]{2,1,0:T(8,128)(2,1)S(1)} %bitcast.12), channel_id=1, source_target_pairs={{0,12},{1,13},{2,14},{3,15},{4,8},{5,9},{6,10},{7,11},{8,4},{9,5},... | collective-permute-start | bytes 1990664 | tf_op jit(solution)/shard_map/ppermute | solution.py:278
  14.2 3.9 %copy.8 = bf16[256,3456]{0,1:T(8,128)(2,1)} copy(bf16[256,3456]{1,0:T(8,128)(2,1)} %param.10) | data formatting | bytes 3538944 | tf_op args[4]
  18.2 3.0 %fusion.2 = f32[1,3,1152]{2,0,1:T(1,128)S(1)} fusion(f32[256,1,1]{0,1,2:T(1,128)S(1)} %bitcast.20, bf16[3,1152,256]{2,1,0:T(8,128)(2,1)} %bitcast.18), kind=kOutput, calls=%fused_computation.7 | convolution fusion | flops 10616832 | bytes 1784320 | tf_op jit(solution)/shard_map/dot_general | solution.py:51
  21.1 0.0 all-to-all-done.gath
  21.1 3.1 %shard_map.78 = (bf16[256,1152]{1,0:T(8,128)(2,1)S(1)}, bf16[256,1152]{1,0:T(8,128)(2,1)S(1)}, f32[256,1152]{1,0:T(8,128)S(1)}, bf16[3,256,72]{2,1,0:T(8,128)(2,1)S(1)}, bf16[256,256]{1,0:T(8,128)(2,1)S(1)}) custom-call(bf16[8,2,32,1152]{3,2,1,0:T(8,128)(2,1)S(1)} %all-to-all-done.gath, bf16[4,72,1152]{2,1,0:T(8,128)(2,1)S(1)} %bitcast.13, ...), custom_call_target="tpu_custom_call" | custom-call | flops 1000000000 | bytes 6000000 | tf_op jit(solution)/shard_map/pallas_call | solution.py:243
  24.3 1.9 %collective-permute-done.weights.far = bf16[4,72,1152]{2,1,0:T(8,128)(2,1)S(1)} collective-permute-done((bf16[4,72,1152]{2,1,0:T(8,128)(2,1)S(1)}, bf16[4,72,1152]{2,1,0:T(8,128)(2,1)S(1)}, u32[]{:S(2)}, u32[]{:S(2)}) %collective-permute-start) | collective-permute-done | bytes 663584 | tf_op jit(solution)/shard_map/ppermute | solution.py:278
  26.2 0.0 copy-start
  26.2 1.8 %shard_map.79 = (bf16[8,32,1152]{2,1,0:T(8,128)(2,1)S(1)}, bf16[3,256,72]{2,1,0:T(8,128)(2,1)S(1)}, bf16[256,256]{1,0:T(8,128)(2,1)S(1)}) custom-call(bf16[256,1152]{1,0:T(8,128)(2,1)S(1)} %get-tuple-element.16.hidden, bf16[256,1152]{1,0:T(8,128)(2,1)S(1)} %get-tuple-element.17.d_hidden, bf16[4,72,1152]{2,1,0:T(8,128)(2,1)S(1)} %collective-permute-done.weights.far, ...), custom_call_target="tpu_custom_call" | custom-call | flops 1000000000 | bytes 4000000 | tf_op jit(solution)/shard_map/pallas_call | solution.py:243
  28.0 12.9 %all_to_all.40.parts = bf16[8,32,1152]{2,1,0:T(8,128)(2,1)S(1)} all-to-all(bf16[8,32,1152]{2,1,0:T(8,128)(2,1)S(1)} %get-tuple-element.19), channel_id=1, replica_groups=mesh['z'=16,'core'=2,'frame'=2,'part'=8] {'part'}, dimensions={0} | all-to-all | bytes 1179648 | tf_op jit(solution)/shard_map/all_to_all | solution.py:255
  40.9 0.0 copy-done
  40.9 0.1 shard_map.80
  41.0 11.2 %all_to_all.41.gated = bf16[8,32,1152]{2,1,0:T(8,128)(2,1)S(1)} all-to-all(bf16[8,32,1152]{2,1,0:T(8,128)(2,1)S(1)} %get-tuple-element.20), channel_id=1, replica_groups=mesh['z'=16,'core'=2,'frame'=2,'part'=8] {'part'}, dimensions={0} | all-to-all | bytes 1179648 | tf_op jit(solution)/shard_map/all_to_all | solution.py:255
  52.3 0.0 copy-start.1
  52.3 2.6 %shard_map.81 = bf16[8,32,1152]{2,1,0:T(8,128)(2,1)S(1)} custom-call(bf16[8,32,1152]{2,1,0:T(8,128)(2,1)S(1)} %all_to_all.41.gated, bf16[4,72,1152]{2,1,0:T(8,128)(2,1)S(1)} %bitcast.14, bf16[3,256,72]{2,1,0:T(8,128)(2,1)S(1)} %get-tuple-element.21.near_primal, bf16[256,256]{1,0:T(8,128)(2,1)S(1)} %get-tuple-element.22.near_probs, ...), custom_call_target="tpu_custom_call" | custom-call | flops 2000000000 | bytes 5000000 | tf_op jit(solution)/shard_map/pallas_call | solution.py:243
  54.9 10.4 %all_to_all.42.parts = bf16[8,32,1152]{2,1,0:T(8,128)(2,1)S(1)} all-to-all(bf16[8,32,1152]{2,1,0:T(8,128)(2,1)S(1)} %shard_map.81), channel_id=1, replica_groups=mesh['z'=16,'core'=2,'frame'=2,'part'=8] {'part'}, dimensions={0} | all-to-all | bytes 1179648 | tf_op jit(solution)/shard_map/all_to_all | solution.py:255
  65.3 0.0 copy-done.1
  65.3 0.3 shard_map.82
  65.6 37.8 %all_to_all.43.by_probe = f32[32,1,1152]{2,1,0:T(1,128)S(1)} all-to-all(f32[32,1,1152]{2,1,0:T(1,128)S(1)} %shard_map.82), channel_id=1, replica_groups=mesh['z'=16,'core'=2,'frame'=2,'part'=8] {'z','core'}, dimensions={0} | all-to-all | bytes 294912 | tf_op jit(solution)/shard_map/all_to_all | solution.py:255
  103.4 0.4 shard_map.83
  103.8 13.9 %all_to_all.44.arrived = f32[32,8,128]{2,1,0:T(8,128)S(1)} all-to-all(f32[32,8,128]{2,1,0:T(8,128)S(1)} %get-tuple-element.26), channel_id=1, replica_groups=mesh['z'=16,'core'=2,'frame'=2,'part'=8] {'core','frame','part'}, dimensions={0} | all-to-all | bytes 262144 | tf_op jit(solution)/shard_map/all_to_all | solution.py:255
  117.7 14.2 %all_to_all.45.arrived = f32[16,8,128]{2,1,0:T(8,128)S(1)} all-to-all(f32[16,8,128]{2,1,0:T(8,128)S(1)} %shard_map.84), channel_id=1, replica_groups=mesh['z'=16,'core'=2,'frame'=2,'part'=8] {'z'}, dimensions={0} | all-to-all | bytes 131072 | tf_op jit(solution)/shard_map/all_to_all | solution.py:255
  131.9 1.8 %shard_map.85 = (f32[32,32]{1,0:T(8,128)}, bf16[32,2,576]{2,1,0:T(2,128)(2,1)S(1)}) custom-call(f32[16,8,128]{2,1,0:T(8,128)S(1)} %all_to_all.45.arrived, f32[32,1152]{1,0:T(8,128)S(1)} %get-tuple-element.27.flat), custom_call_target="tpu_custom_call" | custom-call | bytes 300000 | tf_op jit(solution)/shard_map/pallas_call | solution.py:243
  133.7 18.5 %all_to_all.46.halves = bf16[32,2,576]{2,1,0:T(2,128)(2,1)S(1)} all-to-all(bf16[32,2,576]{2,1,0:T(2,128)(2,1)S(1)} %get-tuple-element.28), channel_id=1, replica_groups=mesh['z'=16,'core'=2,'frame'=2,'part'=8] {'z','core'}, dimensions={0} | all-to-all | bytes 147456 | tf_op jit(solution)/shard_map/all_to_all | solution.py:255
  152.2 0.8 shard_map.86
  (4 shorter events, 0.1 us)
Async XLA Ops:
  2.7 6.1 %copy-start.2 = (bf16[1152,216]{0,1:T(8,128)(2,1)S(1)}, bf16[1152,216]{0,1:T(8,128)(2,1)}, u32[]{:S(2)}) copy-start(bf16[1152,216]{0,1:T(8,128)(2,1)} %param.8) | copy-start | bytes 1492996
  2.7 6.1 %copy-start.3 = (bf16[72,1152]{1,0:T(8,128)(2,1)S(1)}, bf16[72,1152]{1,0:T(8,128)(2,1)}, u32[]{:S(2)}) copy-start(bf16[72,1152]{1,0:T(8,128)(2,1)} %param.9) | copy-start | bytes 497668
  2.8 18.4 %all-to-all-start = ((bf16[8,2,32,1152]{3,2,1,0:T(8,128)(2,1)}), bf16[8,2,32,1152]{3,2,1,0:T(8,128)(2,1)S(1)}, u32[]{:S(2)}, u32[]{:S(2)}) async-start(bf16[8,2,32,1152]{3,2,1,0:T(8,128)(2,1)} %shard_map.77), calls=%async_computation | async-start | bytes 2359296 | tf_op jit(solution)/shard_map/all_to_all | solution.py:255
  8.9 17.3 %collective-permute-start = (bf16[4,72,1152]{2,1,0:T(8,128)(2,1)S(1)}, bf16[4,72,1152]{2,1,0:T(8,128)(2,1)S(1)}, u32[]{:S(2)}, u32[]{:S(2)}) collective-permute-start(bf16[4,72,1152]{2,1,0:T(8,128)(2,1)S(1)} %bitcast.12), channel_id=1, source_target_pairs={{0,12},{1,13},{2,14},{3,15},{4,8},{5,9},{6,10},{7,11},{8,4},{9,5},... | collective-permute-start | bytes 1990664 | tf_op jit(solution)/shard_map/ppermute | solution.py:278
  26.2 14.7 %copy-start = (bf16[1,32,1152]{2,1,0:T(8,128)(2,1)S(1)}, bf16[1,32,1152]{2,1,0:T(8,128)(2,1)}, u32[]{:S(2)}) copy-start(bf16[1,32,1152]{2,1,0:T(8,128)(2,1)} %probe.3) | copy-start | bytes 221188
  52.3 13.0 %copy-start.1 = (bf16[32,1152]{1,0:T(8,128)(2,1)S(1)}, bf16[32,1152]{1,0:T(8,128)(2,1)}, u32[]{:S(2)}) copy-start(bf16[32,1152]{1,0:T(8,128)(2,1)} %noisy.3) | copy-start | bytes 221188

commit v2 on v1

--- a/solution.py
+++ b/solution.py
@@ -81,10 +81,20 @@
         copy.wait()
 
 
-def head_forward(hidden, d_hidden, weights, primal, probs):
+def thirds(value):
+    return [value[:, i * HEAD_DIM : (i + 1) * HEAD_DIM].astype(BF) for i in range(3)]
+
+
+def project_in(weights):
+    return weights[pl.ds(0, 3 * HEAD_DIM), :]
+
+
+def head_forward(tokens, flat_weights, weights, primal, probs):
     c = HEAD_DIM ** (-0.5)
-    q, k, v = [mm(hidden, weights[i], NT).astype(BF) for i in range(3)]
-    dq, dk, dv = [mm(d_hidden, weights[i], NT).astype(BF) for i in range(3)]
+    count = tokens.shape[0] // 2
+    projected = mm(tokens[...], project_in(flat_weights), NT)
+    q, k, v = thirds(projected[:count])
+    dq, dk, dv = thirds(projected[count:])
     scores = mm(q, k, NT) * c
     expon = jnp.exp(scores - jnp.max(scores, axis=-1, keepdims=True))
     p = (expon / jnp.sum(expon, axis=-1, keepdims=True)).astype(BF)
@@ -98,25 +108,20 @@
     return mm(out.astype(BF), weights[3])
 
 
-def near_kernel(gath, weights, mods, hidden, d_hidden, term, primal, probs):
+def near_kernel(gath, flat_weights, weights, mods, tokens, term, primal, probs):
     blocks, _, rows, _ = gath.shape
     scale = 1.0 + mods[1:2, :]
     shift = mods[0:1, :]
-
-    def block(i, carry):
+    for i in range(blocks):
         normed, inverse = normalize(gath[i, 0].astype(F32))
-        at = pl.ds(pl.multiple_of(i * rows, rows), rows)
-        hidden[at, :] = (normed * scale + shift).astype(BF)
+        tokens[pl.ds(i * rows, rows), :] = (normed * scale + shift).astype(BF)
         field = norm_tangent(gath[i, 1].astype(F32), normed, inverse)
-        d_hidden[at, :] = (field * scale).astype(BF)
-        return carry
-
-    lax.fori_loop(0, blocks, block, 0, unroll=2)
-    term[...] = head_forward(hidden[...], d_hidden[...], weights, primal, probs)
-
-
-def far_kernel(hidden, d_hidden, weights, term, parts, primal, probs):
-    total = term[...] + head_forward(hidden[...], d_hidden[...], weights, primal, probs)
+        tokens[pl.ds((blocks + i) * rows, rows), :] = (field * scale).astype(BF)
+    term[...] = head_forward(tokens, flat_weights, weights, primal, probs)
+
+
+def far_kernel(tokens, flat_weights, weights, term, parts, primal, probs):
+    total = term[...] + head_forward(tokens, flat_weights, weights, primal, probs)
     parts[...] = total.astype(BF).reshape(parts.shape)
 
 
@@ -132,14 +137,16 @@
         gated[j] = value
 
 
-def adjoint_kernel(gated, near, near_primal, near_probs, far, far_primal, far_probs, parts):
+def adjoint_kernel(
+    gated, near_flat, near, near_primal, near_probs, far_flat, far, far_primal, far_probs, parts
+):
     c = HEAD_DIM ** (-0.5)
     blocks, rows, width = gated.shape
     whole = gated[...].reshape(blocks * rows, width)
     total = None
-    for weights, primal, probs in (
-        (near, near_primal, near_probs),
-        (far, far_primal, far_probs),
+    for flat_weights, weights, primal, probs in (
+        (near_flat, near, near_primal, near_probs),
+        (far_flat, far, far_primal, far_probs),
     ):
         co = mm(whole, weights[3], NT).astype(BF)
         q, k, v = primal[0], primal[1], primal[2]
@@ -149,25 +156,32 @@
         row_dot = jnp.sum(p_float * d_probs, axis=-1, keepdims=True)
         scaled = (p_float * (d_probs - row_dot) * c).astype(BF)
         grads = (mm(scaled, k), mm(flip(scaled), q), mm(flip(p), co))
-        for i, grad in enumerate(grads):
-            term = mm(grad.astype(BF), weights[i])
-            total = term if total is None else total + term
+        grads = jnp.concatenate(grads, axis=1).astype(BF)
+        term = mm(grads, project_in(flat_weights))
+        total = term if total is None else total + term
     parts[...] = total.astype(BF).reshape(parts.shape)
 
 
-def pulled_kernel(parts, update, noisy, mods, pulled):
+def pulled_kernel(parts, update, noisy, mods, pulled, lost):
     total = parts[0].astype(F32)
     for j in range(1, parts.shape[0]):
         total = total + parts[j].astype(F32)
     normed, inverse = normalize(noisy[...].astype(F32))
     value = update[...] + norm_tangent((1.0 + mods[1:2, :]) * total, normed, inverse)
-    pulled[:, 0, :] = value
-
-
-def gram_kernel(scale, by_probe, copies, flat):
-    rows = by_probe[:, 0, :]
-    flat[...] = rows
-    gram = exact(rows, rows, NT) * scale
+    rounded = value.astype(BF)
+    lost[...] = value - rounded.astype(F32)
+    pairs, each, _ = pulled.shape
+    for i in range(pairs):
+        pulled[i] = value[i * each : (i + 1) * each].astype(BF)
+
+
+def gram_kernel(scale, core, mine, other, copies, rows):
+    first = core[0] == 0
+    for i in range(mine.shape[0]):
+        rows[2 * i] = jnp.where(first, mine[i], other[i])
+        rows[2 * i + 1] = jnp.where(first, other[i], mine[i])
+    each = [rows[:, t, :] for t in range(rows.shape[1])]
+    gram = sum(mm(row, row, NT) for row in each) * scale
     n = gram.shape[0]
     width = LANES // n
     high = n // width
@@ -188,9 +202,15 @@
         copies[j] = total
 
 
-def solve_kernel(arrived, flat, factor, solved):
+def picked(n, core):
+    row = lax.broadcasted_iota(jnp.int32, (n // 2, n), 0)
+    col = lax.broadcasted_iota(jnp.int32, (n // 2, n), 1)
+    return jnp.where(col == 2 * row + core, 1.0, 0.0)
+
+
+def solve_kernel(place, arrived, rows, lost, factor, solved, rest):
     packed = tree_sum([arrived[j] for j in range(arrived.shape[0])])
-    n = flat.shape[0]
+    n = factor.shape[0]
     width = LANES // n
     a = jnp.concatenate([packed[:, i * n : (i + 1) * n] for i in range(width)], axis=0)
     both = jnp.concatenate([a, eye(n)], axis=1)
@@ -221,20 +241,25 @@
     pivots = jnp.sum(jnp.where(row == col, both, 0.0), axis=1, keepdims=True)
     both = both / jnp.sqrt(pivots)
     factor[...] = jnp.where(col >= row, both, 0.0)[:, :n]
-    rows = exact(both[:, n:], flat[...])
-    half = solved.shape[2]
-    for i in range(2):
-        solved[:, i, :] = rows[:, i * half : (i + 1) * half].astype(BF)
-
-
-def basis_kernel(halves, basis):
-    half = halves.shape[2]
-    for i in range(2):
-        basis[0, :, i * half : (i + 1) * half] = halves[:, i, :].astype(F32)
+    own = place[0] * 2 + place[1]
+    square = jnp.where((row == own) & (col == own), both, 0.0)
+    pivot = jnp.sum(jnp.sum(square, axis=0, keepdims=True), axis=1, keepdims=True)
+    rest[...] = lost[...] * (1.0 / pivot)
+    inverse = exact(picked(n, place[1]), both[:, n:])
+    for t in range(rows.shape[1]):
+        solved[:, t, :] = exact(inverse, rows[:, t, :].astype(F32)).astype(BF)
+
+
+def basis_kernel(pairs, rest, basis):
+    count, each, _ = pairs.shape
+    for i in range(count):
+        at = slice(i * each, (i + 1) * each)
+        basis[0, at, :] = pairs[i].astype(F32) + rest[at, :]
 
 
 HBM = pl.BlockSpec(memory_space=pl.ANY)
 LOCAL = pl.BlockSpec(memory_space=pltpu.VMEM)
+SCALAR = pl.BlockSpec(memory_space=pltpu.SMEM)
 
 
 def call(
@@ -276,18 +301,23 @@
     near = jnp.concatenate([w_qkv.T, w_out], axis=0).reshape(4, HEAD_DIM, width)
     half = seq_count - seq_count // 4
     far = lax.ppermute(near, SEQ, [(i, i ^ half) for i in range(seq_count)])
+    near_flat, far_flat = [w.reshape(4 * HEAD_DIM, width) for w in (near, far)]
     mods = modulation(timestep, w_mod, width)
 
     part_sums = jax.ShapeDtypeStruct((parts, rows, width), BF)
-    tokens = jax.ShapeDtypeStruct((frame_rows, width), BF)
     kept = (
         jax.ShapeDtypeStruct((3, frame_rows, HEAD_DIM), BF),
         jax.ShapeDtypeStruct((frame_rows, frame_rows), BF),
     )
-    hidden, d_hidden, term, near_primal, near_probs = call(
+    tokens, term, near_primal, near_probs = call(
         near_kernel,
-        (tokens, tokens, jax.ShapeDtypeStruct((frame_rows, width), F32)) + kept,
+        (
+            jax.ShapeDtypeStruct((2 * frame_rows, width), BF),
+            jax.ShapeDtypeStruct((frame_rows, width), F32),
+        )
+        + kept,
         gath,
+        near_flat,
         near,
         mods,
         flops=10**9,
@@ -297,8 +327,8 @@
     sums, far_primal, far_probs = call(
         far_kernel,
         (part_sums,) + kept,
-        hidden,
-        d_hidden,
+        tokens,
+        far_flat,
         far,
         term,
         flops=10**9,
@@ -319,9 +349,11 @@
         adjoint_kernel,
         part_sums,
         gated,
+        near_flat,
         near,
         near_primal,
         near_probs,
+        far_flat,
         far,
         far_primal,
         far_probs,
@@ -330,36 +362,49 @@
         limit=24,
     )
     sums = exchange(sums, "part")
-    by_row = jax.ShapeDtypeStruct((rows, 1, width), F32)
-    pulled = call(pulled_kernel, by_row, sums, update, noisy, mods, moved=10**6)
-    sub_count = rows // probe_count
-    by_probe = exchange(pulled, PROBE).reshape(probe_count, 1, sub_count * width)
+    pairs = jax.ShapeDtypeStruct((chips, rows // chips, width), BF)
+    own_rows = jax.ShapeDtypeStruct((rows, width), F32)
+    pulled, lost = call(
+        pulled_kernel, (pairs, own_rows), sums, update, noisy, mods, moved=10**6
+    )
+    place = jnp.stack([lax.axis_index("z"), lax.axis_index("core")]).astype(jnp.int32)
+    mine = exchange(pulled, "z")
+    other = lax.ppermute(mine, "core", [(i, i ^ 1) for i in range(cores)])
     high = probe_count * probe_count // LANES
 
     def blocks_of(count):
         return jax.ShapeDtypeStruct((count, high, LANES), F32)
 
-    grams, flat = call(
+    grams, every = call(
         functools.partial(gram_kernel, 1.0 / float(seq_count * rows * width)),
-        (blocks_of(cores * seq_count), jax.ShapeDtypeStruct((probe_count, sub_count * width), F32)),
-        by_probe,
+        (
+            blocks_of(seq_count),
+            jax.ShapeDtypeStruct((probe_count, rows // chips, width), BF),
+        ),
+        place[1:],
+        mine,
+        other,
+        where=[SCALAR, LOCAL, LOCAL],
         moved=10**5,
     )
-    grams = exchange(grams, ("core",) + SEQ)
+    grams = exchange(grams, SEQ)
     grams = call(total_kernel, blocks_of(chips), grams, moved=10**5)
-    factor, solved = call(
+    factor, solved, rest = call(
         solve_kernel,
-        (
-            jax.ShapeDtypeStruct((probe_count, probe_count), F32),
-            jax.ShapeDtypeStruct((rows, 2, width // 2), BF),
-        ),
+        (jax.ShapeDtypeStruct((probe_count, probe_count), F32), pairs, own_rows),
+        place,
         exchange(grams, "z"),
-        flat,
+        every,
+        lost,
+        where=[SCALAR] + [LOCAL] * 3,
         moved=3 * 10**5,
     )
-    halves = exchange(solved, PROBE)
     basis = call(
-        basis_kernel, jax.ShapeDtypeStruct((1, rows, width), F32), halves, moved=3 * 10**5
+        basis_kernel,
+        jax.ShapeDtypeStruct((1, rows, width), F32),
+        exchange(solved, "z"),
+        rest,
+        moved=3 * 10**5,
     )
     return basis, factor
 

time: 154 us -> 149 us (0.968)
  blocking collectives: 119 us -> 87.3 us
  waiting for transfers between devices: 1.95 us -> 14.9 us
  starting transfers between devices: 10.7 us -> 22.8 us
    all_to_all x7 -> x6, blocking collectives: 119 us -> 87.3 us  [exchange(): return lax.all_to_all(blocks, axis, split_axis=0, concat_axis=0, tiled=True)]
    all_to_all x1 -> x2, waiting for transfers between devices: 0.03 us -> 11.5 us  [exchange(): return lax.all_to_all(blocks, axis, split_axis=0, concat_axis=0, tiled=True)]
    ppermute x0 -> x1, starting transfers between devices: none -> 8.55 us  [shards(): other = lax.ppermute(mine, 'core', [(i, i ^ 1) for i in range(cores)])]
    all_to_all x1 -> x2, starting transfers between devices: 6.09 us -> 9.59 us  [exchange(): return lax.all_to_all(blocks, axis, split_axis=0, concat_axis=0, tiled=True)]
  transfers between devices with their start and end apart: 2 -> 4, of which waited for: 1 -> 3; matrix products, arithmetic and copies ran while one was open for 5% -> 5% of each run, Pallas kernels for 2% -> 2%
where the time goes in v2:
time: 149 us; the launch traced here: 147 us
  blocking collectives  87.3 us (59%)
  starting transfers between devices  22.8 us (15%)
  waiting for transfers between devices  14.9 us (10%)
  Pallas kernels  13.3 us (9%)
  local copies, waits for them, and re-layouts  3.89 us (3%)
  matrix products  2.95 us (2%)
    all_to_all x6, blocking collectives, exchange(): return lax.all_to_all(blocks, axis, split_axis=0, concat_axis=0, tiled=True)  87.3 us
    pallas_call x10, Pallas kernels, call(): pl.pallas_call(kernel, out_shape=out_shape, in_specs=where or [LOCAL] * l...  13.3 us
    all_to_all x2, waiting for transfers between devices, exchange(): return lax.all_to_all(blocks, axis, split_axis=0, concat_axis=0, tiled=True)  11.5 us
    all_to_all x2, starting transfers between devices, exchange(): return lax.all_to_all(blocks, axis, split_axis=0, concat_axis=0, tiled=True)  9.59 us
    ppermute x1, starting transfers between devices, shards(): other = lax.ppermute(mine, 'core', [(i, i ^ 1) for i in range(cores)])  8.55 us
    ppermute x1, starting transfers between devices, shards(): far = lax.ppermute(near, SEQ, [(i, i ^ half) for i in range(seq_count)])  4.63 us
    unnamed x9, local copies, waits for them, and re-layouts  3.89 us
  transfers between devices with their start and end apart: 4, of which 3 were waited for; matrix products, arithmetic and copies ran while one was open for 5% of the time, Pallas kernels for 2%

profile of v2, /device:TPU:1, one launch (start us, length us, event | category | flops | bytes accessed | tf_op | source)
XLA Modules:
  0.0 146.8 jit_solution(16159649166429876104)
XLA Ops:
  0.6 2.1 %shard_map.77 = bf16[8,2,32,1152]{3,2,1,0:T(8,128)(2,1)} custom-call(bf16[32,1152]{1,0:T(8,128)(2,1)} %noisy.3, bf16[1,32,1152]{2,1,0:T(8,128)(2,1)} %probe.3), custom_call_target="tpu_custom_call" | custom-call | bytes 2000000 | tf_op jit(solution)/shard_map/pallas_call | solution.py:268
  2.7 0.0 copy-start.2
  2.8 0.0 copy-start.3
  2.8 6.1 %all-to-all-start = ((bf16[8,2,32,1152]{3,2,1,0:T(8,128)(2,1)}), bf16[8,2,32,1152]{3,2,1,0:T(8,128)(2,1)S(1)}, u32[]{:S(2)}, u32[]{:S(2)}) async-start(bf16[8,2,32,1152]{3,2,1,0:T(8,128)(2,1)} %shard_map.77), calls=%async_computation | async-start | bytes 2359296 | tf_op jit(solution)/shard_map/all_to_all | solution.py:280
  8.9 0.0 copy-done.2
  8.9 0.1 pad_maximum_fusion.flat_weights.near_flat
  8.9 4.6 %collective-permute-start = (bf16[4,72,1152]{2,1,0:T(8,128)(2,1)S(1)}, bf16[4,72,1152]{2,1,0:T(8,128)(2,1)S(1)}, u32[]{:S(2)}, u32[]{:S(2)}) collective-permute-start(bf16[4,72,1152]{2,1,0:T(8,128)(2,1)S(1)} %bitcast.15), channel_id=1, source_target_pairs={{0,12},{1,13},{2,14},{3,15},{4,8},{5,9},{6,10},{7,11},{8,4},{9,5},... | collective-permute-start | bytes 1990664 | tf_op jit(solution)/shard_map/ppermute | solution.py:303
  14.2 3.9 %copy.8 = bf16[256,3456]{0,1:T(8,128)(2,1)} copy(bf16[256,3456]{1,0:T(8,128)(2,1)} %param.10) | data formatting | bytes 3538944 | tf_op args[4]
  18.2 3.0 %fusion.2 = f32[1,3,1152]{2,0,1:T(1,128)S(1)} fusion(f32[256,1,1]{0,1,2:T(1,128)S(1)} %bitcast.25, bf16[3,1152,256]{2,1,0:T(8,128)(2,1)} %bitcast.23), kind=kOutput, calls=%fused_computation.8 | convolution fusion | flops 10616832 | bytes 1784320 | tf_op jit(solution)/shard_map/dot_general | solution.py:51
  21.1 0.0 all-to-all-done.gath
  21.2 2.6 %shard_map.78 = (bf16[512,1152]{1,0:T(8,128)(2,1)S(1)}, f32[256,1152]{1,0:T(8,128)S(1)}, bf16[3,256,72]{2,1,0:T(8,128)(2,1)S(1)}, bf16[256,256]{1,0:T(8,128)(2,1)S(1)}) custom-call(bf16[8,2,32,1152]{3,2,1,0:T(8,128)(2,1)S(1)} %all-to-all-done.gath, bf16[288,1152]{1,0:T(8,128)(2,1)S(1)} %pad_maximum_fusion.flat_weights.near_flat, ...), custom_call_target="tpu_custom_call" | custom-call | flops 1000000000 | bytes 6000000 | tf_op jit(solution)/shard_map/pallas_call | solution.py:268
  23.7 2.5 %collective-permute-done.weights.far = bf16[4,72,1152]{2,1,0:T(8,128)(2,1)S(1)} collective-permute-done((bf16[4,72,1152]{2,1,0:T(8,128)(2,1)S(1)}, bf16[4,72,1152]{2,1,0:T(8,128)(2,1)S(1)}, u32[]{:S(2)}, u32[]{:S(2)}) %collective-permute-start) | collective-permute-done | bytes 663584 | tf_op jit(solution)/shard_map/ppermute | solution.py:303
  26.2 1.9 %shard_map.79 = (bf16[8,32,1152]{2,1,0:T(8,128)(2,1)S(1)}, bf16[3,256,72]{2,1,0:T(8,128)(2,1)S(1)}, bf16[256,256]{1,0:T(8,128)(2,1)S(1)}) custom-call(bf16[512,1152]{1,0:T(8,128)(2,1)S(1)} %get-tuple-element.18.tokens, bf16[288,1152]{1,0:T(8,128)(2,1)S(1)} %bitcast.21, bf16[4,72,1152]{2,1,0:T(8,128)(2,1)S(1)} %collective-permute-done.weights.far, ...), custom_call_target="tpu_custom_call" | custom-call | flops 1000000000 | bytes 4000000 | tf_op jit(solution)/shard_map/pallas_call | solution.py:268
  28.1 12.4 %all_to_all.40.parts = bf16[8,32,1152]{2,1,0:T(8,128)(2,1)S(1)} all-to-all(bf16[8,32,1152]{2,1,0:T(8,128)(2,1)S(1)} %get-tuple-element.20), channel_id=1, replica_groups=mesh['z'=16,'core'=2,'frame'=2,'part'=8] {'part'}, dimensions={0} | all-to-all | bytes 1179648 | tf_op jit(solution)/shard_map/all_to_all | solution.py:280
  40.6 0.1 shard_map.80
  40.7 10.4 %all_to_all.41.gated = bf16[8,32,1152]{2,1,0:T(8,128)(2,1)S(1)} all-to-all(bf16[8,32,1152]{2,1,0:T(8,128)(2,1)S(1)} %get-tuple-element.21), channel_id=1, replica_groups=mesh['z'=16,'core'=2,'frame'=2,'part'=8] {'part'}, dimensions={0} | all-to-all | bytes 1179648 | tf_op jit(solution)/shard_map/all_to_all | solution.py:280
  51.1 2.1 %shard_map.81 = bf16[8,32,1152]{2,1,0:T(8,128)(2,1)S(1)} custom-call(bf16[8,32,1152]{2,1,0:T(8,128)(2,1)S(1)} %all_to_all.41.gated, bf16[288,1152]{1,0:T(8,128)(2,1)S(1)} %pad_maximum_fusion.flat_weights.near_flat, bf16[4,72,1152]{2,1,0:T(8,128)(2,1)S(1)} %bitcast.17, bf16[3,256,72]{2,1,0:T(8,128)(2,1)S(1)} %get-tuple-element.22.near_primal, ...), custom_call_target="tpu_custom_call" | custom-call | flops 2000000000 | bytes 5000000 | tf_op jit(solution)/shard_map/pallas_call | solution.py:268
  53.2 10.4 %all_to_all.42.parts = bf16[8,32,1152]{2,1,0:T(8,128)(2,1)S(1)} all-to-all(bf16[8,32,1152]{2,1,0:T(8,128)(2,1)S(1)} %shard_map.81), channel_id=1, replica_groups=mesh['z'=16,'core'=2,'frame'=2,'part'=8] {'part'}, dimensions={0} | all-to-all | bytes 1179648 | tf_op jit(solution)/shard_map/all_to_all | solution.py:280
  63.6 0.0 copy-done
  63.6 0.3 shard_map.82
  63.9 28.1 %all_to_all.43.mine = bf16[16,2,1152]{2,1,0:T(2,128)(2,1)S(1)} all-to-all(bf16[16,2,1152]{2,1,0:T(2,128)(2,1)S(1)} %get-tuple-element.27), channel_id=1, replica_groups=mesh['z'=16,'core'=2,'frame'=2,'part'=8] {'z'}, dimensions={0} | all-to-all | bytes 147456 | tf_op jit(solution)/shard_map/all_to_all | solution.py:280
  92.0 8.5 %collective-permute-start.1 = (bf16[16,2,1152]{2,1,0:T(2,128)(2,1)S(1)}, bf16[16,2,1152]{2,1,0:T(2,128)(2,1)S(1)}, u32[]{:S(2)}, u32[]{:S(2)}) collective-permute-start(bf16[16,2,1152]{2,1,0:T(2,128)(2,1)S(1)} %all_to_all.43.mine), channel_id=1, source_target_pairs={{0,16},{16,0},{1,17},{17,1},{2,18},{18,2},{3,19},{19,3},{4,20},{20... | collective-permute-start | bytes 221192 | tf_op jit(solution)/shard_map/ppermute | solution.py:372
  100.6 0.9 collective-permute-done.1.other
  101.4 0.5 shard_map.83
  102.0 11.6 %all_to_all.44.arrived = f32[16,8,128]{2,1,0:T(8,128)S(1)} all-to-all(f32[16,8,128]{2,1,0:T(8,128)S(1)} %get-tuple-element.28), channel_id=1, replica_groups=mesh['z'=16,'core'=2,'frame'=2,'part'=8] {'frame','part'}, dimensions={0} | all-to-all | bytes 131072 | tf_op jit(solution)/shard_map/all_to_all | solution.py:280
  113.6 0.6 shard_map.84
  114.2 3.5 %all-to-all-start.6 = ((f32[16,8,128]{2,1,0:T(8,128)}), f32[16,8,128]{2,1,0:T(8,128)S(1)}, u32[]{:S(2)}, u32[]{:S(2)}) async-start(f32[16,8,128]{2,1,0:T(8,128)} %shard_map.84), calls=%async_computation.6 | async-start | bytes 131072 | tf_op jit(solution)/shard_map/all_to_all | solution.py:280
  117.7 0.1 pad_add_fusion.place
  117.8 11.5 %all-to-all-done.6.arrived = f32[16,8,128]{2,1,0:T(8,128)S(1)} async-done(((f32[16,8,128]{2,1,0:T(8,128)}), f32[16,8,128]{2,1,0:T(8,128)S(1)}, u32[]{:S(2)}, u32[]{:S(2)}) %all-to-all-start.6) | async-done | bytes 65568 | tf_op jit(solution)/shard_map/all_to_all | solution.py:280
  129.3 2.3 %shard_map.85 = (f32[32,32]{1,0:T(8,128)}, bf16[16,2,1152]{2,1,0:T(2,128)(2,1)S(1)}, f32[32,1152]{1,0:T(8,128)S(1)}) custom-call(s32[2]{0:T(128)S(1)} %pad_add_fusion.place, f32[16,8,128]{2,1,0:T(8,128)S(1)} %all-to-all-done.6.arrived, bf16[32,2,1152]{2,1,0:T(2,128)(2,1)S(1)} %get-tuple-element.29.rows, f32[32,1152]{1,0:T(8,128)S(1)} %get-tuple-element.30.lost), custom_call_target="tpu_custom_call" | custom-call | bytes 300000 | tf_op jit(solution)/shard_map/pallas_call | solution.py:268
  131.6 14.4 %all_to_all.45.pairs = bf16[16,2,1152]{2,1,0:T(2,128)(2,1)S(1)} all-to-all(bf16[16,2,1152]{2,1,0:T(2,128)(2,1)S(1)} %get-tuple-element.31), channel_id=1, replica_groups=mesh['z'=16,'core'=2,'frame'=2,'part'=8] {'z'}, dimensions={0} | all-to-all | bytes 147456 | tf_op jit(solution)/shard_map/all_to_all | solution.py:280
  146.0 0.7 shard_map.86
  (7 shorter events, 0.1 us)
Async XLA Ops:
  2.7 6.1 %copy-start.2 = (bf16[1152,216]{0,1:T(8,128)(2,1)S(1)}, bf16[1152,216]{0,1:T(8,128)(2,1)}, u32[]{:S(2)}) copy-start(bf16[1152,216]{0,1:T(8,128)(2,1)} %param.8) | copy-start | bytes 1492996
  2.8 6.1 %copy-start.3 = (bf16[72,1152]{1,0:T(8,128)(2,1)S(1)}, bf16[72,1152]{1,0:T(8,128)(2,1)}, u32[]{:S(2)}) copy-start(bf16[72,1152]{1,0:T(8,128)(2,1)} %param.9) | copy-start | bytes 497668
  2.8 18.4 %all-to-all-start = ((bf16[8,2,32,1152]{3,2,1,0:T(8,128)(2,1)}), bf16[8,2,32,1152]{3,2,1,0:T(8,128)(2,1)S(1)}, u32[]{:S(2)}, u32[]{:S(2)}) async-start(bf16[8,2,32,1152]{3,2,1,0:T(8,128)(2,1)} %shard_map.77), calls=%async_computation | async-start | bytes 2359296 | tf_op jit(solution)/shard_map/all_to_all | solution.py:280
  8.9 17.3 %collective-permute-start = (bf16[4,72,1152]{2,1,0:T(8,128)(2,1)S(1)}, bf16[4,72,1152]{2,1,0:T(8,128)(2,1)S(1)}, u32[]{:S(2)}, u32[]{:S(2)}) collective-permute-start(bf16[4,72,1152]{2,1,0:T(8,128)(2,1)S(1)} %bitcast.15), channel_id=1, source_target_pairs={{0,12},{1,13},{2,14},{3,15},{4,8},{5,9},{6,10},{7,11},{8,4},{9,5},... | collective-permute-start | bytes 1990664 | tf_op jit(solution)/shard_map/ppermute | solution.py:303
  26.2 14.3 %copy-start.1 = (bf16[1,32,1152]{2,1,0:T(8,128)(2,1)S(1)}, bf16[1,32,1152]{2,1,0:T(8,128)(2,1)}, u32[]{:S(2)}) copy-start(bf16[1,32,1152]{2,1,0:T(8,128)(2,1)} %probe.3) | copy-start | bytes 221188
  51.1 12.5 %copy-start = (bf16[32,1152]{1,0:T(8,128)(2,1)S(1)}, bf16[32,1152]{1,0:T(8,128)(2,1)}, u32[]{:S(2)}) copy-start(bf16[32,1152]{1,0:T(8,128)(2,1)} %noisy.3) | copy-start | bytes 221188
  92.0 9.4 %collective-permute-start.1 = (bf16[16,2,1152]{2,1,0:T(2,128)(2,1)S(1)}, bf16[16,2,1152]{2,1,0:T(2,128)(2,1)S(1)}, u32[]{:S(2)}, u32[]{:S(2)}) collective-permute-start(bf16[16,2,1152]{2,1,0:T(2,128)(2,1)S(1)} %all_to_all.43.mine), channel_id=1, source_target_pairs={{0,16},{16,0},{1,17},{17,1},{2,18},{18,2},{3,19},{19,3},{4,20},{20... | collective-permute-start | bytes 221192 | tf_op jit(solution)/shard_map/ppermute | solution.py:372
  114.2 15.1 %all-to-all-start.6 = ((f32[16,8,128]{2,1,0:T(8,128)}), f32[16,8,128]{2,1,0:T(8,128)S(1)}, u32[]{:S(2)}, u32[]{:S(2)}) async-start(f32[16,8,128]{2,1,0:T(8,128)} %shard_map.84), calls=%async_computation.6 | async-start | bytes 131072 | tf_op jit(solution)/shard_map/all_to_all | solution.py:280

commit v3 on v2

--- a/solution.py
+++ b/solution.py
@@ -73,11 +73,11 @@
     return copies
 
 
-def copies_kernel(noisy, probe, out, sems):
+def copies_kernel(noisy, probe, out, staged, sems):
     count = out.shape[0]
-    pairs = [(noisy, out.at[j, 0]) for j in range(count)]
-    pairs += [(probe.at[0], out.at[j, 1]) for j in range(count)]
-    for copy in fetch(pairs, sems):
+    for copy in fetch([(noisy, staged.at[0]), (probe.at[0], staged.at[1])], sems):
+        copy.wait()
+    for copy in fetch([(staged, out.at[j]) for j in range(count)], sems.at[pl.ds(2, count)]):
         copy.wait()
 
 
@@ -97,7 +97,7 @@
     dq, dk, dv = thirds(projected[count:])
     scores = mm(q, k, NT) * c
     expon = jnp.exp(scores - jnp.max(scores, axis=-1, keepdims=True))
-    p = (expon / jnp.sum(expon, axis=-1, keepdims=True)).astype(BF)
+    p = (expon * (1.0 / jnp.sum(expon, axis=-1, keepdims=True))).astype(BF)
     d_scores = (mm(dq, k, NT) + mm(q, dk, NT)) * c
     mixed = p.astype(F32) * d_scores
     row_sum = jnp.sum(mixed, axis=-1, keepdims=True)
@@ -175,8 +175,8 @@
         pulled[i] = value[i * each : (i + 1) * each].astype(BF)
 
 
-def gram_kernel(scale, core, mine, other, copies, rows):
-    first = core[0] == 0
+def gram_kernel(scale, mine, other, copies, rows):
+    first = lax.axis_index("core") == 0
     for i in range(mine.shape[0]):
         rows[2 * i] = jnp.where(first, mine[i], other[i])
         rows[2 * i + 1] = jnp.where(first, other[i], mine[i])
@@ -208,7 +208,7 @@
     return jnp.where(col == 2 * row + core, 1.0, 0.0)
 
 
-def solve_kernel(place, arrived, rows, lost, factor, solved, rest):
+def solve_kernel(arrived, rows, lost, factor, solved, rest):
     packed = tree_sum([arrived[j] for j in range(arrived.shape[0])])
     n = factor.shape[0]
     width = LANES // n
@@ -241,13 +241,23 @@
     pivots = jnp.sum(jnp.where(row == col, both, 0.0), axis=1, keepdims=True)
     both = both / jnp.sqrt(pivots)
     factor[...] = jnp.where(col >= row, both, 0.0)[:, :n]
-    own = place[0] * 2 + place[1]
+    core = lax.axis_index("core")
+    own = lax.axis_index("z") * 2 + core
     square = jnp.where((row == own) & (col == own), both, 0.0)
     pivot = jnp.sum(jnp.sum(square, axis=0, keepdims=True), axis=1, keepdims=True)
     rest[...] = lost[...] * (1.0 / pivot)
-    inverse = exact(picked(n, place[1]), both[:, n:])
+    remains = both[:, n:]
+    choice = picked(n, core).astype(BF)
+    pieces = []
+    for _ in range(3):
+        piece = remains.astype(BF)
+        pieces.append(mm(choice, piece))
+        remains = remains - piece.astype(F32)
+    pieces = jnp.concatenate(pieces, axis=0).astype(BF)
     for t in range(rows.shape[1]):
-        solved[:, t, :] = exact(inverse, rows[:, t, :].astype(F32)).astype(BF)
+        product = mm(pieces, rows[:, t, :])
+        high, middle, low = [product[i * n // 2 : (i + 1) * n // 2] for i in range(3)]
+        solved[:, t, :] = (high + (middle + low)).astype(BF)
 
 
 def basis_kernel(pairs, rest, basis):
@@ -259,7 +269,6 @@
 
 HBM = pl.BlockSpec(memory_space=pl.ANY)
 LOCAL = pl.BlockSpec(memory_space=pltpu.VMEM)
-SCALAR = pl.BlockSpec(memory_space=pltpu.SMEM)
 
 
 def call(
@@ -292,8 +301,12 @@
         jax.ShapeDtypeStruct((parts, 2, rows, width), BF),
         noisy,
         probes,
+        where=[HBM, HBM],
         out_specs=HBM,
-        scratch=(pltpu.SemaphoreType.DMA((2 * parts,)),),
+        scratch=(
+            pltpu.VMEM((2, rows, width), BF),
+            pltpu.SemaphoreType.DMA((2 + parts,)),
+        ),
         moved=2 * 10**6,
         limit=60,
     )
@@ -367,7 +380,6 @@
     pulled, lost = call(
         pulled_kernel, (pairs, own_rows), sums, update, noisy, mods, moved=10**6
     )
-    place = jnp.stack([lax.axis_index("z"), lax.axis_index("core")]).astype(jnp.int32)
     mine = exchange(pulled, "z")
     other = lax.ppermute(mine, "core", [(i, i ^ 1) for i in range(cores)])
     high = probe_count * probe_count // LANES
@@ -381,10 +393,8 @@
             blocks_of(seq_count),
             jax.ShapeDtypeStruct((probe_count, rows // chips, width), BF),
         ),
-        place[1:],
         mine,
         other,
-        where=[SCALAR, LOCAL, LOCAL],
         moved=10**5,
     )
     grams = exchange(grams, SEQ)
@@ -392,11 +402,9 @@
     factor, solved, rest = call(
         solve_kernel,
         (jax.ShapeDtypeStruct((probe_count, probe_count), F32), pairs, own_rows),
-        place,
         exchange(grams, "z"),
         every,
         lost,
-        where=[SCALAR] + [LOCAL] * 3,
         moved=3 * 10**5,
     )
     basis = call(

time: 149 us -> 148 us (level)
  blocking collectives: 87.3 us -> 102 us
  waiting for transfers between devices: 14.9 us -> 3.4 us
  starting transfers between devices: 22.8 us -> 19.3 us
    all_to_all x6 -> x7, blocking collectives: 87.3 us -> 102 us  [exchange(): return lax.all_to_all(blocks, axis, split_axis=0, concat_axis=0, tiled=True)]
    all_to_all x2 -> x1, waiting for transfers between devices: 11.5 us -> 0.03 us  [exchange(): return lax.all_to_all(blocks, axis, split_axis=0, concat_axis=0, tiled=True)]
    all_to_all x2 -> x1, starting transfers between devices: 9.59 us -> 6.09 us  [exchange(): return lax.all_to_all(blocks, axis, split_axis=0, concat_axis=0, tiled=True)]
  transfers between devices with their start and end apart: 4 -> 3, of which waited for: 3 -> 2; matrix products, arithmetic and copies ran while one was open for 5% -> 5% of each run, Pallas kernels for 2% -> 2%
where the time goes in v3:
time: 148 us; the launch traced here: 145 us
  blocking collectives  102 us (69%)
  starting transfers between devices  19.3 us (13%)
  Pallas kernels  12.6 us (9%)
  local copies, waits for them, and re-layouts  3.91 us (3%)
  waiting for transfers between devices  3.4 us (2%)
  matrix products  2.95 us (2%)
    all_to_all x7, blocking collectives, exchange(): return lax.all_to_all(blocks, axis, split_axis=0, concat_axis=0, tiled=True)  102 us
    pallas_call x10, Pallas kernels, call(): pl.pallas_call(kernel, out_shape=out_shape, in_specs=where or [LOCAL] * l...  12.6 us
    ppermute x1, starting transfers between devices, shards(): other = lax.ppermute(mine, 'core', [(i, i ^ 1) for i in range(cores)])  8.55 us
    all_to_all x1, starting transfers between devices, exchange(): return lax.all_to_all(blocks, axis, split_axis=0, concat_axis=0, tiled=True)  6.09 us
    ppermute x1, starting transfers between devices, shards(): far = lax.ppermute(near, SEQ, [(i, i ^ half) for i in range(seq_count)])  4.63 us
    unnamed x9, local copies, waits for them, and re-layouts  3.9 us
  transfers between devices with their start and end apart: 3, of which 2 were waited for; matrix products, arithmetic and copies ran while one was open for 5% of the time, Pallas kernels for 2%

profile of v3, /device:TPU:1, one launch (start us, length us, event | category | flops | bytes accessed | tf_op | source)
XLA Modules:
  0.0 145.1 jit_solution(15335143036522247653)
XLA Ops:
  0.6 2.1 %shard_map.77 = bf16[8,2,32,1152]{3,2,1,0:T(8,128)(2,1)} custom-call(bf16[32,1152]{1,0:T(8,128)(2,1)} %noisy.3, bf16[1,32,1152]{2,1,0:T(8,128)(2,1)} %probe.3), custom_call_target="tpu_custom_call" | custom-call | bytes 2000000 | tf_op jit(solution)/shard_map/pallas_call | solution.py:277
  2.7 0.0 copy-start.2
  2.7 0.0 copy-start.3
  2.7 6.1 %all-to-all-start = ((bf16[8,2,32,1152]{3,2,1,0:T(8,128)(2,1)}), bf16[8,2,32,1152]{3,2,1,0:T(8,128)(2,1)S(1)}, u32[]{:S(2)}, u32[]{:S(2)}) async-start(bf16[8,2,32,1152]{3,2,1,0:T(8,128)(2,1)} %shard_map.77), calls=%async_computation | async-start | bytes 2359296 | tf_op jit(solution)/shard_map/all_to_all | solution.py:289
  8.8 0.0 copy-done.2
  8.8 0.0 copy-done.3
  8.8 0.1 pad_maximum_fusion.flat_weights.near_flat
  8.9 4.6 %collective-permute-start = (bf16[4,72,1152]{2,1,0:T(8,128)(2,1)S(1)}, bf16[4,72,1152]{2,1,0:T(8,128)(2,1)S(1)}, u32[]{:S(2)}, u32[]{:S(2)}) collective-permute-start(bf16[4,72,1152]{2,1,0:T(8,128)(2,1)S(1)} %bitcast.13), channel_id=1, source_target_pairs={{0,12},{1,13},{2,14},{3,15},{4,8},{5,9},{6,10},{7,11},{8,4},{9,5},... | collective-permute-start | bytes 1990664 | tf_op jit(solution)/shard_map/ppermute | solution.py:316
  14.2 3.9 %copy.8 = bf16[256,3456]{0,1:T(8,128)(2,1)} copy(bf16[256,3456]{1,0:T(8,128)(2,1)} %param.10) | data formatting | bytes 3538944 | tf_op args[4]
  18.1 3.0 %fusion.2 = f32[1,3,1152]{2,0,1:T(1,128)S(1)} fusion(f32[256,1,1]{0,1,2:T(1,128)S(1)} %bitcast.23, bf16[3,1152,256]{2,1,0:T(8,128)(2,1)} %bitcast.21), kind=kOutput, calls=%fused_computation.7 | convolution fusion | flops 10616832 | bytes 1784320 | tf_op jit(solution)/shard_map/dot_general | solution.py:51
  21.1 0.0 all-to-all-done.gath
  21.1 2.6 %shard_map.78 = (bf16[512,1152]{1,0:T(8,128)(2,1)S(1)}, f32[256,1152]{1,0:T(8,128)S(1)}, bf16[3,256,72]{2,1,0:T(8,128)(2,1)S(1)}, bf16[256,256]{1,0:T(8,128)(2,1)S(1)}) custom-call(bf16[8,2,32,1152]{3,2,1,0:T(8,128)(2,1)S(1)} %all-to-all-done.gath, bf16[288,1152]{1,0:T(8,128)(2,1)S(1)} %pad_maximum_fusion.flat_weights.near_flat, ...), custom_call_target="tpu_custom_call" | custom-call | flops 1000000000 | bytes 6000000 | tf_op jit(solution)/shard_map/pallas_call | solution.py:277
  23.7 2.5 %collective-permute-done.weights.far = bf16[4,72,1152]{2,1,0:T(8,128)(2,1)S(1)} collective-permute-done((bf16[4,72,1152]{2,1,0:T(8,128)(2,1)S(1)}, bf16[4,72,1152]{2,1,0:T(8,128)(2,1)S(1)}, u32[]{:S(2)}, u32[]{:S(2)}) %collective-permute-start) | collective-permute-done | bytes 663584 | tf_op jit(solution)/shard_map/ppermute | solution.py:316
  26.2 0.0 copy-start.1
  26.2 1.9 %shard_map.79 = (bf16[8,32,1152]{2,1,0:T(8,128)(2,1)S(1)}, bf16[3,256,72]{2,1,0:T(8,128)(2,1)S(1)}, bf16[256,256]{1,0:T(8,128)(2,1)S(1)}) custom-call(bf16[512,1152]{1,0:T(8,128)(2,1)S(1)} %get-tuple-element.18.tokens, bf16[288,1152]{1,0:T(8,128)(2,1)S(1)} %bitcast.19, bf16[4,72,1152]{2,1,0:T(8,128)(2,1)S(1)} %collective-permute-done.weights.far, ...), custom_call_target="tpu_custom_call" | custom-call | flops 1000000000 | bytes 4000000 | tf_op jit(solution)/shard_map/pallas_call | solution.py:277
  28.1 12.4 %all_to_all.40.parts = bf16[8,32,1152]{2,1,0:T(8,128)(2,1)S(1)} all-to-all(bf16[8,32,1152]{2,1,0:T(8,128)(2,1)S(1)} %get-tuple-element.20), channel_id=1, replica_groups=mesh['z'=16,'core'=2,'frame'=2,'part'=8] {'part'}, dimensions={0} | all-to-all | bytes 1179648 | tf_op jit(solution)/shard_map/all_to_all | solution.py:289
  40.5 0.0 copy-done.1
  40.5 0.1 shard_map.80
  40.6 10.4 %all_to_all.41.gated = bf16[8,32,1152]{2,1,0:T(8,128)(2,1)S(1)} all-to-all(bf16[8,32,1152]{2,1,0:T(8,128)(2,1)S(1)} %get-tuple-element.21), channel_id=1, replica_groups=mesh['z'=16,'core'=2,'frame'=2,'part'=8] {'part'}, dimensions={0} | all-to-all | bytes 1179648 | tf_op jit(solution)/shard_map/all_to_all | solution.py:289
  51.0 2.1 %shard_map.81 = bf16[8,32,1152]{2,1,0:T(8,128)(2,1)S(1)} custom-call(bf16[8,32,1152]{2,1,0:T(8,128)(2,1)S(1)} %all_to_all.41.gated, bf16[288,1152]{1,0:T(8,128)(2,1)S(1)} %pad_maximum_fusion.flat_weights.near_flat, bf16[4,72,1152]{2,1,0:T(8,128)(2,1)S(1)} %bitcast.15, bf16[3,256,72]{2,1,0:T(8,128)(2,1)S(1)} %get-tuple-element.22.near_primal, ...), custom_call_target="tpu_custom_call" | custom-call | flops 2000000000 | bytes 5000000 | tf_op jit(solution)/shard_map/pallas_call | solution.py:277
  53.2 10.4 %all_to_all.42.parts = bf16[8,32,1152]{2,1,0:T(8,128)(2,1)S(1)} all-to-all(bf16[8,32,1152]{2,1,0:T(8,128)(2,1)S(1)} %shard_map.81), channel_id=1, replica_groups=mesh['z'=16,'core'=2,'frame'=2,'part'=8] {'part'}, dimensions={0} | all-to-all | bytes 1179648 | tf_op jit(solution)/shard_map/all_to_all | solution.py:289
  63.5 0.0 copy-done
  63.5 0.3 shard_map.82
  63.9 28.1 %all_to_all.43.mine = bf16[16,2,1152]{2,1,0:T(2,128)(2,1)S(1)} all-to-all(bf16[16,2,1152]{2,1,0:T(2,128)(2,1)S(1)} %get-tuple-element.27), channel_id=1, replica_groups=mesh['z'=16,'core'=2,'frame'=2,'part'=8] {'z'}, dimensions={0} | all-to-all | bytes 147456 | tf_op jit(solution)/shard_map/all_to_all | solution.py:289
  91.9 8.5 %collective-permute-start.1 = (bf16[16,2,1152]{2,1,0:T(2,128)(2,1)S(1)}, bf16[16,2,1152]{2,1,0:T(2,128)(2,1)S(1)}, u32[]{:S(2)}, u32[]{:S(2)}) collective-permute-start(bf16[16,2,1152]{2,1,0:T(2,128)(2,1)S(1)} %all_to_all.43.mine), channel_id=1, source_target_pairs={{0,16},{16,0},{1,17},{17,1},{2,18},{18,2},{3,19},{19,3},{4,20},{20... | collective-permute-start | bytes 221192 | tf_op jit(solution)/shard_map/ppermute | solution.py:384
  100.5 0.9 collective-permute-done.1.other
  101.4 0.5 shard_map.83
  101.9 11.6 %all_to_all.44.arrived = f32[16,8,128]{2,1,0:T(8,128)S(1)} all-to-all(f32[16,8,128]{2,1,0:T(8,128)S(1)} %get-tuple-element.28), channel_id=1, replica_groups=mesh['z'=16,'core'=2,'frame'=2,'part'=8] {'frame','part'}, dimensions={0} | all-to-all | bytes 131072 | tf_op jit(solution)/shard_map/all_to_all | solution.py:289
  113.5 14.2 %all_to_all.45.arrived = f32[16,8,128]{2,1,0:T(8,128)S(1)} all-to-all(f32[16,8,128]{2,1,0:T(8,128)S(1)} %shard_map.84), channel_id=1, replica_groups=mesh['z'=16,'core'=2,'frame'=2,'part'=8] {'z'}, dimensions={0} | all-to-all | bytes 131072 | tf_op jit(solution)/shard_map/all_to_all | solution.py:289
  127.8 2.2 %shard_map.85 = (f32[32,32]{1,0:T(8,128)}, bf16[16,2,1152]{2,1,0:T(2,128)(2,1)S(1)}, f32[32,1152]{1,0:T(8,128)S(1)}) custom-call(f32[16,8,128]{2,1,0:T(8,128)S(1)} %all_to_all.45.arrived, bf16[32,2,1152]{2,1,0:T(2,128)(2,1)S(1)} %get-tuple-element.29.rows, f32[32,1152]{1,0:T(8,128)S(1)} %get-tuple-element.30.lost), custom_call_target="tpu_custom_call" | custom-call | bytes 300000 | tf_op jit(solution)/shard_map/pallas_call | solution.py:277
  130.0 14.4 %all_to_all.46.pairs = bf16[16,2,1152]{2,1,0:T(2,128)(2,1)S(1)} all-to-all(bf16[16,2,1152]{2,1,0:T(2,128)(2,1)S(1)} %get-tuple-element.31), channel_id=1, replica_groups=mesh['z'=16,'core'=2,'frame'=2,'part'=8] {'z'}, dimensions={0} | all-to-all | bytes 147456 | tf_op jit(solution)/shard_map/all_to_all | solution.py:289
  144.4 0.7 shard_map.86
  (5 shorter events, 0.1 us)
Async XLA Ops:
  2.7 6.1 %copy-start.2 = (bf16[1152,216]{0,1:T(8,128)(2,1)S(1)}, bf16[1152,216]{0,1:T(8,128)(2,1)}, u32[]{:S(2)}) copy-start(bf16[1152,216]{0,1:T(8,128)(2,1)} %param.8) | copy-start | bytes 1492996
  2.7 6.1 %copy-start.3 = (bf16[72,1152]{1,0:T(8,128)(2,1)S(1)}, bf16[72,1152]{1,0:T(8,128)(2,1)}, u32[]{:S(2)}) copy-start(bf16[72,1152]{1,0:T(8,128)(2,1)} %param.9) | copy-start | bytes 497668
  2.7 18.4 %all-to-all-start = ((bf16[8,2,32,1152]{3,2,1,0:T(8,128)(2,1)}), bf16[8,2,32,1152]{3,2,1,0:T(8,128)(2,1)S(1)}, u32[]{:S(2)}, u32[]{:S(2)}) async-start(bf16[8,2,32,1152]{3,2,1,0:T(8,128)(2,1)} %shard_map.77), calls=%async_computation | async-start | bytes 2359296 | tf_op jit(solution)/shard_map/all_to_all | solution.py:289
  8.9 17.3 %collective-permute-start = (bf16[4,72,1152]{2,1,0:T(8,128)(2,1)S(1)}, bf16[4,72,1152]{2,1,0:T(8,128)(2,1)S(1)}, u32[]{:S(2)}, u32[]{:S(2)}) collective-permute-start(bf16[4,72,1152]{2,1,0:T(8,128)(2,1)S(1)} %bitcast.13), channel_id=1, source_target_pairs={{0,12},{1,13},{2,14},{3,15},{4,8},{5,9},{6,10},{7,11},{8,4},{9,5},... | collective-permute-start | bytes 1990664 | tf_op jit(solution)/shard_map/ppermute | solution.py:316
  26.2 14.3 %copy-start.1 = (bf16[1,32,1152]{2,1,0:T(8,128)(2,1)S(1)}, bf16[1,32,1152]{2,1,0:T(8,128)(2,1)}, u32[]{:S(2)}) copy-start(bf16[1,32,1152]{2,1,0:T(8,128)(2,1)} %probe.3) | copy-start | bytes 221188
  51.0 12.5 %copy-start = (bf16[32,1152]{1,0:T(8,128)(2,1)S(1)}, bf16[32,1152]{1,0:T(8,128)(2,1)}, u32[]{:S(2)}) copy-start(bf16[32,1152]{1,0:T(8,128)(2,1)} %noisy.3) | copy-start | bytes 221188
  91.9 9.4 %collective-permute-start.1 = (bf16[16,2,1152]{2,1,0:T(2,128)(2,1)S(1)}, bf16[16,2,1152]{2,1,0:T(2,128)(2,1)S(1)}, u32[]{:S(2)}, u32[]{:S(2)}) collective-permute-start(bf16[16,2,1152]{2,1,0:T(2,128)(2,1)S(1)} %all_to_all.43.mine), channel_id=1, source_target_pairs={{0,16},{16,0},{1,17},{17,1},{2,18},{18,2},{3,19},{19,3},{4,20},{20... | collective-permute-start | bytes 221192 | tf_op jit(solution)/shard_map/ppermute | solution.py:384

commit v4 on v3

--- a/solution.py
+++ b/solution.py
@@ -85,14 +85,10 @@
     return [value[:, i * HEAD_DIM : (i + 1) * HEAD_DIM].astype(BF) for i in range(3)]
 
 
-def project_in(weights):
-    return weights[pl.ds(0, 3 * HEAD_DIM), :]
-
-
-def head_forward(tokens, flat_weights, weights, primal, probs):
+def head_forward(tokens, w_in, primal, probs):
     c = HEAD_DIM ** (-0.5)
     count = tokens.shape[0] // 2
-    projected = mm(tokens[...], project_in(flat_weights), NT)
+    projected = mm(tokens[...], w_in[...], NT)
     q, k, v = thirds(projected[:count])
     dq, dk, dv = thirds(projected[count:])
     scores = mm(q, k, NT) * c
@@ -105,10 +101,10 @@
     probs[...] = p
     for i, value in enumerate((q, k, v)):
         primal[i] = value
-    return mm(out.astype(BF), weights[3])
-
-
-def near_kernel(gath, flat_weights, weights, mods, tokens, term, primal, probs):
+    return out.astype(BF)
+
+
+def near_kernel(gath, w_in, w_out, mods, tokens, term, primal, probs):
     blocks, _, rows, _ = gath.shape
     scale = 1.0 + mods[1:2, :]
     shift = mods[0:1, :]
@@ -117,11 +113,15 @@
         tokens[pl.ds(i * rows, rows), :] = (normed * scale + shift).astype(BF)
         field = norm_tangent(gath[i, 1].astype(F32), normed, inverse)
         tokens[pl.ds((blocks + i) * rows, rows), :] = (field * scale).astype(BF)
-    term[...] = head_forward(tokens, flat_weights, weights, primal, probs)
-
-
-def far_kernel(tokens, flat_weights, weights, term, parts, primal, probs):
-    total = term[...] + head_forward(tokens, flat_weights, weights, primal, probs)
+    term[...] = mm(head_forward(tokens, w_in, primal, probs), w_out[...])
+
+
+def far_kernel(tokens, w_in, out, primal, probs):
+    out[...] = head_forward(tokens, w_in, primal, probs)
+
+
+def sum_kernel(term, out, w_out, parts):
+    total = term[...] + mm(out[...], w_out[...])
     parts[...] = total.astype(BF).reshape(parts.shape)
 
 
@@ -138,17 +138,17 @@
 
 
 def adjoint_kernel(
-    gated, near_flat, near, near_primal, near_probs, far_flat, far, far_primal, far_probs, parts
+    gated, near_in, near_out, near_primal, near_probs, far_in, far_out, far_primal, far_probs, parts
 ):
     c = HEAD_DIM ** (-0.5)
     blocks, rows, width = gated.shape
     whole = gated[...].reshape(blocks * rows, width)
     total = None
-    for flat_weights, weights, primal, probs in (
-        (near_flat, near, near_primal, near_probs),
-        (far_flat, far, far_primal, far_probs),
+    for w_in, w_out, primal, probs in (
+        (near_in, near_out, near_primal, near_probs),
+        (far_in, far_out, far_primal, far_probs),
     ):
-        co = mm(whole, weights[3], NT).astype(BF)
+        co = mm(whole, w_out[...], NT).astype(BF)
         q, k, v = primal[0], primal[1], primal[2]
         p = probs[...]
         p_float = p.astype(F32)
@@ -157,7 +157,7 @@
         scaled = (p_float * (d_probs - row_dot) * c).astype(BF)
         grads = (mm(scaled, k), mm(flip(scaled), q), mm(flip(p), co))
         grads = jnp.concatenate(grads, axis=1).astype(BF)
-        term = mm(grads, project_in(flat_weights))
+        term = mm(grads, w_in[...])
         total = term if total is None else total + term
     parts[...] = total.astype(BF).reshape(parts.shape)
 
@@ -310,11 +310,12 @@
         moved=2 * 10**6,
         limit=60,
     )
+    outgoing, w_in, w_out = lax.optimization_barrier((outgoing, w_qkv.T, w_out))
     gath = exchange(outgoing, "part")
-    near = jnp.concatenate([w_qkv.T, w_out], axis=0).reshape(4, HEAD_DIM, width)
     half = seq_count - seq_count // 4
-    far = lax.ppermute(near, SEQ, [(i, i ^ half) for i in range(seq_count)])
-    near_flat, far_flat = [w.reshape(4 * HEAD_DIM, width) for w in (near, far)]
+    partner = [(i, i ^ half) for i in range(seq_count)]
+    far_in = lax.ppermute(w_in, SEQ, partner)
+    far_out = lax.ppermute(w_out, SEQ, partner)
     mods = modulation(timestep, w_mod, width)
 
     part_sums = jax.ShapeDtypeStruct((parts, rows, width), BF)
@@ -330,24 +331,23 @@
         )
         + kept,
         gath,
-        near_flat,
-        near,
+        w_in,
+        w_out,
         mods,
         flops=10**9,
         moved=6 * 10**6,
         limit=24,
     )
-    sums, far_primal, far_probs = call(
+    out, far_primal, far_probs = call(
         far_kernel,
-        (part_sums,) + kept,
+        (jax.ShapeDtypeStruct((frame_rows, HEAD_DIM), BF),) + kept,
         tokens,
-        far_flat,
-        far,
-        term,
+        far_in,
         flops=10**9,
         moved=4 * 10**6,
         limit=24,
     )
+    sums = call(sum_kernel, part_sums, term, out, far_out, flops=10**8, moved=10**6)
     sums = exchange(sums, "part")
     gated, update = call(
         update_kernel,
@@ -362,12 +362,12 @@
         adjoint_kernel,
         part_sums,
         gated,
-        near_flat,
-        near,
+        w_in,
+        w_out,
         near_primal,
         near_probs,
-        far_flat,
-        far,
+        far_in,
+        far_out,
         far_primal,
         far_probs,
         flops=2 * 10**9,

time: 148 us -> 147 us (level)
  waiting for transfers between devices: 3.4 us -> 0.92 us
    ppermute x1 -> x2, waiting for transfers between devices: 2.48 us -> 0.01 us  [the longest x1 0.01 us: shards(): far_in = lax.ppermute(w_in, SEQ, partner)]
    ppermute x1 -> x2, starting transfers between devices: 4.63 us -> 6.54 us  [the longest x1 4.62 us: shards(): far_in = lax.ppermute(w_in, SEQ, partner)]
    pallas_call x10 -> x11, Pallas kernels: 12.6 us -> 12.4 us  [call(): pl.pallas_call(kernel, out_shape=out_shape, in_specs=where or [LOCAL] * l...]
  transfers between devices with their start and end apart: 3 -> 4, of which waited for: 2 -> 1; matrix products, arithmetic and copies ran while one was open for 5% -> 5% of each run, Pallas kernels for 2% -> 3%
where the time goes in v4:
time: 147 us; the launch traced here: 144 us
  blocking collectives  103 us (70%)
  starting transfers between devices  19.6 us (13%)
  Pallas kernels  12.4 us (8%)
  local copies, waits for them, and re-layouts  3.9 us (3%)
  matrix products  2.95 us (2%)
    all_to_all x7, blocking collectives, exchange(): return lax.all_to_all(blocks, axis, split_axis=0, concat_axis=0, tiled=True)  103 us
    pallas_call x11, Pallas kernels, call(): pl.pallas_call(kernel, out_shape=out_shape, in_specs=where or [LOCAL] * l...  12.4 us
    ppermute x1, starting transfers between devices, shards(): other = lax.ppermute(mine, 'core', [(i, i ^ 1) for i in range(cores)])  7.08 us
    all_to_all x1, starting transfers between devices, exchange(): return lax.all_to_all(blocks, axis, split_axis=0, concat_axis=0, tiled=True)  5.96 us
    ppermute x1, starting transfers between devices, shards(): far_in = lax.ppermute(w_in, SEQ, partner)  4.62 us
    unnamed x9, local copies, waits for them, and re-layouts  3.9 us
    dot_general x1, matrix products, modulation(): jnp.dot(jax.nn.silu(embedding)[None, :], w_mod.astype(jnp.float32), preci...  2.95 us
  transfers between devices with their start and end apart: 4, of which 1 were waited for; matrix products, arithmetic and copies ran while one was open for 5% of the time, Pallas kernels for 3%

profile of v4, /device:TPU:1, one launch (start us, length us, event | category | flops | bytes accessed | tf_op | source)
XLA Modules:
  0.0 144.3 jit_solution(12136920872795948428)
XLA Ops:
  0.6 0.0 copy-start.2
  0.6 0.0 copy-start.3
  0.6 2.1 %shard_map.77 = bf16[8,2,32,1152]{3,2,1,0:T(8,128)(2,1)} custom-call(bf16[32,1152]{1,0:T(8,128)(2,1)} %noisy.3, bf16[1,32,1152]{2,1,0:T(8,128)(2,1)} %probe.3), custom_call_target="tpu_custom_call" | custom-call | bytes 2000000 | tf_op jit(solution)/shard_map/pallas_call | solution.py:277
  2.8 6.0 %all-to-all-start = ((bf16[8,2,32,1152]{3,2,1,0:T(8,128)(2,1)}), bf16[8,2,32,1152]{3,2,1,0:T(8,128)(2,1)S(1)}, u32[]{:S(2)}, u32[]{:S(2)}) async-start(bf16[8,2,32,1152]{3,2,1,0:T(8,128)(2,1)} %shard_map.77), calls=%async_computation | async-start | bytes 2359296 | tf_op jit(solution)/shard_map/all_to_all | solution.py:289
  8.7 0.0 copy-done.2
  8.7 4.6 %collective-permute-start = (bf16[216,1152]{1,0:T(8,128)(2,1)S(1)}, bf16[216,1152]{1,0:T(8,128)(2,1)S(1)}, u32[]{:S(2)}, u32[]{:S(2)}) collective-permute-start(bf16[216,1152]{1,0:T(8,128)(2,1)S(1)} %bitcast.14), channel_id=1, source_target_pairs={{0,12},{1,13},{2,14},{3,15},{4,8},{5,9},{6,10},{7,11},{8,4},{9,5},... | collective-permute-start | bytes 1493000 | tf_op jit(solution)/shard_map/ppermute | solution.py:317
  13.4 0.0 copy-done.3
  13.4 1.9 %collective-permute-start.1 = (bf16[72,1152]{1,0:T(8,128)(2,1)S(1)}, bf16[72,1152]{1,0:T(8,128)(2,1)S(1)}, u32[]{:S(2)}, u32[]{:S(2)}) collective-permute-start(bf16[72,1152]{1,0:T(8,128)(2,1)S(1)} %copy-done.3), channel_id=1, source_target_pairs={{0,12},{1,13},{2,14},{3,15},{4,8},{5,9},{6,10},{7,11},{8,4},{9,5},... | collective-permute-start | bytes 497672 | tf_op jit(solution)/shard_map/ppermute | solution.py:318
  16.0 3.9 %copy.8 = bf16[256,3456]{0,1:T(8,128)(2,1)} copy(bf16[256,3456]{1,0:T(8,128)(2,1)} %param.10) | data formatting | bytes 3538944 | tf_op args[4]
  19.9 3.0 %fusion.2 = f32[1,3,1152]{2,0,1:T(1,128)S(1)} fusion(f32[256,1,1]{0,1,2:T(1,128)S(1)} %bitcast.18, bf16[3,1152,256]{2,1,0:T(8,128)(2,1)} %bitcast.17), kind=kOutput, calls=%fused_computation.6 | convolution fusion | flops 10616832 | bytes 1784320 | tf_op jit(solution)/shard_map/dot_general | solution.py:51
  22.9 0.0 all-to-all-done.gath
  22.9 2.6 %shard_map.78 = (bf16[512,1152]{1,0:T(8,128)(2,1)S(1)}, f32[256,1152]{1,0:T(8,128)S(1)}, bf16[3,256,72]{2,1,0:T(8,128)(2,1)S(1)}, bf16[256,256]{1,0:T(8,128)(2,1)S(1)}) custom-call(bf16[8,2,32,1152]{3,2,1,0:T(8,128)(2,1)S(1)} %all-to-all-done.gath, bf16[216,1152]{1,0:T(8,128)(2,1)S(1)} %bitcast.15, bf16[72,1152]{1,0:T(8,128)(2,1)S(1)} %copy-done.3, ...), custom_call_target="tpu_custom_call" | custom-call | flops 1000000000 | bytes 6000000 | tf_op jit(solution)/shard_map/pallas_call | solution.py:277
  25.5 0.0 collective-permute-done.w_in.far_in
  25.5 1.4 shard_map.79
  26.9 0.0 copy-start.1
  26.9 0.0 collective-permute-done.1.w_out.far_out
  26.9 0.3 shard_map.80
  27.2 12.9 %all_to_all.40.parts = bf16[8,32,1152]{2,1,0:T(8,128)(2,1)S(1)} all-to-all(bf16[8,32,1152]{2,1,0:T(8,128)(2,1)S(1)} %shard_map.80), channel_id=1, replica_groups=mesh['z'=16,'core'=2,'frame'=2,'part'=8] {'part'}, dimensions={0} | all-to-all | bytes 1179648 | tf_op jit(solution)/shard_map/all_to_all | solution.py:289
  40.1 0.1 shard_map.81
  40.2 10.4 %all_to_all.41.gated = bf16[8,32,1152]{2,1,0:T(8,128)(2,1)S(1)} all-to-all(bf16[8,32,1152]{2,1,0:T(8,128)(2,1)S(1)} %get-tuple-element.27), channel_id=1, replica_groups=mesh['z'=16,'core'=2,'frame'=2,'part'=8] {'part'}, dimensions={0} | all-to-all | bytes 1179648 | tf_op jit(solution)/shard_map/all_to_all | solution.py:289
  50.6 2.1 %shard_map.82 = bf16[8,32,1152]{2,1,0:T(8,128)(2,1)S(1)} custom-call(bf16[8,32,1152]{2,1,0:T(8,128)(2,1)S(1)} %all_to_all.41.gated, bf16[216,1152]{1,0:T(8,128)(2,1)S(1)} %bitcast.16, bf16[72,1152]{1,0:T(8,128)(2,1)S(1)} %copy-done.3, bf16[3,256,72]{2,1,0:T(8,128)(2,1)S(1)} %get-tuple-element.28.near_primal, ...), custom_call_target="tpu_custom_call" | custom-call | flops 2000000000 | bytes 5000000 | tf_op jit(solution)/shard_map/pallas_call | solution.py:277
  52.7 10.4 %all_to_all.42.parts = bf16[8,32,1152]{2,1,0:T(8,128)(2,1)S(1)} all-to-all(bf16[8,32,1152]{2,1,0:T(8,128)(2,1)S(1)} %shard_map.82), channel_id=1, replica_groups=mesh['z'=16,'core'=2,'frame'=2,'part'=8] {'part'}, dimensions={0} | all-to-all | bytes 1179648 | tf_op jit(solution)/shard_map/all_to_all | solution.py:289
  63.1 0.3 shard_map.83
  63.5 30.9 %all_to_all.43.mine = bf16[16,2,1152]{2,1,0:T(2,128)(2,1)S(1)} all-to-all(bf16[16,2,1152]{2,1,0:T(2,128)(2,1)S(1)} %get-tuple-element.33), channel_id=1, replica_groups=mesh['z'=16,'core'=2,'frame'=2,'part'=8] {'z'}, dimensions={0} | all-to-all | bytes 147456 | tf_op jit(solution)/shard_map/all_to_all | solution.py:289
  94.4 7.1 %collective-permute-start.2 = (bf16[16,2,1152]{2,1,0:T(2,128)(2,1)S(1)}, bf16[16,2,1152]{2,1,0:T(2,128)(2,1)S(1)}, u32[]{:S(2)}, u32[]{:S(2)}) collective-permute-start(bf16[16,2,1152]{2,1,0:T(2,128)(2,1)S(1)} %all_to_all.43.mine), channel_id=1, source_target_pairs={{0,16},{16,0},{1,17},{17,1},{2,18},{18,2},{3,19},{19,3},{4,20},{20... | collective-permute-start | bytes 221192 | tf_op jit(solution)/shard_map/ppermute | solution.py:384
  101.5 0.9 collective-permute-done.2.other
  102.4 0.5 shard_map.84
  102.9 9.7 %all_to_all.44.arrived = f32[16,8,128]{2,1,0:T(8,128)S(1)} all-to-all(f32[16,8,128]{2,1,0:T(8,128)S(1)} %get-tuple-element.34), channel_id=1, replica_groups=mesh['z'=16,'core'=2,'frame'=2,'part'=8] {'frame','part'}, dimensions={0} | all-to-all | bytes 131072 | tf_op jit(solution)/shard_map/all_to_all | solution.py:289
  112.7 14.2 %all_to_all.45.arrived = f32[16,8,128]{2,1,0:T(8,128)S(1)} all-to-all(f32[16,8,128]{2,1,0:T(8,128)S(1)} %shard_map.85), channel_id=1, replica_groups=mesh['z'=16,'core'=2,'frame'=2,'part'=8] {'z'}, dimensions={0} | all-to-all | bytes 131072 | tf_op jit(solution)/shard_map/all_to_all | solution.py:289
  126.9 2.2 %shard_map.86 = (f32[32,32]{1,0:T(8,128)}, bf16[16,2,1152]{2,1,0:T(2,128)(2,1)S(1)}, f32[32,1152]{1,0:T(8,128)S(1)}) custom-call(f32[16,8,128]{2,1,0:T(8,128)S(1)} %all_to_all.45.arrived, bf16[32,2,1152]{2,1,0:T(2,128)(2,1)S(1)} %get-tuple-element.35.rows, f32[32,1152]{1,0:T(8,128)S(1)} %get-tuple-element.36.lost), custom_call_target="tpu_custom_call" | custom-call | bytes 300000 | tf_op jit(solution)/shard_map/pallas_call | solution.py:277
  129.1 14.4 %all_to_all.46.pairs = bf16[16,2,1152]{2,1,0:T(2,128)(2,1)S(1)} all-to-all(bf16[16,2,1152]{2,1,0:T(2,128)(2,1)S(1)} %get-tuple-element.37), channel_id=1, replica_groups=mesh['z'=16,'core'=2,'frame'=2,'part'=8] {'z'}, dimensions={0} | all-to-all | bytes 147456 | tf_op jit(solution)/shard_map/all_to_all | solution.py:289
  143.5 0.7 shard_map.87
  (7 shorter events, 0.1 us)
Async XLA Ops:
  0.6 8.1 %copy-start.2 = (bf16[1152,216]{0,1:T(8,128)(2,1)S(1)}, bf16[1152,216]{0,1:T(8,128)(2,1)}, u32[]{:S(2)}) copy-start(bf16[1152,216]{0,1:T(8,128)(2,1)} %param.8) | copy-start | bytes 1492996
  0.6 12.7 %copy-start.3 = (bf16[72,1152]{1,0:T(8,128)(2,1)S(1)}, bf16[72,1152]{1,0:T(8,128)(2,1)}, u32[]{:S(2)}) copy-start(bf16[72,1152]{1,0:T(8,128)(2,1)} %near_out) | copy-start | bytes 497668
  2.8 20.1 %all-to-all-start = ((bf16[8,2,32,1152]{3,2,1,0:T(8,128)(2,1)}), bf16[8,2,32,1152]{3,2,1,0:T(8,128)(2,1)S(1)}, u32[]{:S(2)}, u32[]{:S(2)}) async-start(bf16[8,2,32,1152]{3,2,1,0:T(8,128)(2,1)} %shard_map.77), calls=%async_computation | async-start | bytes 2359296 | tf_op jit(solution)/shard_map/all_to_all | solution.py:289
  8.7 16.7 %collective-permute-start = (bf16[216,1152]{1,0:T(8,128)(2,1)S(1)}, bf16[216,1152]{1,0:T(8,128)(2,1)S(1)}, u32[]{:S(2)}, u32[]{:S(2)}) collective-permute-start(bf16[216,1152]{1,0:T(8,128)(2,1)S(1)} %bitcast.14), channel_id=1, source_target_pairs={{0,12},{1,13},{2,14},{3,15},{4,8},{5,9},{6,10},{7,11},{8,4},{9,5},... | collective-permute-start | bytes 1493000 | tf_op jit(solution)/shard_map/ppermute | solution.py:317
  13.4 13.5 %collective-permute-start.1 = (bf16[72,1152]{1,0:T(8,128)(2,1)S(1)}, bf16[72,1152]{1,0:T(8,128)(2,1)S(1)}, u32[]{:S(2)}, u32[]{:S(2)}) collective-permute-start(bf16[72,1152]{1,0:T(8,128)(2,1)S(1)} %copy-done.3), channel_id=1, source_target_pairs={{0,12},{1,13},{2,14},{3,15},{4,8},{5,9},{6,10},{7,11},{8,4},{9,5},... | collective-permute-start | bytes 497672 | tf_op jit(solution)/shard_map/ppermute | solution.py:318
  26.9 13.2 %copy-start.1 = (bf16[1,32,1152]{2,1,0:T(8,128)(2,1)S(1)}, bf16[1,32,1152]{2,1,0:T(8,128)(2,1)}, u32[]{:S(2)}) copy-start(bf16[1,32,1152]{2,1,0:T(8,128)(2,1)} %probe.3) | copy-start | bytes 221188
  50.6 12.5 %copy-start = (bf16[32,1152]{1,0:T(8,128)(2,1)S(1)}, bf16[32,1152]{1,0:T(8,128)(2,1)}, u32[]{:S(2)}) copy-start(bf16[32,1152]{1,0:T(8,128)(2,1)} %noisy.3) | copy-start | bytes 221188
  94.4 8.0 %collective-permute-start.2 = (bf16[16,2,1152]{2,1,0:T(2,128)(2,1)S(1)}, bf16[16,2,1152]{2,1,0:T(2,128)(2,1)S(1)}, u32[]{:S(2)}, u32[]{:S(2)}) collective-permute-start(bf16[16,2,1152]{2,1,0:T(2,128)(2,1)S(1)} %all_to_all.43.mine), channel_id=1, source_target_pairs={{0,16},{16,0},{1,17},{17,1},{2,18},{18,2},{3,19},{19,3},{4,20},{20... | collective-permute-start | bytes 221192 | tf_op jit(solution)/shard_map/ppermute | solution.py:384

commit v5 on v4

--- a/solution.py
+++ b/solution.py
@@ -47,11 +47,13 @@
     freq_index = jnp.arange(half_dim, dtype=jnp.float32)
     frequency = jnp.exp(-math.log(10000.0) * freq_index / half_dim)
     angles = timestep[0].astype(jnp.float32) * frequency
-    embedding = jnp.concatenate([jnp.cos(angles), jnp.sin(angles)])
-    modulated = jnp.dot(
-        jax.nn.silu(embedding)[None, :], w_mod.astype(jnp.float32), precision=lax.Precision.HIGHEST
-    )
-    return modulated.reshape(3, feat_width)
+    rest = jax.nn.silu(jnp.concatenate([jnp.cos(angles), jnp.sin(angles)]))
+    pieces = []
+    for _ in range(3):
+        pieces.append(lax.reduce_precision(rest, 8, 7))
+        rest = rest - pieces[-1]
+    rows = jnp.pad(jnp.stack(pieces), ((0, 13), (0, 0))).astype(BF)
+    return jnp.sum(mm(rows, w_mod), axis=0).reshape(3, feat_width)
 
 
 def normalize(values_f):
@@ -260,7 +262,8 @@
         solved[:, t, :] = (high + (middle + low)).astype(BF)
 
 
-def basis_kernel(pairs, rest, basis):
+def basis_kernel(pairs, rest, triangle, basis, factor):
+    factor[...] = triangle[...]
     count, each, _ = pairs.shape
     for i in range(count):
         at = slice(i * each, (i + 1) * each)
@@ -399,19 +402,21 @@
     )
     grams = exchange(grams, SEQ)
     grams = call(total_kernel, blocks_of(chips), grams, moved=10**5)
-    factor, solved, rest = call(
+    square = jax.ShapeDtypeStruct((probe_count, probe_count), F32)
+    triangle, solved, rest = call(
         solve_kernel,
-        (jax.ShapeDtypeStruct((probe_count, probe_count), F32), pairs, own_rows),
+        (square, pairs, own_rows),
         exchange(grams, "z"),
         every,
         lost,
         moved=3 * 10**5,
     )
-    basis = call(
+    basis, factor = call(
         basis_kernel,
-        jax.ShapeDtypeStruct((1, rows, width), F32),
+        (jax.ShapeDtypeStruct((1, rows, width), F32), square),
         exchange(solved, "z"),
         rest,
+        triangle,
         moved=3 * 10**5,
     )
     return basis, factor

time: 147 us -> 151 us (1.027)
  blocking collectives: 103 us -> 107 us
  local copies, waits for them, and re-layouts: 3.9 us -> 0.04 us
  waiting for transfers between devices: 0.92 us -> 4.63 us
  Pallas kernels: 12.4 us -> 15.3 us
  matrix products: 2.95 us -> 0.36 us
    unnamed x9 -> x8, local copies, waits for them, and re-layouts: 3.9 us -> 0.02 us
    all_to_all x7, blocking collectives: 103 us -> 107 us  [exchange(): return lax.all_to_all(blocks, axis, split_axis=0, concat_axis=0, tiled=True)]
    all_to_all x1, waiting for transfers between devices: 0.03 us -> 3.15 us  [exchange(): return lax.all_to_all(blocks, axis, split_axis=0, concat_axis=0, tiled=True)]
    pallas_call x11, Pallas kernels: 12.4 us -> 15.3 us  [call(): pl.pallas_call(kernel, out_shape=out_shape, in_specs=where or [LOCAL] * l...]
    dot_general x1, matrix products: 2.95 us -> 0.36 us  [mm(): return lax.dot_general(a, b, dims, preferred_element_type=F32)]
  transfers between devices with their start and end apart: 4 -> 4, of which waited for: 1 -> 3; matrix products, arithmetic and copies ran while one was open for 5% -> 0% of each run, Pallas kernels for 3% -> 4%
where the time goes in v5:
time: 151 us; the launch traced here: 148 us
  blocking collectives  107 us (71%)
  starting transfers between devices  19.6 us (13%)
  Pallas kernels  15.3 us (10%)
  waiting for transfers between devices  4.63 us (3%)
    all_to_all x7, blocking collectives, exchange(): return lax.all_to_all(blocks, axis, split_axis=0, concat_axis=0, tiled=True)  107 us
    pallas_call x11, Pallas kernels, call(): pl.pallas_call(kernel, out_shape=out_shape, in_specs=where or [LOCAL] * l...  15.3 us
    ppermute x1, starting transfers between devices, shards(): other = lax.ppermute(mine, 'core', [(i, i ^ 1) for i in range(cores)])  7.08 us
    all_to_all x1, starting transfers between devices, exchange(): return lax.all_to_all(blocks, axis, split_axis=0, concat_axis=0, tiled=True)  5.96 us
    ppermute x1, starting transfers between devices, shards(): far_in = lax.ppermute(w_in, SEQ, partner)  4.63 us
    all_to_all x1, waiting for transfers between devices, exchange(): return lax.all_to_all(blocks, axis, split_axis=0, concat_axis=0, tiled=True)  3.15 us
  transfers between devices with their start and end apart: 4, of which 3 were waited for; matrix products, arithmetic and copies ran while one was open for 0% of the time, Pallas kernels for 4%

profile of v5, /device:TPU:1, one launch (start us, length us, event | category | flops | bytes accessed | tf_op | source)
XLA Modules:
  0.0 148.3 jit_solution(1093410598245936462)
XLA Ops:
  0.6 0.0 copy-start
  0.6 0.0 copy-start.3
  0.7 2.2 %shard_map.77 = bf16[8,2,32,1152]{3,2,1,0:T(8,128)(2,1)} custom-call(bf16[32,1152]{1,0:T(8,128)(2,1)} %noisy.3, bf16[1,32,1152]{2,1,0:T(8,128)(2,1)} %probe.3), custom_call_target="tpu_custom_call" | custom-call | bytes 2000000 | tf_op jit(solution)/shard_map/pallas_call | solution.py:280
  2.9 6.0 %all-to-all-start = ((bf16[8,2,32,1152]{3,2,1,0:T(8,128)(2,1)}), bf16[8,2,32,1152]{3,2,1,0:T(8,128)(2,1)S(1)}, u32[]{:S(2)}, u32[]{:S(2)}) async-start(bf16[8,2,32,1152]{3,2,1,0:T(8,128)(2,1)} %shard_map.77), calls=%async_computation | async-start | bytes 2359296 | tf_op jit(solution)/shard_map/all_to_all | solution.py:292
  8.8 4.6 %collective-permute-start = (bf16[216,1152]{1,0:T(8,128)(2,1)}, bf16[216,1152]{1,0:T(8,128)(2,1)}, u32[]{:S(2)}, u32[]{:S(2)}) collective-permute-start(bf16[216,1152]{1,0:T(8,128)(2,1)} %bitcast.w_in.near_in), channel_id=1, source_target_pairs={{0,12},{1,13},{2,14},{3,15},{4,8},{5,9},{6,10},{7,11},{8,4},{9,5},... | collective-permute-start | bytes 1493000 | tf_op jit(solution)/shard_map/ppermute | solution.py:320
  13.5 0.0 copy-done.3
  13.5 1.9 %collective-permute-start.1 = (bf16[72,1152]{1,0:T(8,128)(2,1)S(1)}, bf16[72,1152]{1,0:T(8,128)(2,1)S(1)}, u32[]{:S(2)}, u32[]{:S(2)}) collective-permute-start(bf16[72,1152]{1,0:T(8,128)(2,1)S(1)} %copy-done.3), channel_id=1, source_target_pairs={{0,12},{1,13},{2,14},{3,15},{4,8},{5,9},{6,10},{7,11},{8,4},{9,5},... | collective-permute-start | bytes 497672 | tf_op jit(solution)/shard_map/ppermute | solution.py:321
  16.1 0.0 copy-done
  16.1 0.4 convolution_reduce_fusion
  16.5 3.1 %all-to-all-done.gath = bf16[8,2,32,1152]{3,2,1,0:T(8,128)(2,1)S(1)} async-done(((bf16[8,2,32,1152]{3,2,1,0:T(8,128)(2,1)}), bf16[8,2,32,1152]{3,2,1,0:T(8,128)(2,1)S(1)}, u32[]{:S(2)}, u32[]{:S(2)}) %all-to-all-start) | async-done | bytes 1179680 | tf_op jit(solution)/shard_map/all_to_all | solution.py:292
  19.7 3.6 %shard_map.78 = (bf16[512,1152]{1,0:T(8,128)(2,1)S(1)}, f32[256,1152]{1,0:T(8,128)S(1)}, bf16[3,256,72]{2,1,0:T(8,128)(2,1)S(1)}, bf16[256,256]{1,0:T(8,128)(2,1)S(1)}) custom-call(bf16[8,2,32,1152]{3,2,1,0:T(8,128)(2,1)S(1)} %all-to-all-done.gath, bf16[216,1152]{1,0:T(8,128)(2,1)} %bitcast.w_in.near_in, bf16[72,1152]{1,0:T(8,128)(2,1)S(1)} %copy-done.3, ...), custom_call_target="tpu_custom_call" | custom-call | flops 1000000000 | bytes 6000000 | tf_op jit(solution)/shard_map/pallas_call | solution.py:280
  23.3 0.0 collective-permute-done.w_in.far_in
  23.3 2.4 %shard_map.79 = (bf16[256,72]{1,0:T(8,128)(2,1)S(1)}, bf16[3,256,72]{2,1,0:T(8,128)(2,1)S(1)}, bf16[256,256]{1,0:T(8,128)(2,1)S(1)}) custom-call(bf16[512,1152]{1,0:T(8,128)(2,1)S(1)} %get-tuple-element.25.tokens, bf16[216,1152]{1,0:T(8,128)(2,1)} %collective-permute-done.w_in.far_in), custom_call_target="tpu_custom_call" | custom-call | flops 1000000000 | bytes 4000000 | tf_op jit(solution)/shard_map/pallas_call | solution.py:280
  25.7 0.0 copy-start.2
  25.7 0.6 collective-permute-done.1.w_out.far_out
  26.3 0.3 shard_map.80
  26.6 16.8 %all_to_all.40.parts = bf16[8,32,1152]{2,1,0:T(8,128)(2,1)S(1)} all-to-all(bf16[8,32,1152]{2,1,0:T(8,128)(2,1)S(1)} %shard_map.80), channel_id=1, replica_groups=mesh['z'=16,'core'=2,'frame'=2,'part'=8] {'part'}, dimensions={0} | all-to-all | bytes 1179648 | tf_op jit(solution)/shard_map/all_to_all | solution.py:292
  43.4 0.1 shard_map.81
  43.5 10.9 %all_to_all.41.gated = bf16[8,32,1152]{2,1,0:T(8,128)(2,1)S(1)} all-to-all(bf16[8,32,1152]{2,1,0:T(8,128)(2,1)S(1)} %get-tuple-element.27), channel_id=1, replica_groups=mesh['z'=16,'core'=2,'frame'=2,'part'=8] {'part'}, dimensions={0} | all-to-all | bytes 1179648 | tf_op jit(solution)/shard_map/all_to_all | solution.py:292
  54.4 3.4 %shard_map.82 = bf16[8,32,1152]{2,1,0:T(8,128)(2,1)S(1)} custom-call(bf16[8,32,1152]{2,1,0:T(8,128)(2,1)S(1)} %all_to_all.41.gated, bf16[216,1152]{1,0:T(8,128)(2,1)} %bitcast.w_in.near_in, bf16[72,1152]{1,0:T(8,128)(2,1)S(1)} %copy-done.3, bf16[3,256,72]{2,1,0:T(8,128)(2,1)S(1)} %get-tuple-element.28.near_primal, ...), custom_call_target="tpu_custom_call" | custom-call | flops 2000000000 | bytes 5000000 | tf_op jit(solution)/shard_map/pallas_call | solution.py:280
  57.8 11.2 %all_to_all.42.parts = bf16[8,32,1152]{2,1,0:T(8,128)(2,1)S(1)} all-to-all(bf16[8,32,1152]{2,1,0:T(8,128)(2,1)S(1)} %shard_map.82), channel_id=1, replica_groups=mesh['z'=16,'core'=2,'frame'=2,'part'=8] {'part'}, dimensions={0} | all-to-all | bytes 1179648 | tf_op jit(solution)/shard_map/all_to_all | solution.py:292
  69.0 0.0 copy-done.1
  69.0 0.3 shard_map.83
  69.3 28.6 %all_to_all.43.mine = bf16[16,2,1152]{2,1,0:T(2,128)(2,1)S(1)} all-to-all(bf16[16,2,1152]{2,1,0:T(2,128)(2,1)S(1)} %get-tuple-element.33), channel_id=1, replica_groups=mesh['z'=16,'core'=2,'frame'=2,'part'=8] {'z'}, dimensions={0} | all-to-all | bytes 147456 | tf_op jit(solution)/shard_map/all_to_all | solution.py:292
  97.9 7.1 %collective-permute-start.2 = (bf16[16,2,1152]{2,1,0:T(2,128)(2,1)S(1)}, bf16[16,2,1152]{2,1,0:T(2,128)(2,1)S(1)}, u32[]{:S(2)}, u32[]{:S(2)}) collective-permute-start(bf16[16,2,1152]{2,1,0:T(2,128)(2,1)S(1)} %all_to_all.43.mine), channel_id=1, source_target_pairs={{0,16},{16,0},{1,17},{17,1},{2,18},{18,2},{3,19},{19,3},{4,20},{20... | collective-permute-start | bytes 221192 | tf_op jit(solution)/shard_map/ppermute | solution.py:387
  105.0 0.9 collective-permute-done.2.other
  105.9 0.5 shard_map.84
  106.4 10.7 %all_to_all.44.arrived = f32[16,8,128]{2,1,0:T(8,128)S(1)} all-to-all(f32[16,8,128]{2,1,0:T(8,128)S(1)} %get-tuple-element.34), channel_id=1, replica_groups=mesh['z'=16,'core'=2,'frame'=2,'part'=8] {'frame','part'}, dimensions={0} | all-to-all | bytes 131072 | tf_op jit(solution)/shard_map/all_to_all | solution.py:292
  117.1 14.2 %all_to_all.45.arrived = f32[16,8,128]{2,1,0:T(8,128)S(1)} all-to-all(f32[16,8,128]{2,1,0:T(8,128)S(1)} %shard_map.85), channel_id=1, replica_groups=mesh['z'=16,'core'=2,'frame'=2,'part'=8] {'z'}, dimensions={0} | all-to-all | bytes 131072 | tf_op jit(solution)/shard_map/all_to_all | solution.py:292
  131.4 1.7 %shard_map.86 = (f32[32,32]{1,0:T(8,128)S(1)}, bf16[16,2,1152]{2,1,0:T(2,128)(2,1)S(1)}, f32[32,1152]{1,0:T(8,128)S(1)}) custom-call(f32[16,8,128]{2,1,0:T(8,128)S(1)} %all_to_all.45.arrived, bf16[32,2,1152]{2,1,0:T(2,128)(2,1)S(1)} %get-tuple-element.35.rows, f32[32,1152]{1,0:T(8,128)S(1)} %get-tuple-element.36.lost), custom_call_target="tpu_custom_call" | custom-call | bytes 300000 | tf_op jit(solution)/shard_map/pallas_call | solution.py:280
  133.1 14.4 %all_to_all.46.pairs = bf16[16,2,1152]{2,1,0:T(2,128)(2,1)S(1)} all-to-all(bf16[16,2,1152]{2,1,0:T(2,128)(2,1)S(1)} %get-tuple-element.37), channel_id=1, replica_groups=mesh['z'=16,'core'=2,'frame'=2,'part'=8] {'z'}, dimensions={0} | all-to-all | bytes 147456 | tf_op jit(solution)/shard_map/all_to_all | solution.py:292
  147.5 0.7 shard_map.87
  (7 shorter events, 0.1 us)
Async XLA Ops:
  0.6 15.5 %copy-start = (bf16[256,3456]{1,0:T(8,128)(2,1)S(1)}, bf16[256,3456]{1,0:T(8,128)(2,1)}, u32[]{:S(2)}) copy-start(bf16[256,3456]{1,0:T(8,128)(2,1)} %param.10) | copy-start | bytes 5308420
  0.6 12.8 %copy-start.3 = (bf16[72,1152]{1,0:T(8,128)(2,1)S(1)}, bf16[72,1152]{1,0:T(8,128)(2,1)}, u32[]{:S(2)}) copy-start(bf16[72,1152]{1,0:T(8,128)(2,1)} %near_out) | copy-start | bytes 497668
  2.9 16.8 %all-to-all-start = ((bf16[8,2,32,1152]{3,2,1,0:T(8,128)(2,1)}), bf16[8,2,32,1152]{3,2,1,0:T(8,128)(2,1)S(1)}, u32[]{:S(2)}, u32[]{:S(2)}) async-start(bf16[8,2,32,1152]{3,2,1,0:T(8,128)(2,1)} %shard_map.77), calls=%async_computation | async-start | bytes 2359296 | tf_op jit(solution)/shard_map/all_to_all | solution.py:292
  8.8 14.5 %collective-permute-start = (bf16[216,1152]{1,0:T(8,128)(2,1)}, bf16[216,1152]{1,0:T(8,128)(2,1)}, u32[]{:S(2)}, u32[]{:S(2)}) collective-permute-start(bf16[216,1152]{1,0:T(8,128)(2,1)} %bitcast.w_in.near_in), channel_id=1, source_target_pairs={{0,12},{1,13},{2,14},{3,15},{4,8},{5,9},{6,10},{7,11},{8,4},{9,5},... | collective-permute-start | bytes 1493000 | tf_op jit(solution)/shard_map/ppermute | solution.py:320
  13.5 12.9 %collective-permute-start.1 = (bf16[72,1152]{1,0:T(8,128)(2,1)S(1)}, bf16[72,1152]{1,0:T(8,128)(2,1)S(1)}, u32[]{:S(2)}, u32[]{:S(2)}) collective-permute-start(bf16[72,1152]{1,0:T(8,128)(2,1)S(1)} %copy-done.3), channel_id=1, source_target_pairs={{0,12},{1,13},{2,14},{3,15},{4,8},{5,9},{6,10},{7,11},{8,4},{9,5},... | collective-permute-start | bytes 497672 | tf_op jit(solution)/shard_map/ppermute | solution.py:321
  25.7 17.7 %copy-start.2 = (bf16[1,32,1152]{2,1,0:T(8,128)(2,1)S(1)}, bf16[1,32,1152]{2,1,0:T(8,128)(2,1)}, u32[]{:S(2)}) copy-start(bf16[1,32,1152]{2,1,0:T(8,128)(2,1)} %probe.3) | copy-start | bytes 221188
  54.4 14.6 %copy-start.1 = (bf16[32,1152]{1,0:T(8,128)(2,1)S(1)}, bf16[32,1152]{1,0:T(8,128)(2,1)}, u32[]{:S(2)}) copy-start(bf16[32,1152]{1,0:T(8,128)(2,1)} %noisy.3) | copy-start | bytes 221188
  97.9 8.0 %collective-permute-start.2 = (bf16[16,2,1152]{2,1,0:T(2,128)(2,1)S(1)}, bf16[16,2,1152]{2,1,0:T(2,128)(2,1)S(1)}, u32[]{:S(2)}, u32[]{:S(2)}) collective-permute-start(bf16[16,2,1152]{2,1,0:T(2,128)(2,1)S(1)} %all_to_all.43.mine), channel_id=1, source_target_pairs={{0,16},{16,0},{1,17},{17,1},{2,18},{18,2},{3,19},{19,3},{4,20},{20... | collective-permute-start | bytes 221192 | tf_op jit(solution)/shard_map/ppermute | solution.py:387

commit v6 on v5

--- a/solution.py
+++ b/solution.py
@@ -42,8 +42,8 @@
     return mm(eye(a.shape[1]).astype(BF), a, NT).astype(BF)
 
 
-def modulation(timestep, w_mod, feat_width):
-    half_dim = w_mod.shape[0] // 2
+def embedding_rows(timestep, freq_dim):
+    half_dim = freq_dim // 2
     freq_index = jnp.arange(half_dim, dtype=jnp.float32)
     frequency = jnp.exp(-math.log(10000.0) * freq_index / half_dim)
     angles = timestep[0].astype(jnp.float32) * frequency
@@ -52,8 +52,16 @@
     for _ in range(3):
         pieces.append(lax.reduce_precision(rest, 8, 7))
         rest = rest - pieces[-1]
-    rows = jnp.pad(jnp.stack(pieces), ((0, 13), (0, 0))).astype(BF)
-    return jnp.sum(mm(rows, w_mod), axis=0).reshape(3, feat_width)
+    return jnp.pad(jnp.stack(pieces), ((0, 13), (0, 0))).astype(BF)
+
+
+def modulation_kernel(embedding, w_mod, mods, staged, sems):
+    width = mods.shape[1]
+    spans = [pl.ds(i * width, width) for i in range(3)]
+    copies = fetch([(w_mod.at[:, at], staged.at[:, at]) for at in spans], sems)
+    for i, at in enumerate(spans):
+        copies[i].wait()
+        mods[i : i + 1, :] = jnp.sum(mm(embedding[...], staged[:, at]), axis=0, keepdims=True)
 
 
 def normalize(values_f):
@@ -319,7 +327,16 @@
     partner = [(i, i ^ half) for i in range(seq_count)]
     far_in = lax.ppermute(w_in, SEQ, partner)
     far_out = lax.ppermute(w_out, SEQ, partner)
-    mods = modulation(timestep, w_mod, width)
+    mods = call(
+        modulation_kernel,
+        jax.ShapeDtypeStruct((3, width), F32),
+        embedding_rows(timestep, w_mod.shape[0]),
+        w_mod,
+        where=[LOCAL, HBM],
+        scratch=(pltpu.VMEM(w_mod.shape, BF), pltpu.SemaphoreType.DMA((3,))),
+        moved=2 * 10**6,
+        limit=59,
+    )
 
     part_sums = jax.ShapeDtypeStruct((parts, rows, width), BF)
     kept = (

time: 151 us -> 148 us (0.980)
  waiting for transfers between devices: 4.63 us -> 2.49 us
  blocking collectives: 107 us -> 105 us
    all_to_all x1, waiting for transfers between devices: 3.15 us -> 0.01 us  [exchange(): return lax.all_to_all(blocks, axis, split_axis=0, concat_axis=0, tiled=True)]
    all_to_all x7, blocking collectives: 107 us -> 105 us  [exchange(): return lax.all_to_all(blocks, axis, split_axis=0, concat_axis=0, tiled=True)]
    pallas_call x11 -> x12, Pallas kernels: 15.3 us -> 15 us  [call(): pl.pallas_call(kernel, out_shape=out_shape, in_specs=where or [LOCAL] * l...]
  transfers between devices with their start and end apart: 4 -> 4, of which waited for: 3 -> 2; matrix products, arithmetic and copies ran while one was open for 0% -> 0% of each run, Pallas kernels for 4% -> 5%
where the time goes in v6:
time: 148 us; the launch traced here: 145 us
  blocking collectives  105 us (71%)
  starting transfers between devices  19.7 us (13%)
  Pallas kernels  15 us (10%)
  waiting for transfers between devices  2.49 us (2%)
    all_to_all x7, blocking collectives, exchange(): return lax.all_to_all(blocks, axis, split_axis=0, concat_axis=0, tiled=True)  105 us
    pallas_call x12, Pallas kernels, call(): pl.pallas_call(kernel, out_shape=out_shape, in_specs=where or [LOCAL] * l...  15 us
    ppermute x1, starting transfers between devices, shards(): other = lax.ppermute(mine, 'core', [(i, i ^ 1) for i in range(cores)])  7.08 us
    all_to_all x1, starting transfers between devices, exchange(): return lax.all_to_all(blocks, axis, split_axis=0, concat_axis=0, tiled=True)  6.09 us
    ppermute x1, starting transfers between devices, shards(): far_in = lax.ppermute(w_in, SEQ, partner)  4.62 us
  transfers between devices with their start and end apart: 4, of which 2 were waited for; matrix products, arithmetic and copies ran while one was open for 0% of the time, Pallas kernels for 5%

profile of v6, /device:TPU:1, one launch (start us, length us, event | category | flops | bytes accessed | tf_op | source)
XLA Modules:
  0.0 145.0 jit_solution(7612934261224887315)
XLA Ops:
  0.6 2.1 %shard_map.77 = bf16[8,2,32,1152]{3,2,1,0:T(8,128)(2,1)} custom-call(bf16[32,1152]{1,0:T(8,128)(2,1)} %noisy.3, bf16[1,32,1152]{2,1,0:T(8,128)(2,1)} %probe.3), custom_call_target="tpu_custom_call" | custom-call | bytes 2000000 | tf_op jit(solution)/shard_map/pallas_call | solution.py:288
  2.7 0.0 copy-start.4
  2.7 0.0 copy-start.5
  2.7 6.1 %all-to-all-start = ((bf16[8,2,32,1152]{3,2,1,0:T(8,128)(2,1)}), bf16[8,2,32,1152]{3,2,1,0:T(8,128)(2,1)S(1)}, u32[]{:S(2)}, u32[]{:S(2)}) async-start(bf16[8,2,32,1152]{3,2,1,0:T(8,128)(2,1)} %shard_map.77), calls=%async_computation | async-start | bytes 2359296 | tf_op jit(solution)/shard_map/all_to_all | solution.py:300
  8.8 4.6 %collective-permute-start = (bf16[216,1152]{1,0:T(8,128)(2,1)S(1)}, bf16[216,1152]{1,0:T(8,128)(2,1)S(1)}, u32[]{:S(2)}, u32[]{:S(2)}) collective-permute-start(bf16[216,1152]{1,0:T(8,128)(2,1)S(1)} %bitcast.6), channel_id=1, source_target_pairs={{0,12},{1,13},{2,14},{3,15},{4,8},{5,9},{6,10},{7,11},{8,4},{9,5},... | collective-permute-start | bytes 1493000 | tf_op jit(solution)/shard_map/ppermute | solution.py:328
  13.5 1.9 %collective-permute-start.1 = (bf16[72,1152]{1,0:T(8,128)(2,1)S(1)}, bf16[72,1152]{1,0:T(8,128)(2,1)S(1)}, u32[]{:S(2)}, u32[]{:S(2)}) collective-permute-start(bf16[72,1152]{1,0:T(8,128)(2,1)S(1)} %copy-done.5), channel_id=1, source_target_pairs={{0,12},{1,13},{2,14},{3,15},{4,8},{5,9},{6,10},{7,11},{8,4},{9,5},... | collective-permute-start | bytes 497672 | tf_op jit(solution)/shard_map/ppermute | solution.py:329
  16.1 0.6 fusion.4.embedding
  16.7 3.0 %shard_map.78.mods = f32[3,1152]{1,0:T(4,128)} custom-call(bf16[16,256]{1,0:T(8,128)(2,1)} %fusion.4.embedding, bf16[256,3456]{1,0:T(8,128)(2,1)} %w_mod.1), custom_call_target="tpu_custom_call" | custom-call | bytes 2000000 | tf_op jit(solution)/shard_map/pallas_call | solution.py:288
  19.8 0.0 all-to-all-done.gath
  19.8 0.0 copy-start.2
  19.8 0.7 copy-done.2
  20.5 2.6 %shard_map.79 = (bf16[512,1152]{1,0:T(8,128)(2,1)S(1)}, f32[256,1152]{1,0:T(8,128)S(1)}, bf16[3,256,72]{2,1,0:T(8,128)(2,1)S(1)}, bf16[256,256]{1,0:T(8,128)(2,1)S(1)}) custom-call(bf16[8,2,32,1152]{3,2,1,0:T(8,128)(2,1)S(1)} %all-to-all-done.gath, bf16[216,1152]{1,0:T(8,128)(2,1)S(1)} %bitcast.7, bf16[72,1152]{1,0:T(8,128)(2,1)S(1)} %copy-done.5, ...), custom_call_target="tpu_custom_call" | custom-call | flops 1000000000 | bytes 6000000 | tf_op jit(solution)/shard_map/pallas_call | solution.py:288
  23.1 0.0 collective-permute-done.w_in.far_in
  23.1 1.4 shard_map.80
  24.5 1.6 %collective-permute-done.1.w_out.far_out = bf16[72,1152]{1,0:T(8,128)(2,1)S(1)} collective-permute-done((bf16[72,1152]{1,0:T(8,128)(2,1)S(1)}, bf16[72,1152]{1,0:T(8,128)(2,1)S(1)}, u32[]{:S(2)}, u32[]{:S(2)}) %collective-permute-start.1) | collective-permute-done | bytes 165920 | tf_op jit(solution)/shard_map/ppermute | solution.py:329
  26.1 0.3 shard_map.81
  26.4 15.6 %all_to_all.40.parts = bf16[8,32,1152]{2,1,0:T(8,128)(2,1)S(1)} all-to-all(bf16[8,32,1152]{2,1,0:T(8,128)(2,1)S(1)} %shard_map.81), channel_id=1, replica_groups=mesh['z'=16,'core'=2,'frame'=2,'part'=8] {'part'}, dimensions={0} | all-to-all | bytes 1179648 | tf_op jit(solution)/shard_map/all_to_all | solution.py:300
  42.0 0.1 shard_map.82
  42.1 10.9 %all_to_all.41.gated = bf16[8,32,1152]{2,1,0:T(8,128)(2,1)S(1)} all-to-all(bf16[8,32,1152]{2,1,0:T(8,128)(2,1)S(1)} %get-tuple-element.27), channel_id=1, replica_groups=mesh['z'=16,'core'=2,'frame'=2,'part'=8] {'part'}, dimensions={0} | all-to-all | bytes 1179648 | tf_op jit(solution)/shard_map/all_to_all | solution.py:300
  53.0 2.2 %shard_map.83 = bf16[8,32,1152]{2,1,0:T(8,128)(2,1)S(1)} custom-call(bf16[8,32,1152]{2,1,0:T(8,128)(2,1)S(1)} %all_to_all.41.gated, bf16[216,1152]{1,0:T(8,128)(2,1)S(1)} %bitcast.8, bf16[72,1152]{1,0:T(8,128)(2,1)S(1)} %copy-done.5, bf16[3,256,72]{2,1,0:T(8,128)(2,1)S(1)} %get-tuple-element.28.near_primal, ...), custom_call_target="tpu_custom_call" | custom-call | flops 2000000000 | bytes 5000000 | tf_op jit(solution)/shard_map/pallas_call | solution.py:288
  55.1 0.0 copy-start
  55.2 11.3 %all_to_all.42.parts = bf16[8,32,1152]{2,1,0:T(8,128)(2,1)S(1)} all-to-all(bf16[8,32,1152]{2,1,0:T(8,128)(2,1)S(1)} %shard_map.83), channel_id=1, replica_groups=mesh['z'=16,'core'=2,'frame'=2,'part'=8] {'part'}, dimensions={0} | all-to-all | bytes 1179648 | tf_op jit(solution)/shard_map/all_to_all | solution.py:300
  66.5 0.3 shard_map.84
  66.8 28.7 %all_to_all.43.mine = bf16[16,2,1152]{2,1,0:T(2,128)(2,1)S(1)} all-to-all(bf16[16,2,1152]{2,1,0:T(2,128)(2,1)S(1)} %get-tuple-element.33), channel_id=1, replica_groups=mesh['z'=16,'core'=2,'frame'=2,'part'=8] {'z'}, dimensions={0} | all-to-all | bytes 147456 | tf_op jit(solution)/shard_map/all_to_all | solution.py:300
  95.5 7.1 %collective-permute-start.2 = (bf16[16,2,1152]{2,1,0:T(2,128)(2,1)S(1)}, bf16[16,2,1152]{2,1,0:T(2,128)(2,1)S(1)}, u32[]{:S(2)}, u32[]{:S(2)}) collective-permute-start(bf16[16,2,1152]{2,1,0:T(2,128)(2,1)S(1)} %all_to_all.43.mine), channel_id=1, source_target_pairs={{0,16},{16,0},{1,17},{17,1},{2,18},{18,2},{3,19},{19,3},{4,20},{20... | collective-permute-start | bytes 221192 | tf_op jit(solution)/shard_map/ppermute | solution.py:404
  102.6 0.9 collective-permute-done.2.other
  103.5 0.5 shard_map.85
  104.0 9.9 %all_to_all.44.arrived = f32[16,8,128]{2,1,0:T(8,128)S(1)} all-to-all(f32[16,8,128]{2,1,0:T(8,128)S(1)} %get-tuple-element.34), channel_id=1, replica_groups=mesh['z'=16,'core'=2,'frame'=2,'part'=8] {'frame','part'}, dimensions={0} | all-to-all | bytes 131072 | tf_op jit(solution)/shard_map/all_to_all | solution.py:300
  113.9 14.2 %all_to_all.45.arrived = f32[16,8,128]{2,1,0:T(8,128)S(1)} all-to-all(f32[16,8,128]{2,1,0:T(8,128)S(1)} %shard_map.86), channel_id=1, replica_groups=mesh['z'=16,'core'=2,'frame'=2,'part'=8] {'z'}, dimensions={0} | all-to-all | bytes 131072 | tf_op jit(solution)/shard_map/all_to_all | solution.py:300
  128.1 1.7 %shard_map.87 = (f32[32,32]{1,0:T(8,128)S(1)}, bf16[16,2,1152]{2,1,0:T(2,128)(2,1)S(1)}, f32[32,1152]{1,0:T(8,128)S(1)}) custom-call(f32[16,8,128]{2,1,0:T(8,128)S(1)} %all_to_all.45.arrived, bf16[32,2,1152]{2,1,0:T(2,128)(2,1)S(1)} %get-tuple-element.35.rows, f32[32,1152]{1,0:T(8,128)S(1)} %get-tuple-element.36.lost), custom_call_target="tpu_custom_call" | custom-call | bytes 300000 | tf_op jit(solution)/shard_map/pallas_call | solution.py:288
  129.8 14.4 %all_to_all.46.pairs = bf16[16,2,1152]{2,1,0:T(2,128)(2,1)S(1)} all-to-all(bf16[16,2,1152]{2,1,0:T(2,128)(2,1)S(1)} %get-tuple-element.37), channel_id=1, replica_groups=mesh['z'=16,'core'=2,'frame'=2,'part'=8] {'z'}, dimensions={0} | all-to-all | bytes 147456 | tf_op jit(solution)/shard_map/all_to_all | solution.py:300
  144.3 0.7 shard_map.88
  (11 shorter events, 0.1 us)
Async XLA Ops:
  2.7 6.1 %copy-start.4 = (bf16[1152,216]{0,1:T(8,128)(2,1)S(1)}, bf16[1152,216]{0,1:T(8,128)(2,1)}, u32[]{:S(2)}) copy-start(bf16[1152,216]{0,1:T(8,128)(2,1)} %param.8) | copy-start | bytes 1492996
  2.7 10.7 %copy-start.5 = (bf16[72,1152]{1,0:T(8,128)(2,1)S(1)}, bf16[72,1152]{1,0:T(8,128)(2,1)}, u32[]{:S(2)}) copy-start(bf16[72,1152]{1,0:T(8,128)(2,1)} %near_out) | copy-start | bytes 497668
  2.7 17.1 %all-to-all-start = ((bf16[8,2,32,1152]{3,2,1,0:T(8,128)(2,1)}), bf16[8,2,32,1152]{3,2,1,0:T(8,128)(2,1)S(1)}, u32[]{:S(2)}, u32[]{:S(2)}) async-start(bf16[8,2,32,1152]{3,2,1,0:T(8,128)(2,1)} %shard_map.77), calls=%async_computation | async-start | bytes 2359296 | tf_op jit(solution)/shard_map/all_to_all | solution.py:300
  8.8 14.3 %collective-permute-start = (bf16[216,1152]{1,0:T(8,128)(2,1)S(1)}, bf16[216,1152]{1,0:T(8,128)(2,1)S(1)}, u32[]{:S(2)}, u32[]{:S(2)}) collective-permute-start(bf16[216,1152]{1,0:T(8,128)(2,1)S(1)} %bitcast.6), channel_id=1, source_target_pairs={{0,12},{1,13},{2,14},{3,15},{4,8},{5,9},{6,10},{7,11},{8,4},{9,5},... | collective-permute-start | bytes 1493000 | tf_op jit(solution)/shard_map/ppermute | solution.py:328
  13.5 12.6 %collective-permute-start.1 = (bf16[72,1152]{1,0:T(8,128)(2,1)S(1)}, bf16[72,1152]{1,0:T(8,128)(2,1)S(1)}, u32[]{:S(2)}, u32[]{:S(2)}) collective-permute-start(bf16[72,1152]{1,0:T(8,128)(2,1)S(1)} %copy-done.5), channel_id=1, source_target_pairs={{0,12},{1,13},{2,14},{3,15},{4,8},{5,9},{6,10},{7,11},{8,4},{9,5},... | collective-permute-start | bytes 497672 | tf_op jit(solution)/shard_map/ppermute | solution.py:329
  19.8 0.7 copy-start.2
  26.1 15.9 %copy-start.1 = (bf16[1,32,1152]{2,1,0:T(8,128)(2,1)S(1)}, bf16[1,32,1152]{2,1,0:T(8,128)(2,1)}, u32[]{:S(2)}) copy-start(bf16[1,32,1152]{2,1,0:T(8,128)(2,1)} %probe.3) | copy-start | bytes 221188
  26.1 15.9 %copy-start.3 = (f32[3,1152]{1,0:T(4,128)S(1)}, f32[3,1152]{1,0:T(4,128)}, u32[]{:S(2)}) copy-start(f32[3,1152]{1,0:T(4,128)} %shard_map.78.mods) | copy-start | bytes 41476
  55.1 11.4 %copy-start = (bf16[32,1152]{1,0:T(8,128)(2,1)S(1)}, bf16[32,1152]{1,0:T(8,128)(2,1)}, u32[]{:S(2)}) copy-start(bf16[32,1152]{1,0:T(8,128)(2,1)} %noisy.3) | copy-start | bytes 221188
  95.5 8.0 %collective-permute-start.2 = (bf16[16,2,1152]{2,1,0:T(2,128)(2,1)S(1)}, bf16[16,2,1152]{2,1,0:T(2,128)(2,1)S(1)}, u32[]{:S(2)}, u32[]{:S(2)}) collective-permute-start(bf16[16,2,1152]{2,1,0:T(2,128)(2,1)S(1)} %all_to_all.43.mine), channel_id=1, source_target_pairs={{0,16},{16,0},{1,17},{17,1},{2,18},{18,2},{3,19},{19,3},{4,20},{20... | collective-permute-start | bytes 221192 | tf_op jit(solution)/shard_map/ppermute | solution.py:404

commit v7 on v5

--- a/solution.py
+++ b/solution.py
@@ -47,13 +47,11 @@
     freq_index = jnp.arange(half_dim, dtype=jnp.float32)
     frequency = jnp.exp(-math.log(10000.0) * freq_index / half_dim)
     angles = timestep[0].astype(jnp.float32) * frequency
-    rest = jax.nn.silu(jnp.concatenate([jnp.cos(angles), jnp.sin(angles)]))
-    pieces = []
-    for _ in range(3):
-        pieces.append(lax.reduce_precision(rest, 8, 7))
-        rest = rest - pieces[-1]
-    rows = jnp.pad(jnp.stack(pieces), ((0, 13), (0, 0))).astype(BF)
-    return jnp.sum(mm(rows, w_mod), axis=0).reshape(3, feat_width)
+    embedding = jnp.concatenate([jnp.cos(angles), jnp.sin(angles)])
+    modulated = jnp.dot(
+        jax.nn.silu(embedding)[None, :], w_mod.astype(jnp.float32), precision=lax.Precision.HIGHEST
+    )
+    return modulated.reshape(3, feat_width)
 
 
 def normalize(values_f):

time: 151 us -> 146 us (0.967)
  blocking collectives: 107 us -> 103 us
  local copies, waits for them, and re-layouts: 0.04 us -> 3.9 us
  waiting for transfers between devices: 4.63 us -> 0.92 us
  Pallas kernels: 15.3 us -> 12 us
  matrix products: 0.36 us -> 2.95 us
    unnamed x8 -> x9, local copies, waits for them, and re-layouts: 0.02 us -> 3.9 us
    all_to_all x7, blocking collectives: 107 us -> 103 us  [exchange(): return lax.all_to_all(blocks, axis, split_axis=0, concat_axis=0, tiled=True)]
    pallas_call x11, Pallas kernels: 15.3 us -> 12 us  [call(): pl.pallas_call(kernel, out_shape=out_shape, in_specs=where or [LOCAL] * l...]
    all_to_all x1, waiting for transfers between devices: 3.15 us -> 0.03 us  [exchange(): return lax.all_to_all(blocks, axis, split_axis=0, concat_axis=0, tiled=True)]
    dot_general x1, matrix products: 0.36 us -> 2.95 us  [modulation(): jnp.dot(jax.nn.silu(embedding)[None, :], w_mod.astype(jnp.float32), preci...]
  transfers between devices with their start and end apart: 4 -> 4, of which waited for: 3 -> 1; matrix products, arithmetic and copies ran while one was open for 0% -> 5% of each run, Pallas kernels for 4% -> 3%
where the time goes in v7:
time: 146 us; the launch traced here: 144 us
  blocking collectives  103 us (71%)
  starting transfers between devices  19.6 us (13%)
  Pallas kernels  12 us (8%)
  local copies, waits for them, and re-layouts  3.9 us (3%)
  matrix products  2.95 us (2%)
    all_to_all x7, blocking collectives, exchange(): return lax.all_to_all(blocks, axis, split_axis=0, concat_axis=0, tiled=True)  103 us
    pallas_call x11, Pallas kernels, call(): pl.pallas_call(kernel, out_shape=out_shape, in_specs=where or [LOCAL] * l...  12 us
    ppermute x1, starting transfers between devices, shards(): other = lax.ppermute(mine, 'core', [(i, i ^ 1) for i in range(cores)])  7.08 us
    all_to_all x1, starting transfers between devices, exchange(): return lax.all_to_all(blocks, axis, split_axis=0, concat_axis=0, tiled=True)  5.96 us
    ppermute x1, starting transfers between devices, shards(): far_in = lax.ppermute(w_in, SEQ, partner)  4.62 us
    unnamed x9, local copies, waits for them, and re-layouts  3.9 us
    dot_general x1, matrix products, modulation(): jnp.dot(jax.nn.silu(embedding)[None, :], w_mod.astype(jnp.float32), preci...  2.95 us
  transfers between devices with their start and end apart: 4, of which 1 were waited for; matrix products, arithmetic and copies ran while one was open for 5% of the time, Pallas kernels for 3%

profile of v7, /device:TPU:1, one launch (start us, length us, event | category | flops | bytes accessed | tf_op | source)
XLA Modules:
  0.0 143.8 jit_solution(8104456647197802309)
XLA Ops:
  0.6 0.0 copy-start.2
  0.6 0.0 copy-start.3
  0.6 2.1 %shard_map.77 = bf16[8,2,32,1152]{3,2,1,0:T(8,128)(2,1)} custom-call(bf16[32,1152]{1,0:T(8,128)(2,1)} %noisy.3, bf16[1,32,1152]{2,1,0:T(8,128)(2,1)} %probe.3), custom_call_target="tpu_custom_call" | custom-call | bytes 2000000 | tf_op jit(solution)/shard_map/pallas_call | solution.py:278
  2.8 6.0 %all-to-all-start = ((bf16[8,2,32,1152]{3,2,1,0:T(8,128)(2,1)}), bf16[8,2,32,1152]{3,2,1,0:T(8,128)(2,1)S(1)}, u32[]{:S(2)}, u32[]{:S(2)}) async-start(bf16[8,2,32,1152]{3,2,1,0:T(8,128)(2,1)} %shard_map.77), calls=%async_computation | async-start | bytes 2359296 | tf_op jit(solution)/shard_map/all_to_all | solution.py:290
  8.7 0.0 copy-done.2
  8.7 4.6 %collective-permute-start = (bf16[216,1152]{1,0:T(8,128)(2,1)S(1)}, bf16[216,1152]{1,0:T(8,128)(2,1)S(1)}, u32[]{:S(2)}, u32[]{:S(2)}) collective-permute-start(bf16[216,1152]{1,0:T(8,128)(2,1)S(1)} %bitcast.14), channel_id=1, source_target_pairs={{0,12},{1,13},{2,14},{3,15},{4,8},{5,9},{6,10},{7,11},{8,4},{9,5},... | collective-permute-start | bytes 1493000 | tf_op jit(solution)/shard_map/ppermute | solution.py:318
  13.4 0.0 copy-done.3
  13.4 1.9 %collective-permute-start.1 = (bf16[72,1152]{1,0:T(8,128)(2,1)S(1)}, bf16[72,1152]{1,0:T(8,128)(2,1)S(1)}, u32[]{:S(2)}, u32[]{:S(2)}) collective-permute-start(bf16[72,1152]{1,0:T(8,128)(2,1)S(1)} %copy-done.3), channel_id=1, source_target_pairs={{0,12},{1,13},{2,14},{3,15},{4,8},{5,9},{6,10},{7,11},{8,4},{9,5},... | collective-permute-start | bytes 497672 | tf_op jit(solution)/shard_map/ppermute | solution.py:319
  16.0 3.9 %copy.8 = bf16[256,3456]{0,1:T(8,128)(2,1)} copy(bf16[256,3456]{1,0:T(8,128)(2,1)} %param.10) | data formatting | bytes 3538944 | tf_op args[4]
  19.9 3.0 %fusion.2 = f32[1,3,1152]{2,0,1:T(1,128)S(1)} fusion(f32[256,1,1]{0,1,2:T(1,128)S(1)} %bitcast.18, bf16[3,1152,256]{2,1,0:T(8,128)(2,1)} %bitcast.17), kind=kOutput, calls=%fused_computation.6 | convolution fusion | flops 10616832 | bytes 1784320 | tf_op jit(solution)/shard_map/dot_general | solution.py:51
  22.9 0.0 all-to-all-done.gath
  22.9 2.6 %shard_map.78 = (bf16[512,1152]{1,0:T(8,128)(2,1)S(1)}, f32[256,1152]{1,0:T(8,128)S(1)}, bf16[3,256,72]{2,1,0:T(8,128)(2,1)S(1)}, bf16[256,256]{1,0:T(8,128)(2,1)S(1)}) custom-call(bf16[8,2,32,1152]{3,2,1,0:T(8,128)(2,1)S(1)} %all-to-all-done.gath, bf16[216,1152]{1,0:T(8,128)(2,1)S(1)} %bitcast.15, bf16[72,1152]{1,0:T(8,128)(2,1)S(1)} %copy-done.3, ...), custom_call_target="tpu_custom_call" | custom-call | flops 1000000000 | bytes 6000000 | tf_op jit(solution)/shard_map/pallas_call | solution.py:278
  25.5 0.0 collective-permute-done.w_in.far_in
  25.5 1.4 shard_map.79
  26.9 0.0 copy-start.1
  26.9 0.0 collective-permute-done.1.w_out.far_out
  26.9 0.3 shard_map.80
  27.2 12.9 %all_to_all.40.parts = bf16[8,32,1152]{2,1,0:T(8,128)(2,1)S(1)} all-to-all(bf16[8,32,1152]{2,1,0:T(8,128)(2,1)S(1)} %shard_map.80), channel_id=1, replica_groups=mesh['z'=16,'core'=2,'frame'=2,'part'=8] {'part'}, dimensions={0} | all-to-all | bytes 1179648 | tf_op jit(solution)/shard_map/all_to_all | solution.py:290
  40.1 0.1 shard_map.81
  40.2 10.4 %all_to_all.41.gated = bf16[8,32,1152]{2,1,0:T(8,128)(2,1)S(1)} all-to-all(bf16[8,32,1152]{2,1,0:T(8,128)(2,1)S(1)} %get-tuple-element.27), channel_id=1, replica_groups=mesh['z'=16,'core'=2,'frame'=2,'part'=8] {'part'}, dimensions={0} | all-to-all | bytes 1179648 | tf_op jit(solution)/shard_map/all_to_all | solution.py:290
  50.6 2.1 %shard_map.82 = bf16[8,32,1152]{2,1,0:T(8,128)(2,1)S(1)} custom-call(bf16[8,32,1152]{2,1,0:T(8,128)(2,1)S(1)} %all_to_all.41.gated, bf16[216,1152]{1,0:T(8,128)(2,1)S(1)} %bitcast.16, bf16[72,1152]{1,0:T(8,128)(2,1)S(1)} %copy-done.3, bf16[3,256,72]{2,1,0:T(8,128)(2,1)S(1)} %get-tuple-element.28.near_primal, ...), custom_call_target="tpu_custom_call" | custom-call | flops 2000000000 | bytes 5000000 | tf_op jit(solution)/shard_map/pallas_call | solution.py:278
  52.7 10.4 %all_to_all.42.parts = bf16[8,32,1152]{2,1,0:T(8,128)(2,1)S(1)} all-to-all(bf16[8,32,1152]{2,1,0:T(8,128)(2,1)S(1)} %shard_map.82), channel_id=1, replica_groups=mesh['z'=16,'core'=2,'frame'=2,'part'=8] {'part'}, dimensions={0} | all-to-all | bytes 1179648 | tf_op jit(solution)/shard_map/all_to_all | solution.py:290
  63.1 0.3 shard_map.83
  63.5 30.9 %all_to_all.43.mine = bf16[16,2,1152]{2,1,0:T(2,128)(2,1)S(1)} all-to-all(bf16[16,2,1152]{2,1,0:T(2,128)(2,1)S(1)} %get-tuple-element.33), channel_id=1, replica_groups=mesh['z'=16,'core'=2,'frame'=2,'part'=8] {'z'}, dimensions={0} | all-to-all | bytes 147456 | tf_op jit(solution)/shard_map/all_to_all | solution.py:290
  94.4 7.1 %collective-permute-start.2 = (bf16[16,2,1152]{2,1,0:T(2,128)(2,1)S(1)}, bf16[16,2,1152]{2,1,0:T(2,128)(2,1)S(1)}, u32[]{:S(2)}, u32[]{:S(2)}) collective-permute-start(bf16[16,2,1152]{2,1,0:T(2,128)(2,1)S(1)} %all_to_all.43.mine), channel_id=1, source_target_pairs={{0,16},{16,0},{1,17},{17,1},{2,18},{18,2},{3,19},{19,3},{4,20},{20... | collective-permute-start | bytes 221192 | tf_op jit(solution)/shard_map/ppermute | solution.py:385
  101.5 0.9 collective-permute-done.2.other
  102.4 0.5 shard_map.84
  102.9 9.7 %all_to_all.44.arrived = f32[16,8,128]{2,1,0:T(8,128)S(1)} all-to-all(f32[16,8,128]{2,1,0:T(8,128)S(1)} %get-tuple-element.34), channel_id=1, replica_groups=mesh['z'=16,'core'=2,'frame'=2,'part'=8] {'frame','part'}, dimensions={0} | all-to-all | bytes 131072 | tf_op jit(solution)/shard_map/all_to_all | solution.py:290
  112.7 14.2 %all_to_all.45.arrived = f32[16,8,128]{2,1,0:T(8,128)S(1)} all-to-all(f32[16,8,128]{2,1,0:T(8,128)S(1)} %shard_map.85), channel_id=1, replica_groups=mesh['z'=16,'core'=2,'frame'=2,'part'=8] {'z'}, dimensions={0} | all-to-all | bytes 131072 | tf_op jit(solution)/shard_map/all_to_all | solution.py:290
  126.9 1.7 %shard_map.86 = (f32[32,32]{1,0:T(8,128)S(1)}, bf16[16,2,1152]{2,1,0:T(2,128)(2,1)S(1)}, f32[32,1152]{1,0:T(8,128)S(1)}) custom-call(f32[16,8,128]{2,1,0:T(8,128)S(1)} %all_to_all.45.arrived, bf16[32,2,1152]{2,1,0:T(2,128)(2,1)S(1)} %get-tuple-element.35.rows, f32[32,1152]{1,0:T(8,128)S(1)} %get-tuple-element.36.lost), custom_call_target="tpu_custom_call" | custom-call | bytes 300000 | tf_op jit(solution)/shard_map/pallas_call | solution.py:278
  128.6 14.5 %all_to_all.46.pairs = bf16[16,2,1152]{2,1,0:T(2,128)(2,1)S(1)} all-to-all(bf16[16,2,1152]{2,1,0:T(2,128)(2,1)S(1)} %get-tuple-element.37), channel_id=1, replica_groups=mesh['z'=16,'core'=2,'frame'=2,'part'=8] {'z'}, dimensions={0} | all-to-all | bytes 147456 | tf_op jit(solution)/shard_map/all_to_all | solution.py:290
  143.1 0.7 shard_map.87
  (7 shorter events, 0.1 us)
Async XLA Ops:
  0.6 8.1 %copy-start.2 = (bf16[1152,216]{0,1:T(8,128)(2,1)S(1)}, bf16[1152,216]{0,1:T(8,128)(2,1)}, u32[]{:S(2)}) copy-start(bf16[1152,216]{0,1:T(8,128)(2,1)} %param.8) | copy-start | bytes 1492996
  0.6 12.7 %copy-start.3 = (bf16[72,1152]{1,0:T(8,128)(2,1)S(1)}, bf16[72,1152]{1,0:T(8,128)(2,1)}, u32[]{:S(2)}) copy-start(bf16[72,1152]{1,0:T(8,128)(2,1)} %near_out) | copy-start | bytes 497668
  2.8 20.1 %all-to-all-start = ((bf16[8,2,32,1152]{3,2,1,0:T(8,128)(2,1)}), bf16[8,2,32,1152]{3,2,1,0:T(8,128)(2,1)S(1)}, u32[]{:S(2)}, u32[]{:S(2)}) async-start(bf16[8,2,32,1152]{3,2,1,0:T(8,128)(2,1)} %shard_map.77), calls=%async_computation | async-start | bytes 2359296 | tf_op jit(solution)/shard_map/all_to_all | solution.py:290
  8.7 16.7 %collective-permute-start = (bf16[216,1152]{1,0:T(8,128)(2,1)S(1)}, bf16[216,1152]{1,0:T(8,128)(2,1)S(1)}, u32[]{:S(2)}, u32[]{:S(2)}) collective-permute-start(bf16[216,1152]{1,0:T(8,128)(2,1)S(1)} %bitcast.14), channel_id=1, source_target_pairs={{0,12},{1,13},{2,14},{3,15},{4,8},{5,9},{6,10},{7,11},{8,4},{9,5},... | collective-permute-start | bytes 1493000 | tf_op jit(solution)/shard_map/ppermute | solution.py:318
  13.4 13.5 %collective-permute-start.1 = (bf16[72,1152]{1,0:T(8,128)(2,1)S(1)}, bf16[72,1152]{1,0:T(8,128)(2,1)S(1)}, u32[]{:S(2)}, u32[]{:S(2)}) collective-permute-start(bf16[72,1152]{1,0:T(8,128)(2,1)S(1)} %copy-done.3), channel_id=1, source_target_pairs={{0,12},{1,13},{2,14},{3,15},{4,8},{5,9},{6,10},{7,11},{8,4},{9,5},... | collective-permute-start | bytes 497672 | tf_op jit(solution)/shard_map/ppermute | solution.py:319
  26.9 13.2 %copy-start.1 = (bf16[1,32,1152]{2,1,0:T(8,128)(2,1)S(1)}, bf16[1,32,1152]{2,1,0:T(8,128)(2,1)}, u32[]{:S(2)}) copy-start(bf16[1,32,1152]{2,1,0:T(8,128)(2,1)} %probe.3) | copy-start | bytes 221188
  50.6 12.5 %copy-start = (bf16[32,1152]{1,0:T(8,128)(2,1)S(1)}, bf16[32,1152]{1,0:T(8,128)(2,1)}, u32[]{:S(2)}) copy-start(bf16[32,1152]{1,0:T(8,128)(2,1)} %noisy.3) | copy-start | bytes 221188
  94.4 8.0 %collective-permute-start.2 = (bf16[16,2,1152]{2,1,0:T(2,128)(2,1)S(1)}, bf16[16,2,1152]{2,1,0:T(2,128)(2,1)S(1)}, u32[]{:S(2)}, u32[]{:S(2)}) collective-permute-start(bf16[16,2,1152]{2,1,0:T(2,128)(2,1)S(1)} %all_to_all.43.mine), channel_id=1, source_target_pairs={{0,16},{16,0},{1,17},{17,1},{2,18},{18,2},{3,19},{19,3},{4,20},{20... | collective-permute-start | bytes 221192 | tf_op jit(solution)/shard_map/ppermute | solution.py:385

commit v8 on v7

--- a/solution.py
+++ b/solution.py
@@ -16,6 +16,7 @@
 PROBE = ("z", "core")
 MIB = 1024 * 1024
 STEP = 4
+FEW = 16
 NT = (((1,), (1,)), ((), ()))
 NN = (((1,), (0,)), ((), ()))
 BF = jnp.bfloat16
@@ -109,10 +110,12 @@
     scale = 1.0 + mods[1:2, :]
     shift = mods[0:1, :]
     for i in range(blocks):
-        normed, inverse = normalize(gath[i, 0].astype(F32))
-        tokens[pl.ds(i * rows, rows), :] = (normed * scale + shift).astype(BF)
-        field = norm_tangent(gath[i, 1].astype(F32), normed, inverse)
-        tokens[pl.ds((blocks + i) * rows, rows), :] = (field * scale).astype(BF)
+        for at in range(0, rows, FEW):
+            few = pl.ds(at, FEW)
+            normed, inverse = normalize(gath[i, 0, few, :].astype(F32))
+            tokens[pl.ds(i * rows + at, FEW), :] = (normed * scale + shift).astype(BF)
+            field = norm_tangent(gath[i, 1, few, :].astype(F32), normed, inverse)
+            tokens[pl.ds((blocks + i) * rows + at, FEW), :] = (field * scale).astype(BF)
     term[...] = mm(head_forward(tokens, w_in, primal, probs), w_out[...])
 
 
@@ -138,15 +141,28 @@
 
 
 def adjoint_kernel(
-    gated, near_in, near_out, near_primal, near_probs, far_in, far_out, far_primal, far_probs, parts
+    gated,
+    near_in,
+    near_out,
+    near_primal,
+    near_probs,
+    far_in,
+    far_out,
+    far_primal,
+    far_probs,
+    parts,
+    w_in,
 ):
     c = HEAD_DIM ** (-0.5)
     blocks, rows, width = gated.shape
     whole = gated[...].reshape(blocks * rows, width)
-    total = None
-    for w_in, w_out, primal, probs in (
-        (near_in, near_out, near_primal, near_probs),
-        (far_in, far_out, far_primal, far_probs),
+    third = 3 * HEAD_DIM
+    w_in[pl.ds(0, third), :] = near_in[...].astype(F32)
+    w_in[pl.ds(third, third), :] = far_in[...].astype(F32)
+    grads = []
+    for w_out, primal, probs in (
+        (near_out, near_primal, near_probs),
+        (far_out, far_primal, far_probs),
     ):
         co = mm(whole, w_out[...], NT).astype(BF)
         q, k, v = primal[0], primal[1], primal[2]
@@ -155,11 +171,9 @@
         d_probs = mm(co, v, NT)
         row_dot = jnp.sum(p_float * d_probs, axis=-1, keepdims=True)
         scaled = (p_float * (d_probs - row_dot) * c).astype(BF)
-        grads = (mm(scaled, k), mm(flip(scaled), q), mm(flip(p), co))
-        grads = jnp.concatenate(grads, axis=1).astype(BF)
-        term = mm(grads, w_in[...])
-        total = term if total is None else total + term
-    parts[...] = total.astype(BF).reshape(parts.shape)
+        grads += [mm(scaled, k), mm(flip(scaled), q), mm(flip(p), co)]
+    grads = jnp.concatenate(grads, axis=1).astype(BF)
+    parts[...] = mm(grads, w_in[...].astype(BF)).astype(BF).reshape(parts.shape)
 
 
 def pulled_kernel(parts, update, noisy, mods, pulled, lost):
@@ -371,6 +385,7 @@
         far_out,
         far_primal,
         far_probs,
+        scratch=(pltpu.VMEM((6 * HEAD_DIM, width), F32),),
         flops=2 * 10**9,
         moved=5 * 10**6,
         limit=24,

time: 146 us -> 146 us (level)
  no operation moved by 1% of the time
where the time goes in v8:
time: 146 us; the launch traced here: 144 us
  blocking collectives  103 us (71%)
  starting transfers between devices  19.6 us (13%)
  Pallas kernels  11.9 us (8%)
  local copies, waits for them, and re-layouts  3.9 us (3%)
  matrix products  2.95 us (2%)
    all_to_all x7, blocking collectives, exchange(): return lax.all_to_all(blocks, axis, split_axis=0, concat_axis=0, tiled=True)  103 us
    pallas_call x11, Pallas kernels, call(): pl.pallas_call(kernel, out_shape=out_shape, in_specs=where or [LOCAL] * l...  11.9 us
    ppermute x1, starting transfers between devices, shards(): other = lax.ppermute(mine, 'core', [(i, i ^ 1) for i in range(cores)])  7.08 us
    all_to_all x1, starting transfers between devices, exchange(): return lax.all_to_all(blocks, axis, split_axis=0, concat_axis=0, tiled=True)  5.96 us
    ppermute x1, starting transfers between devices, shards(): far_in = lax.ppermute(w_in, SEQ, partner)  4.62 us
    unnamed x9, local copies, waits for them, and re-layouts  3.9 us
    dot_general x1, matrix products, modulation(): jnp.dot(jax.nn.silu(embedding)[None, :], w_mod.astype(jnp.float32), preci...  2.95 us
  transfers between devices with their start and end apart: 4, of which 1 were waited for; matrix products, arithmetic and copies ran while one was open for 5% of the time, Pallas kernels for 3%

profile of v8, /device:TPU:1, one launch (start us, length us, event | category | flops | bytes accessed | tf_op | source)
XLA Modules:
  0.0 143.7 jit_solution(9416983059287046675)
XLA Ops:
  0.6 0.0 copy-start.2
  0.6 0.0 copy-start.3
  0.6 2.1 %shard_map.77 = bf16[8,2,32,1152]{3,2,1,0:T(8,128)(2,1)} custom-call(bf16[32,1152]{1,0:T(8,128)(2,1)} %noisy.3, bf16[1,32,1152]{2,1,0:T(8,128)(2,1)} %probe.3), custom_call_target="tpu_custom_call" | custom-call | bytes 2000000 | tf_op jit(solution)/shard_map/pallas_call | solution.py:292
  2.8 6.0 %all-to-all-start = ((bf16[8,2,32,1152]{3,2,1,0:T(8,128)(2,1)}), bf16[8,2,32,1152]{3,2,1,0:T(8,128)(2,1)S(1)}, u32[]{:S(2)}, u32[]{:S(2)}) async-start(bf16[8,2,32,1152]{3,2,1,0:T(8,128)(2,1)} %shard_map.77), calls=%async_computation | async-start | bytes 2359296 | tf_op jit(solution)/shard_map/all_to_all | solution.py:304
  8.7 0.0 copy-done.2
  8.7 4.6 %collective-permute-start = (bf16[216,1152]{1,0:T(8,128)(2,1)S(1)}, bf16[216,1152]{1,0:T(8,128)(2,1)S(1)}, u32[]{:S(2)}, u32[]{:S(2)}) collective-permute-start(bf16[216,1152]{1,0:T(8,128)(2,1)S(1)} %bitcast.14), channel_id=1, source_target_pairs={{0,12},{1,13},{2,14},{3,15},{4,8},{5,9},{6,10},{7,11},{8,4},{9,5},... | collective-permute-start | bytes 1493000 | tf_op jit(solution)/shard_map/ppermute | solution.py:332
  13.4 0.0 copy-done.3
  13.4 1.9 %collective-permute-start.1 = (bf16[72,1152]{1,0:T(8,128)(2,1)S(1)}, bf16[72,1152]{1,0:T(8,128)(2,1)S(1)}, u32[]{:S(2)}, u32[]{:S(2)}) collective-permute-start(bf16[72,1152]{1,0:T(8,128)(2,1)S(1)} %copy-done.3), channel_id=1, source_target_pairs={{0,12},{1,13},{2,14},{3,15},{4,8},{5,9},{6,10},{7,11},{8,4},{9,5},... | collective-permute-start | bytes 497672 | tf_op jit(solution)/shard_map/ppermute | solution.py:333
  16.0 3.9 %copy.8 = bf16[256,3456]{0,1:T(8,128)(2,1)} copy(bf16[256,3456]{1,0:T(8,128)(2,1)} %param.10) | data formatting | bytes 3538944 | tf_op args[4]
  19.9 3.0 %fusion.2 = f32[1,3,1152]{2,0,1:T(1,128)S(1)} fusion(f32[256,1,1]{0,1,2:T(1,128)S(1)} %bitcast.18, bf16[3,1152,256]{2,1,0:T(8,128)(2,1)} %bitcast.17), kind=kOutput, calls=%fused_computation.6 | convolution fusion | flops 10616832 | bytes 1784320 | tf_op jit(solution)/shard_map/dot_general | solution.py:52
  22.9 0.0 all-to-all-done.gath
  22.9 2.6 %shard_map.78 = (bf16[512,1152]{1,0:T(8,128)(2,1)S(1)}, f32[256,1152]{1,0:T(8,128)S(1)}, bf16[3,256,72]{2,1,0:T(8,128)(2,1)S(1)}, bf16[256,256]{1,0:T(8,128)(2,1)S(1)}) custom-call(bf16[8,2,32,1152]{3,2,1,0:T(8,128)(2,1)S(1)} %all-to-all-done.gath, bf16[216,1152]{1,0:T(8,128)(2,1)S(1)} %bitcast.15, bf16[72,1152]{1,0:T(8,128)(2,1)S(1)} %copy-done.3, ...), custom_call_target="tpu_custom_call" | custom-call | flops 1000000000 | bytes 6000000 | tf_op jit(solution)/shard_map/pallas_call | solution.py:292
  25.5 0.0 collective-permute-done.w_in.far_in
  25.5 1.4 shard_map.79
  26.9 0.0 copy-start.1
  26.9 0.0 collective-permute-done.1.w_out.far_out
  26.9 0.3 shard_map.80
  27.2 12.9 %all_to_all.40.parts = bf16[8,32,1152]{2,1,0:T(8,128)(2,1)S(1)} all-to-all(bf16[8,32,1152]{2,1,0:T(8,128)(2,1)S(1)} %shard_map.80), channel_id=1, replica_groups=mesh['z'=16,'core'=2,'frame'=2,'part'=8] {'part'}, dimensions={0} | all-to-all | bytes 1179648 | tf_op jit(solution)/shard_map/all_to_all | solution.py:304
  40.1 0.1 shard_map.81
  40.2 10.4 %all_to_all.41.gated = bf16[8,32,1152]{2,1,0:T(8,128)(2,1)S(1)} all-to-all(bf16[8,32,1152]{2,1,0:T(8,128)(2,1)S(1)} %get-tuple-element.27), channel_id=1, replica_groups=mesh['z'=16,'core'=2,'frame'=2,'part'=8] {'part'}, dimensions={0} | all-to-all | bytes 1179648 | tf_op jit(solution)/shard_map/all_to_all | solution.py:304
  50.6 2.1 %shard_map.82 = bf16[8,32,1152]{2,1,0:T(8,128)(2,1)S(1)} custom-call(bf16[8,32,1152]{2,1,0:T(8,128)(2,1)S(1)} %all_to_all.41.gated, bf16[216,1152]{1,0:T(8,128)(2,1)S(1)} %bitcast.16, bf16[72,1152]{1,0:T(8,128)(2,1)S(1)} %copy-done.3, bf16[3,256,72]{2,1,0:T(8,128)(2,1)S(1)} %get-tuple-element.28.near_primal, ...), custom_call_target="tpu_custom_call" | custom-call | flops 2000000000 | bytes 5000000 | tf_op jit(solution)/shard_map/pallas_call | solution.py:292
  52.7 10.4 %all_to_all.42.parts = bf16[8,32,1152]{2,1,0:T(8,128)(2,1)S(1)} all-to-all(bf16[8,32,1152]{2,1,0:T(8,128)(2,1)S(1)} %shard_map.82), channel_id=1, replica_groups=mesh['z'=16,'core'=2,'frame'=2,'part'=8] {'part'}, dimensions={0} | all-to-all | bytes 1179648 | tf_op jit(solution)/shard_map/all_to_all | solution.py:304
  63.1 0.3 shard_map.83
  63.4 30.9 %all_to_all.43.mine = bf16[16,2,1152]{2,1,0:T(2,128)(2,1)S(1)} all-to-all(bf16[16,2,1152]{2,1,0:T(2,128)(2,1)S(1)} %get-tuple-element.33), channel_id=1, replica_groups=mesh['z'=16,'core'=2,'frame'=2,'part'=8] {'z'}, dimensions={0} | all-to-all | bytes 147456 | tf_op jit(solution)/shard_map/all_to_all | solution.py:304
  94.3 7.1 %collective-permute-start.2 = (bf16[16,2,1152]{2,1,0:T(2,128)(2,1)S(1)}, bf16[16,2,1152]{2,1,0:T(2,128)(2,1)S(1)}, u32[]{:S(2)}, u32[]{:S(2)}) collective-permute-start(bf16[16,2,1152]{2,1,0:T(2,128)(2,1)S(1)} %all_to_all.43.mine), channel_id=1, source_target_pairs={{0,16},{16,0},{1,17},{17,1},{2,18},{18,2},{3,19},{19,3},{4,20},{20... | collective-permute-start | bytes 221192 | tf_op jit(solution)/shard_map/ppermute | solution.py:400
  101.4 0.9 collective-permute-done.2.other
  102.3 0.5 shard_map.84
  102.8 9.7 %all_to_all.44.arrived = f32[16,8,128]{2,1,0:T(8,128)S(1)} all-to-all(f32[16,8,128]{2,1,0:T(8,128)S(1)} %get-tuple-element.34), channel_id=1, replica_groups=mesh['z'=16,'core'=2,'frame'=2,'part'=8] {'frame','part'}, dimensions={0} | all-to-all | bytes 131072 | tf_op jit(solution)/shard_map/all_to_all | solution.py:304
  112.6 14.2 %all_to_all.45.arrived = f32[16,8,128]{2,1,0:T(8,128)S(1)} all-to-all(f32[16,8,128]{2,1,0:T(8,128)S(1)} %shard_map.85), channel_id=1, replica_groups=mesh['z'=16,'core'=2,'frame'=2,'part'=8] {'z'}, dimensions={0} | all-to-all | bytes 131072 | tf_op jit(solution)/shard_map/all_to_all | solution.py:304
  126.8 1.7 %shard_map.86 = (f32[32,32]{1,0:T(8,128)S(1)}, bf16[16,2,1152]{2,1,0:T(2,128)(2,1)S(1)}, f32[32,1152]{1,0:T(8,128)S(1)}) custom-call(f32[16,8,128]{2,1,0:T(8,128)S(1)} %all_to_all.45.arrived, bf16[32,2,1152]{2,1,0:T(2,128)(2,1)S(1)} %get-tuple-element.35.rows, f32[32,1152]{1,0:T(8,128)S(1)} %get-tuple-element.36.lost), custom_call_target="tpu_custom_call" | custom-call | bytes 300000 | tf_op jit(solution)/shard_map/pallas_call | solution.py:292
  128.6 14.4 %all_to_all.46.pairs = bf16[16,2,1152]{2,1,0:T(2,128)(2,1)S(1)} all-to-all(bf16[16,2,1152]{2,1,0:T(2,128)(2,1)S(1)} %get-tuple-element.37), channel_id=1, replica_groups=mesh['z'=16,'core'=2,'frame'=2,'part'=8] {'z'}, dimensions={0} | all-to-all | bytes 147456 | tf_op jit(solution)/shard_map/all_to_all | solution.py:304
  143.0 0.7 shard_map.87
  (7 shorter events, 0.1 us)
Async XLA Ops:
  0.6 8.1 %copy-start.2 = (bf16[1152,216]{0,1:T(8,128)(2,1)S(1)}, bf16[1152,216]{0,1:T(8,128)(2,1)}, u32[]{:S(2)}) copy-start(bf16[1152,216]{0,1:T(8,128)(2,1)} %param.8) | copy-start | bytes 1492996
  0.6 12.7 %copy-start.3 = (bf16[72,1152]{1,0:T(8,128)(2,1)S(1)}, bf16[72,1152]{1,0:T(8,128)(2,1)}, u32[]{:S(2)}) copy-start(bf16[72,1152]{1,0:T(8,128)(2,1)} %near_out) | copy-start | bytes 497668
  2.8 20.1 %all-to-all-start = ((bf16[8,2,32,1152]{3,2,1,0:T(8,128)(2,1)}), bf16[8,2,32,1152]{3,2,1,0:T(8,128)(2,1)S(1)}, u32[]{:S(2)}, u32[]{:S(2)}) async-start(bf16[8,2,32,1152]{3,2,1,0:T(8,128)(2,1)} %shard_map.77), calls=%async_computation | async-start | bytes 2359296 | tf_op jit(solution)/shard_map/all_to_all | solution.py:304
  8.7 16.7 %collective-permute-start = (bf16[216,1152]{1,0:T(8,128)(2,1)S(1)}, bf16[216,1152]{1,0:T(8,128)(2,1)S(1)}, u32[]{:S(2)}, u32[]{:S(2)}) collective-permute-start(bf16[216,1152]{1,0:T(8,128)(2,1)S(1)} %bitcast.14), channel_id=1, source_target_pairs={{0,12},{1,13},{2,14},{3,15},{4,8},{5,9},{6,10},{7,11},{8,4},{9,5},... | collective-permute-start | bytes 1493000 | tf_op jit(solution)/shard_map/ppermute | solution.py:332
  13.4 13.5 %collective-permute-start.1 = (bf16[72,1152]{1,0:T(8,128)(2,1)S(1)}, bf16[72,1152]{1,0:T(8,128)(2,1)S(1)}, u32[]{:S(2)}, u32[]{:S(2)}) collective-permute-start(bf16[72,1152]{1,0:T(8,128)(2,1)S(1)} %copy-done.3), channel_id=1, source_target_pairs={{0,12},{1,13},{2,14},{3,15},{4,8},{5,9},{6,10},{7,11},{8,4},{9,5},... | collective-permute-start | bytes 497672 | tf_op jit(solution)/shard_map/ppermute | solution.py:333
  26.9 13.2 %copy-start.1 = (bf16[1,32,1152]{2,1,0:T(8,128)(2,1)S(1)}, bf16[1,32,1152]{2,1,0:T(8,128)(2,1)}, u32[]{:S(2)}) copy-start(bf16[1,32,1152]{2,1,0:T(8,128)(2,1)} %probe.3) | copy-start | bytes 221188
  50.6 12.5 %copy-start = (bf16[32,1152]{1,0:T(8,128)(2,1)S(1)}, bf16[32,1152]{1,0:T(8,128)(2,1)}, u32[]{:S(2)}) copy-start(bf16[32,1152]{1,0:T(8,128)(2,1)} %noisy.3) | copy-start | bytes 221188
  94.3 8.0 %collective-permute-start.2 = (bf16[16,2,1152]{2,1,0:T(2,128)(2,1)S(1)}, bf16[16,2,1152]{2,1,0:T(2,128)(2,1)S(1)}, u32[]{:S(2)}, u32[]{:S(2)}) collective-permute-start(bf16[16,2,1152]{2,1,0:T(2,128)(2,1)S(1)} %all_to_all.43.mine), channel_id=1, source_target_pairs={{0,16},{16,0},{1,17},{17,1},{2,18},{18,2},{3,19},{19,3},{4,20},{20... | collective-permute-start | bytes 221192 | tf_op jit(solution)/shard_map/ppermute | solution.py:400

commit v9 on v8

--- a/solution.py
+++ b/solution.py
@@ -49,9 +49,7 @@
     frequency = jnp.exp(-math.log(10000.0) * freq_index / half_dim)
     angles = timestep[0].astype(jnp.float32) * frequency
     embedding = jnp.concatenate([jnp.cos(angles), jnp.sin(angles)])
-    modulated = jnp.dot(
-        jax.nn.silu(embedding)[None, :], w_mod.astype(jnp.float32), precision=lax.Precision.HIGHEST
-    )
+    modulated = jnp.sum(jax.nn.silu(embedding)[:, None] * w_mod.astype(jnp.float32), axis=0)
     return modulated.reshape(3, feat_width)
 
 

time: 146 us -> 146 us (level)
  waiting for transfers between devices: 0.92 us -> 4.91 us
  local copies, waits for them, and re-layouts: 3.9 us -> 0.03 us
  matrix products: 2.95 us -> 0 us
  other arithmetic: 0.06 us -> 2.03 us
    unnamed x9 -> x8, local copies, waits for them, and re-layouts: 3.9 us -> 0.02 us
    dot_general x1 -> x0, matrix products: 2.95 us -> none  [modulation(): jnp.dot(jax.nn.silu(embedding)[None, :], w_mod.astype(jnp.float32), preci...]
    ppermute x1, waiting for transfers between devices: 0.01 us -> 2.16 us  [shards(): far_out = lax.ppermute(w_out, SEQ, partner)]
    reduce_sum x0 -> x1, other arithmetic: none -> 1.97 us  [modulation(): jnp.sum(jax.nn.silu(embedding)[:, None] * w_mod.astype(jnp.float32), axis=0)]
    all_to_all x1, waiting for transfers between devices: 0.03 us -> 1.57 us  [exchange(): return lax.all_to_all(blocks, axis, split_axis=0, concat_axis=0, tiled=True)]
  transfers between devices with their start and end apart: 4 -> 4, of which waited for: 1 -> 4; matrix products, arithmetic and copies ran while one was open for 5% -> 1% of each run, Pallas kernels for 3% -> 3%
where the time goes in v9:
time: 146 us; the launch traced here: 144 us
  blocking collectives  104 us (71%)
  starting transfers between devices  19.6 us (13%)
  Pallas kernels  11.9 us (8%)
  waiting for transfers between devices  4.91 us (3%)
  other arithmetic  2.03 us (1%)
    all_to_all x7, blocking collectives, exchange(): return lax.all_to_all(blocks, axis, split_axis=0, concat_axis=0, tiled=True)  104 us
    pallas_call x11, Pallas kernels, call(): pl.pallas_call(kernel, out_shape=out_shape, in_specs=where or [LOCAL] * l...  11.9 us
    ppermute x1, starting transfers between devices, shards(): other = lax.ppermute(mine, 'core', [(i, i ^ 1) for i in range(cores)])  7.08 us
    all_to_all x1, starting transfers between devices, exchange(): return lax.all_to_all(blocks, axis, split_axis=0, concat_axis=0, tiled=True)  5.96 us
    ppermute x1, starting transfers between devices, shards(): far_in = lax.ppermute(w_in, SEQ, partner)  4.62 us
  transfers between devices with their start and end apart: 4, of which 4 were waited for; matrix products, arithmetic and copies ran while one was open for 1% of the time, Pallas kernels for 3%

profile of v9, /device:TPU:1, one launch (start us, length us, event | category | flops | bytes accessed | tf_op | source)
XLA Modules:
  0.0 143.7 jit_solution(12983514798490511713)
XLA Ops:
  0.6 0.0 copy-start.2
  0.6 0.0 copy-start.3
  0.6 2.1 %shard_map.77 = bf16[8,2,32,1152]{3,2,1,0:T(8,128)(2,1)} custom-call(bf16[32,1152]{1,0:T(8,128)(2,1)} %noisy.3, bf16[1,32,1152]{2,1,0:T(8,128)(2,1)} %probe.3), custom_call_target="tpu_custom_call" | custom-call | bytes 2000000 | tf_op jit(solution)/shard_map/pallas_call | solution.py:290
  2.8 6.0 %all-to-all-start = ((bf16[8,2,32,1152]{3,2,1,0:T(8,128)(2,1)}), bf16[8,2,32,1152]{3,2,1,0:T(8,128)(2,1)S(1)}, u32[]{:S(2)}, u32[]{:S(2)}) async-start(bf16[8,2,32,1152]{3,2,1,0:T(8,128)(2,1)} %shard_map.77), calls=%async_computation | async-start | bytes 2359296 | tf_op jit(solution)/shard_map/all_to_all | solution.py:302
  8.7 0.0 copy-done.2
  8.7 4.6 %collective-permute-start = (bf16[216,1152]{1,0:T(8,128)(2,1)S(1)}, bf16[216,1152]{1,0:T(8,128)(2,1)S(1)}, u32[]{:S(2)}, u32[]{:S(2)}) collective-permute-start(bf16[216,1152]{1,0:T(8,128)(2,1)S(1)} %bitcast.2), channel_id=1, source_target_pairs={{0,12},{1,13},{2,14},{3,15},{4,8},{5,9},{6,10},{7,11},{8,4},{9,5},... | collective-permute-start | bytes 1493000 | tf_op jit(solution)/shard_map/ppermute | solution.py:330
  13.4 0.0 copy-done.3
  13.4 1.9 %collective-permute-start.1 = (bf16[72,1152]{1,0:T(8,128)(2,1)S(1)}, bf16[72,1152]{1,0:T(8,128)(2,1)S(1)}, u32[]{:S(2)}, u32[]{:S(2)}) collective-permute-start(bf16[72,1152]{1,0:T(8,128)(2,1)S(1)} %copy-done.3), channel_id=1, source_target_pairs={{0,12},{1,13},{2,14},{3,15},{4,8},{5,9},{6,10},{7,11},{8,4},{9,5},... | collective-permute-start | bytes 497672 | tf_op jit(solution)/shard_map/ppermute | solution.py:331
  16.0 2.0 %multiply_reduce_fusion = f32[3456]{0:T(1024)S(1)} fusion(bf16[256,3456]{1,0:T(8,128)(2,1)} %param.10, f32[256]{0:T(256)S(1)} %divide_multiply_fusion), kind=kLoop, calls=%fused_computation | loop fusion | flops 2650752 | bytes 1784320 | tf_op jit(solution)/shard_map/reduce_sum | solution.py:52
  18.0 1.6 %all-to-all-done.gath = bf16[8,2,32,1152]{3,2,1,0:T(8,128)(2,1)S(1)} async-done(((bf16[8,2,32,1152]{3,2,1,0:T(8,128)(2,1)}), bf16[8,2,32,1152]{3,2,1,0:T(8,128)(2,1)S(1)}, u32[]{:S(2)}, u32[]{:S(2)}) %all-to-all-start) | async-done | bytes 1179680 | tf_op jit(solution)/shard_map/all_to_all | solution.py:302
  19.6 2.6 %shard_map.78 = (bf16[512,1152]{1,0:T(8,128)(2,1)S(1)}, f32[256,1152]{1,0:T(8,128)S(1)}, bf16[3,256,72]{2,1,0:T(8,128)(2,1)S(1)}, bf16[256,256]{1,0:T(8,128)(2,1)S(1)}) custom-call(bf16[8,2,32,1152]{3,2,1,0:T(8,128)(2,1)S(1)} %all-to-all-done.gath, bf16[216,1152]{1,0:T(8,128)(2,1)S(1)} %bitcast.3, bf16[72,1152]{1,0:T(8,128)(2,1)S(1)} %copy-done.3, ...), custom_call_target="tpu_custom_call" | custom-call | flops 1000000000 | bytes 6000000 | tf_op jit(solution)/shard_map/pallas_call | solution.py:290
  22.2 0.3 collective-permute-done.w_in.far_in
  22.5 1.4 shard_map.79
  23.8 0.0 copy-start.1
  23.8 2.2 %collective-permute-done.1.w_out.far_out = bf16[72,1152]{1,0:T(8,128)(2,1)S(1)} collective-permute-done((bf16[72,1152]{1,0:T(8,128)(2,1)S(1)}, bf16[72,1152]{1,0:T(8,128)(2,1)S(1)}, u32[]{:S(2)}, u32[]{:S(2)}) %collective-permute-start.1) | collective-permute-done | bytes 165920 | tf_op jit(solution)/shard_map/ppermute | solution.py:331
  26.0 0.3 shard_map.80
  26.3 14.7 %all_to_all.40.parts = bf16[8,32,1152]{2,1,0:T(8,128)(2,1)S(1)} all-to-all(bf16[8,32,1152]{2,1,0:T(8,128)(2,1)S(1)} %shard_map.80), channel_id=1, replica_groups=mesh['z'=16,'core'=2,'frame'=2,'part'=8] {'part'}, dimensions={0} | all-to-all | bytes 1179648 | tf_op jit(solution)/shard_map/all_to_all | solution.py:302
  41.0 0.0 copy-done.1
  41.0 0.1 shard_map.81
  41.1 11.0 %all_to_all.41.gated = bf16[8,32,1152]{2,1,0:T(8,128)(2,1)S(1)} all-to-all(bf16[8,32,1152]{2,1,0:T(8,128)(2,1)S(1)} %get-tuple-element.27), channel_id=1, replica_groups=mesh['z'=16,'core'=2,'frame'=2,'part'=8] {'part'}, dimensions={0} | all-to-all | bytes 1179648 | tf_op jit(solution)/shard_map/all_to_all | solution.py:302
  52.1 2.1 %shard_map.82 = bf16[8,32,1152]{2,1,0:T(8,128)(2,1)S(1)} custom-call(bf16[8,32,1152]{2,1,0:T(8,128)(2,1)S(1)} %all_to_all.41.gated, bf16[216,1152]{1,0:T(8,128)(2,1)S(1)} %bitcast.4, bf16[72,1152]{1,0:T(8,128)(2,1)S(1)} %copy-done.3, bf16[3,256,72]{2,1,0:T(8,128)(2,1)S(1)} %get-tuple-element.28.near_primal, ...), custom_call_target="tpu_custom_call" | custom-call | flops 2000000000 | bytes 5000000 | tf_op jit(solution)/shard_map/pallas_call | solution.py:290
  54.2 11.2 %all_to_all.42.parts = bf16[8,32,1152]{2,1,0:T(8,128)(2,1)S(1)} all-to-all(bf16[8,32,1152]{2,1,0:T(8,128)(2,1)S(1)} %shard_map.82), channel_id=1, replica_groups=mesh['z'=16,'core'=2,'frame'=2,'part'=8] {'part'}, dimensions={0} | all-to-all | bytes 1179648 | tf_op jit(solution)/shard_map/all_to_all | solution.py:302
  65.4 0.3 shard_map.83
  65.8 28.6 %all_to_all.43.mine = bf16[16,2,1152]{2,1,0:T(2,128)(2,1)S(1)} all-to-all(bf16[16,2,1152]{2,1,0:T(2,128)(2,1)S(1)} %get-tuple-element.33), channel_id=1, replica_groups=mesh['z'=16,'core'=2,'frame'=2,'part'=8] {'z'}, dimensions={0} | all-to-all | bytes 147456 | tf_op jit(solution)/shard_map/all_to_all | solution.py:302
  94.3 7.1 %collective-permute-start.2 = (bf16[16,2,1152]{2,1,0:T(2,128)(2,1)S(1)}, bf16[16,2,1152]{2,1,0:T(2,128)(2,1)S(1)}, u32[]{:S(2)}, u32[]{:S(2)}) collective-permute-start(bf16[16,2,1152]{2,1,0:T(2,128)(2,1)S(1)} %all_to_all.43.mine), channel_id=1, source_target_pairs={{0,16},{16,0},{1,17},{17,1},{2,18},{18,2},{3,19},{19,3},{4,20},{20... | collective-permute-start | bytes 221192 | tf_op jit(solution)/shard_map/ppermute | solution.py:398
  101.4 0.9 collective-permute-done.2.other
  102.3 0.5 shard_map.84
  102.8 9.7 %all_to_all.44.arrived = f32[16,8,128]{2,1,0:T(8,128)S(1)} all-to-all(f32[16,8,128]{2,1,0:T(8,128)S(1)} %get-tuple-element.34), channel_id=1, replica_groups=mesh['z'=16,'core'=2,'frame'=2,'part'=8] {'frame','part'}, dimensions={0} | all-to-all | bytes 131072 | tf_op jit(solution)/shard_map/all_to_all | solution.py:302
  112.6 14.2 %all_to_all.45.arrived = f32[16,8,128]{2,1,0:T(8,128)S(1)} all-to-all(f32[16,8,128]{2,1,0:T(8,128)S(1)} %shard_map.85), channel_id=1, replica_groups=mesh['z'=16,'core'=2,'frame'=2,'part'=8] {'z'}, dimensions={0} | all-to-all | bytes 131072 | tf_op jit(solution)/shard_map/all_to_all | solution.py:302
  126.8 1.7 %shard_map.86 = (f32[32,32]{1,0:T(8,128)S(1)}, bf16[16,2,1152]{2,1,0:T(2,128)(2,1)S(1)}, f32[32,1152]{1,0:T(8,128)S(1)}) custom-call(f32[16,8,128]{2,1,0:T(8,128)S(1)} %all_to_all.45.arrived, bf16[32,2,1152]{2,1,0:T(2,128)(2,1)S(1)} %get-tuple-element.35.rows, f32[32,1152]{1,0:T(8,128)S(1)} %get-tuple-element.36.lost), custom_call_target="tpu_custom_call" | custom-call | bytes 300000 | tf_op jit(solution)/shard_map/pallas_call | solution.py:290
  128.6 14.4 %all_to_all.46.pairs = bf16[16,2,1152]{2,1,0:T(2,128)(2,1)S(1)} all-to-all(bf16[16,2,1152]{2,1,0:T(2,128)(2,1)S(1)} %get-tuple-element.37), channel_id=1, replica_groups=mesh['z'=16,'core'=2,'frame'=2,'part'=8] {'z'}, dimensions={0} | all-to-all | bytes 147456 | tf_op jit(solution)/shard_map/all_to_all | solution.py:302
  143.0 0.7 shard_map.87
  (6 shorter events, 0.1 us)
Async XLA Ops:
  0.6 8.1 %copy-start.2 = (bf16[1152,216]{0,1:T(8,128)(2,1)S(1)}, bf16[1152,216]{0,1:T(8,128)(2,1)}, u32[]{:S(2)}) copy-start(bf16[1152,216]{0,1:T(8,128)(2,1)} %param.8) | copy-start | bytes 1492996
  0.6 12.7 %copy-start.3 = (bf16[72,1152]{1,0:T(8,128)(2,1)S(1)}, bf16[72,1152]{1,0:T(8,128)(2,1)}, u32[]{:S(2)}) copy-start(bf16[72,1152]{1,0:T(8,128)(2,1)} %near_out) | copy-start | bytes 497668
  2.8 16.8 %all-to-all-start = ((bf16[8,2,32,1152]{3,2,1,0:T(8,128)(2,1)}), bf16[8,2,32,1152]{3,2,1,0:T(8,128)(2,1)S(1)}, u32[]{:S(2)}, u32[]{:S(2)}) async-start(bf16[8,2,32,1152]{3,2,1,0:T(8,128)(2,1)} %shard_map.77), calls=%async_computation | async-start | bytes 2359296 | tf_op jit(solution)/shard_map/all_to_all | solution.py:302
  8.7 13.7 %collective-permute-start = (bf16[216,1152]{1,0:T(8,128)(2,1)S(1)}, bf16[216,1152]{1,0:T(8,128)(2,1)S(1)}, u32[]{:S(2)}, u32[]{:S(2)}) collective-permute-start(bf16[216,1152]{1,0:T(8,128)(2,1)S(1)} %bitcast.2), channel_id=1, source_target_pairs={{0,12},{1,13},{2,14},{3,15},{4,8},{5,9},{6,10},{7,11},{8,4},{9,5},... | collective-permute-start | bytes 1493000 | tf_op jit(solution)/shard_map/ppermute | solution.py:330
  13.4 12.6 %collective-permute-start.1 = (bf16[72,1152]{1,0:T(8,128)(2,1)S(1)}, bf16[72,1152]{1,0:T(8,128)(2,1)S(1)}, u32[]{:S(2)}, u32[]{:S(2)}) collective-permute-start(bf16[72,1152]{1,0:T(8,128)(2,1)S(1)} %copy-done.3), channel_id=1, source_target_pairs={{0,12},{1,13},{2,14},{3,15},{4,8},{5,9},{6,10},{7,11},{8,4},{9,5},... | collective-permute-start | bytes 497672 | tf_op jit(solution)/shard_map/ppermute | solution.py:331
  23.8 17.2 %copy-start.1 = (bf16[1,32,1152]{2,1,0:T(8,128)(2,1)S(1)}, bf16[1,32,1152]{2,1,0:T(8,128)(2,1)}, u32[]{:S(2)}) copy-start(bf16[1,32,1152]{2,1,0:T(8,128)(2,1)} %probe.3) | copy-start | bytes 221188
  52.1 13.3 %copy-start = (bf16[32,1152]{1,0:T(8,128)(2,1)S(1)}, bf16[32,1152]{1,0:T(8,128)(2,1)}, u32[]{:S(2)}) copy-start(bf16[32,1152]{1,0:T(8,128)(2,1)} %noisy.3) | copy-start | bytes 221188
  94.3 8.0 %collective-permute-start.2 = (bf16[16,2,1152]{2,1,0:T(2,128)(2,1)S(1)}, bf16[16,2,1152]{2,1,0:T(2,128)(2,1)S(1)}, u32[]{:S(2)}, u32[]{:S(2)}) collective-permute-start(bf16[16,2,1152]{2,1,0:T(2,128)(2,1)S(1)} %all_to_all.43.mine), channel_id=1, source_target_pairs={{0,16},{16,0},{1,17},{17,1},{2,18},{18,2},{3,19},{19,3},{4,20},{20... | collective-permute-start | bytes 221192 | tf_op jit(solution)/shard_map/ppermute | solution.py:398

commit v10 on v9

--- a/solution.py
+++ b/solution.py
@@ -19,6 +19,7 @@
 FEW = 16
 NT = (((1,), (1,)), ((), ()))
 NN = (((1,), (0,)), ((), ()))
+TN = (((0,), (0,)), ((), ()))
 BF = jnp.bfloat16
 F32 = jnp.float32
 
@@ -37,10 +38,6 @@
     row = lax.broadcasted_iota(jnp.int32, (n, n), 0)
     col = lax.broadcasted_iota(jnp.int32, (n, n), 1)
     return jnp.where(row == col, 1.0, 0.0)
-
-
-def flip(a):
-    return mm(eye(a.shape[1]).astype(BF), a, NT).astype(BF)
 
 
 def modulation(timestep, w_mod, feat_width):
@@ -84,10 +81,9 @@
     return [value[:, i * HEAD_DIM : (i + 1) * HEAD_DIM].astype(BF) for i in range(3)]
 
 
-def head_forward(tokens, w_in, primal, probs):
+def head_forward(projected, primal, probs):
     c = HEAD_DIM ** (-0.5)
-    count = tokens.shape[0] // 2
-    projected = mm(tokens[...], w_in[...], NT)
+    count = projected.shape[0] // 2
     q, k, v = thirds(projected[:count])
     dq, dk, dv = thirds(projected[count:])
     scores = mm(q, k, NT) * c
@@ -107,18 +103,24 @@
     blocks, _, rows, _ = gath.shape
     scale = 1.0 + mods[1:2, :]
     shift = mods[0:1, :]
-    for i in range(blocks):
-        for at in range(0, rows, FEW):
-            few = pl.ds(at, FEW)
+    count = blocks * rows
+    span = count // 2
+    plain, changed = [], []
+    for start in (0, span):
+        for at in range(start, start + span, FEW):
+            i, few = at // rows, pl.ds(at % rows, FEW)
             normed, inverse = normalize(gath[i, 0, few, :].astype(F32))
-            tokens[pl.ds(i * rows + at, FEW), :] = (normed * scale + shift).astype(BF)
+            tokens[pl.ds(at, FEW), :] = (normed * scale + shift).astype(BF)
             field = norm_tangent(gath[i, 1, few, :].astype(F32), normed, inverse)
-            tokens[pl.ds((blocks + i) * rows + at, FEW), :] = (field * scale).astype(BF)
-    term[...] = mm(head_forward(tokens, w_in, primal, probs), w_out[...])
+            tokens[pl.ds(count + at, FEW), :] = (field * scale).astype(BF)
+        plain.append(mm(tokens[pl.ds(start, span), :], w_in[...], NT))
+        changed.append(mm(tokens[pl.ds(count + start, span), :], w_in[...], NT))
+    projected = jnp.concatenate(plain + changed, axis=0)
+    term[...] = mm(head_forward(projected, primal, probs), w_out[...])
 
 
 def far_kernel(tokens, w_in, out, primal, probs):
-    out[...] = head_forward(tokens, w_in, primal, probs)
+    out[...] = head_forward(mm(tokens[...], w_in[...], NT), primal, probs)
 
 
 def sum_kernel(term, out, w_out, parts):
@@ -169,7 +171,7 @@
         d_probs = mm(co, v, NT)
         row_dot = jnp.sum(p_float * d_probs, axis=-1, keepdims=True)
         scaled = (p_float * (d_probs - row_dot) * c).astype(BF)
-        grads += [mm(scaled, k), mm(flip(scaled), q), mm(flip(p), co)]
+        grads += [mm(scaled, k), mm(scaled, q, TN), mm(p, co, TN)]
     grads = jnp.concatenate(grads, axis=1).astype(BF)
     parts[...] = mm(grads, w_in[...].astype(BF)).astype(BF).reshape(parts.shape)
 

time: 146 us -> 145 us (level)
  no operation moved by 1% of the time
where the time goes in v10:
time: 145 us; the launch traced here: 143 us
  blocking collectives  103 us (71%)
  starting transfers between devices  19.9 us (14%)
  Pallas kernels  11.3 us (8%)
  waiting for transfers between devices  5.24 us (4%)
  other arithmetic  2.03 us (1%)
    all_to_all x7, blocking collectives, exchange(): return lax.all_to_all(blocks, axis, split_axis=0, concat_axis=0, tiled=True)  103 us
    pallas_call x11, Pallas kernels, call(): pl.pallas_call(kernel, out_shape=out_shape, in_specs=where or [LOCAL] * l...  11.3 us
    ppermute x1, starting transfers between devices, shards(): other = lax.ppermute(mine, 'core', [(i, i ^ 1) for i in range(cores)])  7.44 us
    all_to_all x1, starting transfers between devices, exchange(): return lax.all_to_all(blocks, axis, split_axis=0, concat_axis=0, tiled=True)  5.96 us
    ppermute x1, starting transfers between devices, shards(): far_in = lax.ppermute(w_in, SEQ, partner)  4.62 us
  transfers between devices with their start and end apart: 4, of which 4 were waited for; matrix products, arithmetic and copies ran while one was open for 1% of the time, Pallas kernels for 3%

profile of v10, /device:TPU:1, one launch (start us, length us, event | category | flops | bytes accessed | tf_op | source)
XLA Modules:
  0.0 142.9 jit_solution(1203375209754312201)
XLA Ops:
  0.6 0.0 copy-start.2
  0.6 0.0 copy-start.3
  0.6 2.1 %shard_map.77 = bf16[8,2,32,1152]{3,2,1,0:T(8,128)(2,1)} custom-call(bf16[32,1152]{1,0:T(8,128)(2,1)} %noisy.3, bf16[1,32,1152]{2,1,0:T(8,128)(2,1)} %probe.3), custom_call_target="tpu_custom_call" | custom-call | bytes 2000000 | tf_op jit(solution)/shard_map/pallas_call | solution.py:292
  2.8 6.0 %all-to-all-start = ((bf16[8,2,32,1152]{3,2,1,0:T(8,128)(2,1)}), bf16[8,2,32,1152]{3,2,1,0:T(8,128)(2,1)S(1)}, u32[]{:S(2)}, u32[]{:S(2)}) async-start(bf16[8,2,32,1152]{3,2,1,0:T(8,128)(2,1)} %shard_map.77), calls=%async_computation | async-start | bytes 2359296 | tf_op jit(solution)/shard_map/all_to_all | solution.py:304
  8.7 0.0 copy-done.2
  8.7 4.6 %collective-permute-start = (bf16[216,1152]{1,0:T(8,128)(2,1)S(1)}, bf16[216,1152]{1,0:T(8,128)(2,1)S(1)}, u32[]{:S(2)}, u32[]{:S(2)}) collective-permute-start(bf16[216,1152]{1,0:T(8,128)(2,1)S(1)} %bitcast.2), channel_id=1, source_target_pairs={{0,12},{1,13},{2,14},{3,15},{4,8},{5,9},{6,10},{7,11},{8,4},{9,5},... | collective-permute-start | bytes 1493000 | tf_op jit(solution)/shard_map/ppermute | solution.py:332
  13.4 0.0 copy-done.3
  13.4 1.9 %collective-permute-start.1 = (bf16[72,1152]{1,0:T(8,128)(2,1)S(1)}, bf16[72,1152]{1,0:T(8,128)(2,1)S(1)}, u32[]{:S(2)}, u32[]{:S(2)}) collective-permute-start(bf16[72,1152]{1,0:T(8,128)(2,1)S(1)} %copy-done.3), channel_id=1, source_target_pairs={{0,12},{1,13},{2,14},{3,15},{4,8},{5,9},{6,10},{7,11},{8,4},{9,5},... | collective-permute-start | bytes 497672 | tf_op jit(solution)/shard_map/ppermute | solution.py:333
  16.0 2.0 %multiply_reduce_fusion = f32[3456]{0:T(1024)S(1)} fusion(bf16[256,3456]{1,0:T(8,128)(2,1)} %param.10, f32[256]{0:T(256)S(1)} %divide_multiply_fusion), kind=kLoop, calls=%fused_computation | loop fusion | flops 2650752 | bytes 1784320 | tf_op jit(solution)/shard_map/reduce_sum | solution.py:49
  18.0 1.6 %all-to-all-done.gath = bf16[8,2,32,1152]{3,2,1,0:T(8,128)(2,1)S(1)} async-done(((bf16[8,2,32,1152]{3,2,1,0:T(8,128)(2,1)}), bf16[8,2,32,1152]{3,2,1,0:T(8,128)(2,1)S(1)}, u32[]{:S(2)}, u32[]{:S(2)}) %all-to-all-start) | async-done | bytes 1179680 | tf_op jit(solution)/shard_map/all_to_all | solution.py:304
  19.6 2.3 %shard_map.78 = (bf16[512,1152]{1,0:T(8,128)(2,1)S(1)}, f32[256,1152]{1,0:T(8,128)S(1)}, bf16[3,256,72]{2,1,0:T(8,128)(2,1)S(1)}, bf16[256,256]{1,0:T(8,128)(2,1)S(1)}) custom-call(bf16[8,2,32,1152]{3,2,1,0:T(8,128)(2,1)S(1)} %all-to-all-done.gath, bf16[216,1152]{1,0:T(8,128)(2,1)S(1)} %bitcast.3, bf16[72,1152]{1,0:T(8,128)(2,1)S(1)} %copy-done.3, ...), custom_call_target="tpu_custom_call" | custom-call | flops 1000000000 | bytes 6000000 | tf_op jit(solution)/shard_map/pallas_call | solution.py:292
  21.8 0.6 collective-permute-done.w_in.far_in
  22.5 1.4 shard_map.79
  23.8 0.0 copy-start.1
  23.8 2.2 %collective-permute-done.1.w_out.far_out = bf16[72,1152]{1,0:T(8,128)(2,1)S(1)} collective-permute-done((bf16[72,1152]{1,0:T(8,128)(2,1)S(1)}, bf16[72,1152]{1,0:T(8,128)(2,1)S(1)}, u32[]{:S(2)}, u32[]{:S(2)}) %collective-permute-start.1) | collective-permute-done | bytes 165920 | tf_op jit(solution)/shard_map/ppermute | solution.py:333
  26.0 0.3 shard_map.80
  26.3 14.2 %all_to_all.40.parts = bf16[8,32,1152]{2,1,0:T(8,128)(2,1)S(1)} all-to-all(bf16[8,32,1152]{2,1,0:T(8,128)(2,1)S(1)} %shard_map.80), channel_id=1, replica_groups=mesh['z'=16,'core'=2,'frame'=2,'part'=8] {'part'}, dimensions={0} | all-to-all | bytes 1179648 | tf_op jit(solution)/shard_map/all_to_all | solution.py:304
  40.5 0.0 copy-done.1
  40.5 0.1 shard_map.81
  40.6 10.9 %all_to_all.41.gated = bf16[8,32,1152]{2,1,0:T(8,128)(2,1)S(1)} all-to-all(bf16[8,32,1152]{2,1,0:T(8,128)(2,1)S(1)} %get-tuple-element.27), channel_id=1, replica_groups=mesh['z'=16,'core'=2,'frame'=2,'part'=8] {'part'}, dimensions={0} | all-to-all | bytes 1179648 | tf_op jit(solution)/shard_map/all_to_all | solution.py:304
  51.5 1.9 %shard_map.82 = bf16[8,32,1152]{2,1,0:T(8,128)(2,1)S(1)} custom-call(bf16[8,32,1152]{2,1,0:T(8,128)(2,1)S(1)} %all_to_all.41.gated, bf16[216,1152]{1,0:T(8,128)(2,1)S(1)} %bitcast.4, bf16[72,1152]{1,0:T(8,128)(2,1)S(1)} %copy-done.3, bf16[3,256,72]{2,1,0:T(8,128)(2,1)S(1)} %get-tuple-element.28.near_primal, ...), custom_call_target="tpu_custom_call" | custom-call | flops 2000000000 | bytes 5000000 | tf_op jit(solution)/shard_map/pallas_call | solution.py:292
  53.4 10.4 %all_to_all.42.parts = bf16[8,32,1152]{2,1,0:T(8,128)(2,1)S(1)} all-to-all(bf16[8,32,1152]{2,1,0:T(8,128)(2,1)S(1)} %shard_map.82), channel_id=1, replica_groups=mesh['z'=16,'core'=2,'frame'=2,'part'=8] {'part'}, dimensions={0} | all-to-all | bytes 1179648 | tf_op jit(solution)/shard_map/all_to_all | solution.py:304
  63.8 0.3 shard_map.83
  64.1 28.3 %all_to_all.43.mine = bf16[16,2,1152]{2,1,0:T(2,128)(2,1)S(1)} all-to-all(bf16[16,2,1152]{2,1,0:T(2,128)(2,1)S(1)} %get-tuple-element.33), channel_id=1, replica_groups=mesh['z'=16,'core'=2,'frame'=2,'part'=8] {'z'}, dimensions={0} | all-to-all | bytes 147456 | tf_op jit(solution)/shard_map/all_to_all | solution.py:304
  92.5 7.4 %collective-permute-start.2 = (bf16[16,2,1152]{2,1,0:T(2,128)(2,1)S(1)}, bf16[16,2,1152]{2,1,0:T(2,128)(2,1)S(1)}, u32[]{:S(2)}, u32[]{:S(2)}) collective-permute-start(bf16[16,2,1152]{2,1,0:T(2,128)(2,1)S(1)} %all_to_all.43.mine), channel_id=1, source_target_pairs={{0,16},{16,0},{1,17},{17,1},{2,18},{18,2},{3,19},{19,3},{4,20},{20... | collective-permute-start | bytes 221192 | tf_op jit(solution)/shard_map/ppermute | solution.py:400
  99.9 0.9 collective-permute-done.2.other
  100.8 0.5 shard_map.84
  101.3 10.5 %all_to_all.44.arrived = f32[16,8,128]{2,1,0:T(8,128)S(1)} all-to-all(f32[16,8,128]{2,1,0:T(8,128)S(1)} %get-tuple-element.34), channel_id=1, replica_groups=mesh['z'=16,'core'=2,'frame'=2,'part'=8] {'frame','part'}, dimensions={0} | all-to-all | bytes 131072 | tf_op jit(solution)/shard_map/all_to_all | solution.py:304
  111.8 14.2 %all_to_all.45.arrived = f32[16,8,128]{2,1,0:T(8,128)S(1)} all-to-all(f32[16,8,128]{2,1,0:T(8,128)S(1)} %shard_map.85), channel_id=1, replica_groups=mesh['z'=16,'core'=2,'frame'=2,'part'=8] {'z'}, dimensions={0} | all-to-all | bytes 131072 | tf_op jit(solution)/shard_map/all_to_all | solution.py:304
  126.0 1.7 %shard_map.86 = (f32[32,32]{1,0:T(8,128)S(1)}, bf16[16,2,1152]{2,1,0:T(2,128)(2,1)S(1)}, f32[32,1152]{1,0:T(8,128)S(1)}) custom-call(f32[16,8,128]{2,1,0:T(8,128)S(1)} %all_to_all.45.arrived, bf16[32,2,1152]{2,1,0:T(2,128)(2,1)S(1)} %get-tuple-element.35.rows, f32[32,1152]{1,0:T(8,128)S(1)} %get-tuple-element.36.lost), custom_call_target="tpu_custom_call" | custom-call | bytes 300000 | tf_op jit(solution)/shard_map/pallas_call | solution.py:292
  127.8 14.4 %all_to_all.46.pairs = bf16[16,2,1152]{2,1,0:T(2,128)(2,1)S(1)} all-to-all(bf16[16,2,1152]{2,1,0:T(2,128)(2,1)S(1)} %get-tuple-element.37), channel_id=1, replica_groups=mesh['z'=16,'core'=2,'frame'=2,'part'=8] {'z'}, dimensions={0} | all-to-all | bytes 147456 | tf_op jit(solution)/shard_map/all_to_all | solution.py:304
  142.2 0.7 shard_map.87
  (6 shorter events, 0.1 us)
Async XLA Ops:
  0.6 8.1 %copy-start.2 = (bf16[1152,216]{0,1:T(8,128)(2,1)S(1)}, bf16[1152,216]{0,1:T(8,128)(2,1)}, u32[]{:S(2)}) copy-start(bf16[1152,216]{0,1:T(8,128)(2,1)} %param.8) | copy-start | bytes 1492996
  0.6 12.7 %copy-start.3 = (bf16[72,1152]{1,0:T(8,128)(2,1)S(1)}, bf16[72,1152]{1,0:T(8,128)(2,1)}, u32[]{:S(2)}) copy-start(bf16[72,1152]{1,0:T(8,128)(2,1)} %near_out) | copy-start | bytes 497668
  2.8 16.8 %all-to-all-start = ((bf16[8,2,32,1152]{3,2,1,0:T(8,128)(2,1)}), bf16[8,2,32,1152]{3,2,1,0:T(8,128)(2,1)S(1)}, u32[]{:S(2)}, u32[]{:S(2)}) async-start(bf16[8,2,32,1152]{3,2,1,0:T(8,128)(2,1)} %shard_map.77), calls=%async_computation | async-start | bytes 2359296 | tf_op jit(solution)/shard_map/all_to_all | solution.py:304
  8.7 13.7 %collective-permute-start = (bf16[216,1152]{1,0:T(8,128)(2,1)S(1)}, bf16[216,1152]{1,0:T(8,128)(2,1)S(1)}, u32[]{:S(2)}, u32[]{:S(2)}) collective-permute-start(bf16[216,1152]{1,0:T(8,128)(2,1)S(1)} %bitcast.2), channel_id=1, source_target_pairs={{0,12},{1,13},{2,14},{3,15},{4,8},{5,9},{6,10},{7,11},{8,4},{9,5},... | collective-permute-start | bytes 1493000 | tf_op jit(solution)/shard_map/ppermute | solution.py:332
  13.4 12.6 %collective-permute-start.1 = (bf16[72,1152]{1,0:T(8,128)(2,1)S(1)}, bf16[72,1152]{1,0:T(8,128)(2,1)S(1)}, u32[]{:S(2)}, u32[]{:S(2)}) collective-permute-start(bf16[72,1152]{1,0:T(8,128)(2,1)S(1)} %copy-done.3), channel_id=1, source_target_pairs={{0,12},{1,13},{2,14},{3,15},{4,8},{5,9},{6,10},{7,11},{8,4},{9,5},... | collective-permute-start | bytes 497672 | tf_op jit(solution)/shard_map/ppermute | solution.py:333
  23.8 16.7 %copy-start.1 = (bf16[1,32,1152]{2,1,0:T(8,128)(2,1)S(1)}, bf16[1,32,1152]{2,1,0:T(8,128)(2,1)}, u32[]{:S(2)}) copy-start(bf16[1,32,1152]{2,1,0:T(8,128)(2,1)} %probe.3) | copy-start | bytes 221188
  51.5 12.3 %copy-start = (bf16[32,1152]{1,0:T(8,128)(2,1)S(1)}, bf16[32,1152]{1,0:T(8,128)(2,1)}, u32[]{:S(2)}) copy-start(bf16[32,1152]{1,0:T(8,128)(2,1)} %noisy.3) | copy-start | bytes 221188
  92.5 8.3 %collective-permute-start.2 = (bf16[16,2,1152]{2,1,0:T(2,128)(2,1)S(1)}, bf16[16,2,1152]{2,1,0:T(2,128)(2,1)S(1)}, u32[]{:S(2)}, u32[]{:S(2)}) collective-permute-start(bf16[16,2,1152]{2,1,0:T(2,128)(2,1)S(1)} %all_to_all.43.mine), channel_id=1, source_target_pairs={{0,16},{16,0},{1,17},{17,1},{2,18},{18,2},{3,19},{19,3},{4,20},{20... | collective-permute-start | bytes 221192 | tf_op jit(solution)/shard_map/ppermute | solution.py:400

commit v11 on v10

--- a/solution.py
+++ b/solution.py
@@ -89,7 +89,8 @@
     scores = mm(q, k, NT) * c
     expon = jnp.exp(scores - jnp.max(scores, axis=-1, keepdims=True))
     p = (expon * (1.0 / jnp.sum(expon, axis=-1, keepdims=True))).astype(BF)
-    d_scores = (mm(dq, k, NT) + mm(q, dk, NT)) * c
+    beside = [jnp.concatenate(pair, axis=1) for pair in ((dq, q), (k, dk))]
+    d_scores = mm(*beside, NT) * c
     mixed = p.astype(F32) * d_scores
     row_sum = jnp.sum(mixed, axis=-1, keepdims=True)
     out = mm(mixed.astype(BF), v) + mm(p, dv) - row_sum * mm(p, v)

time: 145 us -> 145 us (level)
  no operation moved by 1% of the time
where the time goes in v11:
time: 145 us; the launch traced here: 143 us
  blocking collectives  103 us (71%)
  starting transfers between devices  19.9 us (14%)
  Pallas kernels  11.3 us (8%)
  waiting for transfers between devices  5.22 us (4%)
  other arithmetic  2.03 us (1%)
    all_to_all x7, blocking collectives, exchange(): return lax.all_to_all(blocks, axis, split_axis=0, concat_axis=0, tiled=True)  103 us
    pallas_call x11, Pallas kernels, call(): pl.pallas_call(kernel, out_shape=out_shape, in_specs=where or [LOCAL] * l...  11.3 us
    ppermute x1, starting transfers between devices, shards(): other = lax.ppermute(mine, 'core', [(i, i ^ 1) for i in range(cores)])  7.44 us
    all_to_all x1, starting transfers between devices, exchange(): return lax.all_to_all(blocks, axis, split_axis=0, concat_axis=0, tiled=True)  5.96 us
    ppermute x1, starting transfers between devices, shards(): far_in = lax.ppermute(w_in, SEQ, partner)  4.62 us
  transfers between devices with their start and end apart: 4, of which 4 were waited for; matrix products, arithmetic and copies ran while one was open for 1% of the time, Pallas kernels for 3%

profile of v11, /device:TPU:1, one launch (start us, length us, event | category | flops | bytes accessed | tf_op | source)
XLA Modules:
  0.0 143.0 jit_solution(3815447602930599263)
XLA Ops:
  0.6 0.0 copy-start.2
  0.6 0.0 copy-start.3
  0.6 2.1 %shard_map.77 = bf16[8,2,32,1152]{3,2,1,0:T(8,128)(2,1)} custom-call(bf16[32,1152]{1,0:T(8,128)(2,1)} %noisy.3, bf16[1,32,1152]{2,1,0:T(8,128)(2,1)} %probe.3), custom_call_target="tpu_custom_call" | custom-call | bytes 2000000 | tf_op jit(solution)/shard_map/pallas_call | solution.py:293
  2.8 6.0 %all-to-all-start = ((bf16[8,2,32,1152]{3,2,1,0:T(8,128)(2,1)}), bf16[8,2,32,1152]{3,2,1,0:T(8,128)(2,1)S(1)}, u32[]{:S(2)}, u32[]{:S(2)}) async-start(bf16[8,2,32,1152]{3,2,1,0:T(8,128)(2,1)} %shard_map.77), calls=%async_computation | async-start | bytes 2359296 | tf_op jit(solution)/shard_map/all_to_all | solution.py:305
  8.7 0.0 copy-done.2
  8.7 4.6 %collective-permute-start = (bf16[216,1152]{1,0:T(8,128)(2,1)S(1)}, bf16[216,1152]{1,0:T(8,128)(2,1)S(1)}, u32[]{:S(2)}, u32[]{:S(2)}) collective-permute-start(bf16[216,1152]{1,0:T(8,128)(2,1)S(1)} %bitcast.2), channel_id=1, source_target_pairs={{0,12},{1,13},{2,14},{3,15},{4,8},{5,9},{6,10},{7,11},{8,4},{9,5},... | collective-permute-start | bytes 1493000 | tf_op jit(solution)/shard_map/ppermute | solution.py:333
  13.4 0.0 copy-done.3
  13.4 1.9 %collective-permute-start.1 = (bf16[72,1152]{1,0:T(8,128)(2,1)S(1)}, bf16[72,1152]{1,0:T(8,128)(2,1)S(1)}, u32[]{:S(2)}, u32[]{:S(2)}) collective-permute-start(bf16[72,1152]{1,0:T(8,128)(2,1)S(1)} %copy-done.3), channel_id=1, source_target_pairs={{0,12},{1,13},{2,14},{3,15},{4,8},{5,9},{6,10},{7,11},{8,4},{9,5},... | collective-permute-start | bytes 497672 | tf_op jit(solution)/shard_map/ppermute | solution.py:334
  16.0 2.0 %multiply_reduce_fusion = f32[3456]{0:T(1024)S(1)} fusion(bf16[256,3456]{1,0:T(8,128)(2,1)} %param.10, f32[256]{0:T(256)S(1)} %divide_multiply_fusion), kind=kLoop, calls=%fused_computation | loop fusion | flops 2650752 | bytes 1784320 | tf_op jit(solution)/shard_map/reduce_sum | solution.py:49
  18.0 1.6 %all-to-all-done.gath = bf16[8,2,32,1152]{3,2,1,0:T(8,128)(2,1)S(1)} async-done(((bf16[8,2,32,1152]{3,2,1,0:T(8,128)(2,1)}), bf16[8,2,32,1152]{3,2,1,0:T(8,128)(2,1)S(1)}, u32[]{:S(2)}, u32[]{:S(2)}) %all-to-all-start) | async-done | bytes 1179680 | tf_op jit(solution)/shard_map/all_to_all | solution.py:305
  19.6 2.3 %shard_map.78 = (bf16[512,1152]{1,0:T(8,128)(2,1)S(1)}, f32[256,1152]{1,0:T(8,128)S(1)}, bf16[3,256,72]{2,1,0:T(8,128)(2,1)S(1)}, bf16[256,256]{1,0:T(8,128)(2,1)S(1)}) custom-call(bf16[8,2,32,1152]{3,2,1,0:T(8,128)(2,1)S(1)} %all-to-all-done.gath, bf16[216,1152]{1,0:T(8,128)(2,1)S(1)} %bitcast.3, bf16[72,1152]{1,0:T(8,128)(2,1)S(1)} %copy-done.3, ...), custom_call_target="tpu_custom_call" | custom-call | flops 1000000000 | bytes 6000000 | tf_op jit(solution)/shard_map/pallas_call | solution.py:293
  21.9 0.5 collective-permute-done.w_in.far_in
  22.5 1.3 shard_map.79
  23.8 0.0 copy-start.1
  23.8 2.2 %collective-permute-done.1.w_out.far_out = bf16[72,1152]{1,0:T(8,128)(2,1)S(1)} collective-permute-done((bf16[72,1152]{1,0:T(8,128)(2,1)S(1)}, bf16[72,1152]{1,0:T(8,128)(2,1)S(1)}, u32[]{:S(2)}, u32[]{:S(2)}) %collective-permute-start.1) | collective-permute-done | bytes 165920 | tf_op jit(solution)/shard_map/ppermute | solution.py:334
  26.0 0.3 shard_map.80
  26.3 14.2 %all_to_all.40.parts = bf16[8,32,1152]{2,1,0:T(8,128)(2,1)S(1)} all-to-all(bf16[8,32,1152]{2,1,0:T(8,128)(2,1)S(1)} %shard_map.80), channel_id=1, replica_groups=mesh['z'=16,'core'=2,'frame'=2,'part'=8] {'part'}, dimensions={0} | all-to-all | bytes 1179648 | tf_op jit(solution)/shard_map/all_to_all | solution.py:305
  40.5 0.0 copy-done.1
  40.5 0.1 shard_map.81
  40.6 10.9 %all_to_all.41.gated = bf16[8,32,1152]{2,1,0:T(8,128)(2,1)S(1)} all-to-all(bf16[8,32,1152]{2,1,0:T(8,128)(2,1)S(1)} %get-tuple-element.27), channel_id=1, replica_groups=mesh['z'=16,'core'=2,'frame'=2,'part'=8] {'part'}, dimensions={0} | all-to-all | bytes 1179648 | tf_op jit(solution)/shard_map/all_to_all | solution.py:305
  51.6 1.9 %shard_map.82 = bf16[8,32,1152]{2,1,0:T(8,128)(2,1)S(1)} custom-call(bf16[8,32,1152]{2,1,0:T(8,128)(2,1)S(1)} %all_to_all.41.gated, bf16[216,1152]{1,0:T(8,128)(2,1)S(1)} %bitcast.4, bf16[72,1152]{1,0:T(8,128)(2,1)S(1)} %copy-done.3, bf16[3,256,72]{2,1,0:T(8,128)(2,1)S(1)} %get-tuple-element.28.near_primal, ...), custom_call_target="tpu_custom_call" | custom-call | flops 2000000000 | bytes 5000000 | tf_op jit(solution)/shard_map/pallas_call | solution.py:293
  53.4 10.4 %all_to_all.42.parts = bf16[8,32,1152]{2,1,0:T(8,128)(2,1)S(1)} all-to-all(bf16[8,32,1152]{2,1,0:T(8,128)(2,1)S(1)} %shard_map.82), channel_id=1, replica_groups=mesh['z'=16,'core'=2,'frame'=2,'part'=8] {'part'}, dimensions={0} | all-to-all | bytes 1179648 | tf_op jit(solution)/shard_map/all_to_all | solution.py:305
  63.8 0.3 shard_map.83
  64.2 28.3 %all_to_all.43.mine = bf16[16,2,1152]{2,1,0:T(2,128)(2,1)S(1)} all-to-all(bf16[16,2,1152]{2,1,0:T(2,128)(2,1)S(1)} %get-tuple-element.33), channel_id=1, replica_groups=mesh['z'=16,'core'=2,'frame'=2,'part'=8] {'z'}, dimensions={0} | all-to-all | bytes 147456 | tf_op jit(solution)/shard_map/all_to_all | solution.py:305
  92.5 7.4 %collective-permute-start.2 = (bf16[16,2,1152]{2,1,0:T(2,128)(2,1)S(1)}, bf16[16,2,1152]{2,1,0:T(2,128)(2,1)S(1)}, u32[]{:S(2)}, u32[]{:S(2)}) collective-permute-start(bf16[16,2,1152]{2,1,0:T(2,128)(2,1)S(1)} %all_to_all.43.mine), channel_id=1, source_target_pairs={{0,16},{16,0},{1,17},{17,1},{2,18},{18,2},{3,19},{19,3},{4,20},{20... | collective-permute-start | bytes 221192 | tf_op jit(solution)/shard_map/ppermute | solution.py:401
  99.9 0.9 collective-permute-done.2.other
  100.8 0.5 shard_map.84
  101.4 10.5 %all_to_all.44.arrived = f32[16,8,128]{2,1,0:T(8,128)S(1)} all-to-all(f32[16,8,128]{2,1,0:T(8,128)S(1)} %get-tuple-element.34), channel_id=1, replica_groups=mesh['z'=16,'core'=2,'frame'=2,'part'=8] {'frame','part'}, dimensions={0} | all-to-all | bytes 131072 | tf_op jit(solution)/shard_map/all_to_all | solution.py:305
  111.8 14.2 %all_to_all.45.arrived = f32[16,8,128]{2,1,0:T(8,128)S(1)} all-to-all(f32[16,8,128]{2,1,0:T(8,128)S(1)} %shard_map.85), channel_id=1, replica_groups=mesh['z'=16,'core'=2,'frame'=2,'part'=8] {'z'}, dimensions={0} | all-to-all | bytes 131072 | tf_op jit(solution)/shard_map/all_to_all | solution.py:305
  126.1 1.7 %shard_map.86 = (f32[32,32]{1,0:T(8,128)S(1)}, bf16[16,2,1152]{2,1,0:T(2,128)(2,1)S(1)}, f32[32,1152]{1,0:T(8,128)S(1)}) custom-call(f32[16,8,128]{2,1,0:T(8,128)S(1)} %all_to_all.45.arrived, bf16[32,2,1152]{2,1,0:T(2,128)(2,1)S(1)} %get-tuple-element.35.rows, f32[32,1152]{1,0:T(8,128)S(1)} %get-tuple-element.36.lost), custom_call_target="tpu_custom_call" | custom-call | bytes 300000 | tf_op jit(solution)/shard_map/pallas_call | solution.py:293
  127.8 14.4 %all_to_all.46.pairs = bf16[16,2,1152]{2,1,0:T(2,128)(2,1)S(1)} all-to-all(bf16[16,2,1152]{2,1,0:T(2,128)(2,1)S(1)} %get-tuple-element.37), channel_id=1, replica_groups=mesh['z'=16,'core'=2,'frame'=2,'part'=8] {'z'}, dimensions={0} | all-to-all | bytes 147456 | tf_op jit(solution)/shard_map/all_to_all | solution.py:305
  142.2 0.7 shard_map.87
  (6 shorter events, 0.1 us)
Async XLA Ops:
  0.6 8.1 %copy-start.2 = (bf16[1152,216]{0,1:T(8,128)(2,1)S(1)}, bf16[1152,216]{0,1:T(8,128)(2,1)}, u32[]{:S(2)}) copy-start(bf16[1152,216]{0,1:T(8,128)(2,1)} %param.8) | copy-start | bytes 1492996
  0.6 12.7 %copy-start.3 = (bf16[72,1152]{1,0:T(8,128)(2,1)S(1)}, bf16[72,1152]{1,0:T(8,128)(2,1)}, u32[]{:S(2)}) copy-start(bf16[72,1152]{1,0:T(8,128)(2,1)} %near_out) | copy-start | bytes 497668
  2.8 16.8 %all-to-all-start = ((bf16[8,2,32,1152]{3,2,1,0:T(8,128)(2,1)}), bf16[8,2,32,1152]{3,2,1,0:T(8,128)(2,1)S(1)}, u32[]{:S(2)}, u32[]{:S(2)}) async-start(bf16[8,2,32,1152]{3,2,1,0:T(8,128)(2,1)} %shard_map.77), calls=%async_computation | async-start | bytes 2359296 | tf_op jit(solution)/shard_map/all_to_all | solution.py:305
  8.7 13.7 %collective-permute-start = (bf16[216,1152]{1,0:T(8,128)(2,1)S(1)}, bf16[216,1152]{1,0:T(8,128)(2,1)S(1)}, u32[]{:S(2)}, u32[]{:S(2)}) collective-permute-start(bf16[216,1152]{1,0:T(8,128)(2,1)S(1)} %bitcast.2), channel_id=1, source_target_pairs={{0,12},{1,13},{2,14},{3,15},{4,8},{5,9},{6,10},{7,11},{8,4},{9,5},... | collective-permute-start | bytes 1493000 | tf_op jit(solution)/shard_map/ppermute | solution.py:333
  13.4 12.6 %collective-permute-start.1 = (bf16[72,1152]{1,0:T(8,128)(2,1)S(1)}, bf16[72,1152]{1,0:T(8,128)(2,1)S(1)}, u32[]{:S(2)}, u32[]{:S(2)}) collective-permute-start(bf16[72,1152]{1,0:T(8,128)(2,1)S(1)} %copy-done.3), channel_id=1, source_target_pairs={{0,12},{1,13},{2,14},{3,15},{4,8},{5,9},{6,10},{7,11},{8,4},{9,5},... | collective-permute-start | bytes 497672 | tf_op jit(solution)/shard_map/ppermute | solution.py:334
  23.8 16.7 %copy-start.1 = (bf16[1,32,1152]{2,1,0:T(8,128)(2,1)S(1)}, bf16[1,32,1152]{2,1,0:T(8,128)(2,1)}, u32[]{:S(2)}) copy-start(bf16[1,32,1152]{2,1,0:T(8,128)(2,1)} %probe.3) | copy-start | bytes 221188
  51.6 12.3 %copy-start = (bf16[32,1152]{1,0:T(8,128)(2,1)S(1)}, bf16[32,1152]{1,0:T(8,128)(2,1)}, u32[]{:S(2)}) copy-start(bf16[32,1152]{1,0:T(8,128)(2,1)} %noisy.3) | copy-start | bytes 221188
  92.5 8.3 %collective-permute-start.2 = (bf16[16,2,1152]{2,1,0:T(2,128)(2,1)S(1)}, bf16[16,2,1152]{2,1,0:T(2,128)(2,1)S(1)}, u32[]{:S(2)}, u32[]{:S(2)}) collective-permute-start(bf16[16,2,1152]{2,1,0:T(2,128)(2,1)S(1)} %all_to_all.43.mine), channel_id=1, source_target_pairs={{0,16},{16,0},{1,17},{17,1},{2,18},{18,2},{3,19},{19,3},{4,20},{20... | collective-permute-start | bytes 221192 | tf_op jit(solution)/shard_map/ppermute | solution.py:401
